TPU v7x, 256 devices: a whole 4x4x8 slice. The times are simulated.
256 devices in a mesh: clip: 8 (over y, core), seq: 16 (over z, x_lo), tp: 2 (over x_hi).
Axes of the slice: x: 4 (x_hi: 2, x_lo: 2; x = x_hi * 2 + x_lo), y: 4, z: 8, core: 2. Of those that a mesh axis runs over, the one named last changes fastest.
Arguments:
- frames: bfloat16 [768, 128, 1152], P('tp', ('clip', 'seq')), parts along dimension 1, may hold values from -6 to 6
- timestep: int32 [8], P('clip'), parts along dimension 0, may hold values from 0 to 999
- embed_weight: bfloat16 [256, 1152], replicated, may hold values from -0.375 to 0.375
- block_weight: bfloat16 [1152, 3456], P(('seq', 'tp')), may hold values from -0.1875 to 0.1875
- spatial_table: float32 [3, 1152], replicated, may hold values from -3 to 3
- temporal_table: float32 [3, 1152], replicated, may hold values from -3 to 3
- spatial_qkv: bfloat16 [1152, 3, 1152], P(None, None, 'tp'), may hold values from -1 to 1
- spatial_out: bfloat16 [1152, 1152], P('tp'), may hold values from -0.1875 to 0.1875
- temporal_qkv: bfloat16 [1152, 3, 1152], P(None, None, 'tp'), may hold values from -1 to 1
- temporal_out: bfloat16 [1152, 1152], P('tp'), may hold values from -0.1875 to 0.1875
Outputs:
- mixed: float32 [768, 128, 1152], P('tp', ('clip', 'seq')), parts along dimension 1
There are 8 independent parts, one for each index of `clip`. A program takes and returns all parts, laid end to end along the dimension named above; an argument that names none is the same for every part. Nothing has to cross between parts.
All inputs are finite; a program needn't handle non-finite values.
Results may differ from a plain program's by a relative error of at most 0.0085.
Values may be sent and summed in bfloat16 or wider, within the bound.
No kernel may reach another device: no remote copies, remote signals or barrier semaphores. Data moves between devices by JAX's collectives and lax.ppermute only.
A program may use at most 128 MiB of HBM per device.

v0:
```python
import math

import jax
import jax.numpy as jnp
from jax import lax
from jax.sharding import PartitionSpec as P

HEAD_DIM = 72
FREQ = 256


def layer_norm(values):
    mean = jnp.mean(values, axis=-1, keepdims=True)
    centred = values - mean
    variance = jnp.mean(centred * centred, axis=-1, keepdims=True)
    return centred * lax.rsqrt(variance + 1e-06)


def modulate(tokens, mods):
    normed = layer_norm(tokens.astype(jnp.float32))
    return (normed * (1.0 + mods[1]) + mods[0]).astype(jnp.bfloat16)


def residual_add(tokens, mods, projected):
    return tokens.astype(jnp.float32) + mods[2] * projected


def soft_weights(scores):
    peak = jnp.max(scores, axis=-1, keepdims=True)
    raised = jnp.exp(scores - peak)
    return (raised / jnp.sum(raised, axis=-1, keepdims=True)).astype(jnp.bfloat16)


def time_features(timestep):
    half = FREQ // 2
    ladder = jnp.exp(-math.log(10000.0) * jnp.arange(half, dtype=jnp.float32) / half)
    angles = timestep.astype(jnp.float32)[:, None] * ladder[None, :]
    return jnp.concatenate([jnp.cos(angles), jnp.sin(angles)], axis=-1)


def modulation_rows(timestep, embed_weight, block_weight):
    features = time_features(timestep)
    embedded = jax.nn.silu(
        jnp.dot(features, embed_weight.astype(jnp.float32), precision=lax.Precision.HIGHEST)
    )
    count = block_weight.shape[0]
    start = lax.axis_index(("seq", "tp")) * count
    mine = lax.dynamic_slice_in_dim(embedded, start, count, 1)
    term = jnp.dot(mine, block_weight.astype(jnp.float32), precision=lax.Precision.HIGHEST)
    total = lax.psum(term, ("seq", "tp"))
    return total.reshape(3, -1)


def gather_rows(tokens):
    return lax.all_gather(tokens, "tp", axis=0, tiled=True)


def project_rows(attended, out_weight):
    share = attended.shape[0] // lax.axis_size("tp")

    def term(start, count):
        return jnp.dot(attended, out_weight, preferred_element_type=jnp.float32)

    return lax.psum_scatter(
        term(jnp.int32(0), share * lax.axis_size("tp")), "tp", scatter_dimension=0, tiled=True
    )


def project_in(tokens, qkv_weight):
    flat = qkv_weight.reshape(qkv_weight.shape[0], -1)
    return jnp.dot(tokens, flat, preferred_element_type=jnp.float32).astype(jnp.bfloat16)


def spatial_attend(qkv):
    count, depth = (qkv.shape[0], qkv.shape[1])
    grid = qkv.reshape(count, depth, 3, -1, HEAD_DIM)
    factor = 1.0 / math.sqrt(HEAD_DIM)
    scores = (
        jnp.einsum(
            "qfhd,kfhd->fhqk", grid[:, :, 0], grid[:, :, 1], preferred_element_type=jnp.float32
        )
        * factor
    )
    weights = soft_weights(scores)
    attended = jnp.einsum(
        "fhqk,kfhd->qfhd", weights, grid[:, :, 2], preferred_element_type=jnp.float32
    )
    return attended.astype(jnp.bfloat16).reshape(count, depth, -1)


def temporal_attend(qkv):
    count, depth = (qkv.shape[0], qkv.shape[1])
    grid = qkv.reshape(count, depth, 3, -1, HEAD_DIM)
    factor = 1.0 / math.sqrt(HEAD_DIM)
    scores = (
        jnp.einsum(
            "pfhd,pghd->phfg", grid[:, :, 0], grid[:, :, 1], preferred_element_type=jnp.float32
        )
        * factor
    )
    weights = soft_weights(scores)
    attended = jnp.einsum(
        "phfg,pghd->pfhd", weights, grid[:, :, 2], preferred_element_type=jnp.float32
    )
    return attended.astype(jnp.bfloat16).reshape(count, depth, -1)


def body(
    frames,
    timestep,
    embed_weight,
    block_weight,
    spatial_table,
    temporal_table,
    spatial_qkv,
    spatial_out,
    temporal_qkv,
    temporal_out,
):
    modulation = modulation_rows(timestep, embed_weight, block_weight)
    spatial_mods = spatial_table + modulation
    temporal_mods = temporal_table + modulation
    normed = modulate(frames, spatial_mods)
    whole = gather_rows(normed)
    attended = spatial_attend(project_in(whole, spatial_qkv))
    middle = residual_add(frames, spatial_mods, project_rows(attended, spatial_out))
    normed = modulate(middle, temporal_mods)
    whole = gather_rows(normed)
    qkv = project_in(whole, temporal_qkv)
    moved = lax.all_to_all(qkv, "seq", split_axis=0, concat_axis=1, tiled=True)
    attended = temporal_attend(moved)
    returned = lax.all_to_all(attended, "seq", split_axis=1, concat_axis=0, tiled=True)
    projected = project_rows(returned, temporal_out)
    return residual_add(middle, temporal_mods, projected)


def solution(mesh):
    return jax.shard_map(
        body,
        mesh=mesh,
        in_specs=(
            P("tp", ("clip", "seq"), None),
            P("clip"),
            P(),
            P(("seq", "tp"), None),
            P(),
            P(),
            P(None, None, "tp"),
            P("tp", None),
            P(None, None, "tp"),
            P("tp", None),
        ),
        out_specs=P("tp", ("clip", "seq"), None),
        check_vma=False,
    )
```

profile of v0, /device:TPU:4, one launch (start us, length us, event | category | flops | bytes accessed | tf_op | source)
XLA Modules:
  0.0 552.6 jit_solution(14011660452898259015)
XLA Ops:
  7.4 1.4 convolution_reduce_fusion.1
  8.8 1.3 convolution_reduce_fusion
  10.1 140.6 %psum.7 = f32[3,1152]{1,0:T(4,128)S(1)} all-reduce(f32[3,1152]{1,0:T(4,128)S(1)} %reshape.189), channel_id=1, replica_groups=mesh['clip'=8,'seq'=16,'tp'=2] {'seq','tp'}, use_global_device_ids=true, to_apply=%region_0.1 | all-reduce | flops 3456 | bytes 27648 | tf_op jit(solution)/shard_map/psum | solution.py:50
  151.6 1.4 convert_reduce_fusion
  153.3 1.3 fusion.18
  154.7 34.1 %all-gather.3.cloned.1.call-done = bf16[768,1,1152]{2,0,1:T(8,128)(2,1)} async-done(((bf16[384,1,1152]{2,0,1:T(8,128)(2,1)}), bf16[768,1,1152]{2,0,1:T(8,128)(2,1)}) %all-gather.3.cloned.1.call-update) | async-done | bytes 1769488 | tf_op jit(solution)/shard_map/all_gather | solution.py:55
  188.8 7.8 %convolution_convert_fusion.1 = bf16[768,1728]{0,1:T(8,128)(2,1)} fusion(bf16[1152,1728]{0,1:T(8,128)(2,1)} %bitcast.92, bf16[768,1,1152]{2,0,1:T(8,128)(2,1)} %all-gather.3.cloned.1.call-done), kind=kOutput, calls=%fused_computation.12 | convolution fusion | flops 3058974720 | bytes 8404992 | tf_op jit(solution)/shard_map/dot_general | solution.py:71
  196.6 10.8 %fusion.45 = (f32[8,768]{1,0:T(8,128)S(1)}, f32[8,768,768]{1,2,0:T(8,128)}) fusion(bf16[768,1,3,8,72]{0,4,3,2,1:T(8,128)(2,1)} %bitcast.94), kind=kOutput, calls=%fused_computation.78 | convolution fusion | flops 693633792 | bytes 20668416 | tf_op jit(solution)/shard_map/sub | solution.py:30
  207.4 8.4 %fusion.25 = bf16[8,72,768]{2,1,0:T(8,128)(2,1)S(1)} fusion(f32[8,768,768]{1,2,0:T(8,128)} %get-tuple-element.17, f32[8,768]{1,0:T(8,128)S(1)} %get-tuple-element.16, bf16[768,1,3,8,72]{0,4,3,2,1:T(8,128)(2,1)} %bitcast.95), kind=kOutput, calls=%fused_computation.40 | convolution fusion | flops 689356800 | bytes 20668416 | tf_op jit(solution)/shard_map/fhqk,kfhd->qfhd/dot_general | solution.py:85
  215.9 3.5 convolution_bitcast_fusion.1
  219.6 53.6 %reduce-scatter.3.cloned.1.call-done = f32[384,1,1152]{2,0,1:T(8,128)} async-done(((f32[768,1,1152]{2,0,1:T(8,128)}), f32[384,1,1152]{2,0,1:T(8,128)}) %reduce-scatter.3.cloned.1.call-update) | async-done | bytes 1769488 | tf_op jit(solution)/shard_map/reduce_scatter | solution.py:64
  273.2 1.9 fusion.42
  275.7 1.4 add_convert_fusion
  277.2 35.6 %all-gather.5.cloned.1.call-done = bf16[768,1,1152]{2,0,1:T(8,128)(2,1)} async-done(((bf16[384,1,1152]{2,0,1:T(8,128)(2,1)}), bf16[768,1,1152]{2,0,1:T(8,128)(2,1)}) %all-gather.5.cloned.1.call-update) | async-done | bytes 1769488 | tf_op jit(solution)/shard_map/all_gather | solution.py:55
  312.8 7.8 %fusion.9 = bf16[768,1,1728]{0,2,1:T(8,128)(2,1)} fusion(bf16[1152,1728]{0,1:T(8,128)(2,1)} %bitcast.93, bf16[768,1,1152]{2,0,1:T(8,128)(2,1)} %all-gather.5.cloned.1.call-done), kind=kOutput, calls=%fused_computation.15 | convolution fusion | flops 3058974720 | bytes 8404992 | tf_op jit(solution)/shard_map/dot_general | solution.py:71
  321.2 5.1 reduce.24
  326.3 4.6 copy.52
  330.9 7.6 %reshape.218 = bf16[16,2,41472]{2,1,0:T(2,128)(2,1)} reshape(bf16[768,1728]{1,0:T(8,128)(2,1)} %copy.52) | data formatting | bytes 5308416
  338.5 72.8 %all_to_all.30 = bf16[16,2,41472]{2,1,0:T(2,128)(2,1)} all-to-all(bf16[16,2,41472]{2,1,0:T(2,128)(2,1)} %reshape.218), channel_id=1, replica_groups=mesh['clip'=8,'seq'=16,'tp'=2] {'seq'}, dimensions={0} | all-to-all | bytes 5308416 | tf_op jit(solution)/shard_map/all_to_all | solution.py:130
  411.3 12.1 %reshape.219 = bf16[768,1,1728]{2,1,0:T(2,128)(2,1)} reshape(bf16[16,2,41472]{2,1,0:T(2,128)(2,1)} %all_to_all.30) | data formatting | bytes 5308416
  423.4 4.5 copy.40
  427.9 8.8 %reshape.209 = bf16[48,16,3,8,72]{4,3,2,0,1:T(8,128)(2,1)} reshape(bf16[48,16,1,1728]{3,0,1,2:T(8,128)(2,1)} %bitcast.90) | data formatting | bytes 5308416 | tf_op jit(solution)/shard_map/reshape | solution.py:93
  436.7 2.9 fusion.43
  439.5 1.9 fusion.21
  441.5 12.1 %fusion.46 = (f32[48,8,16]{2,1,0:T(8,128)S(1)}, f32[48,8,16,16]{2,3,1,0:T(8,128)S(1)}) fusion(f32[48,8,16,16]{2,3,1,0:T(8,128)S(1)} %fusion.21), kind=kOutput, calls=%fused_computation.79 | output fusion | flops 393231 | bytes 811008 | tf_op jit(solution)/shard_map/sub | solution.py:30
  454.8 1.6 copy.36
  456.4 3.0 reshape.208
  459.4 29.0 %all_to_all.31 = bf16[48,16,576]{2,0,1:T(8,128)(2,1)S(1)} all-to-all(bf16[48,16,576]{2,0,1:T(8,128)(2,1)S(1)} %reshape.208), channel_id=1, replica_groups=mesh['clip'=8,'seq'=16,'tp'=2] {'seq'}, dimensions={1} | all-to-all | bytes 1769472 | tf_op jit(solution)/shard_map/all_to_all | solution.py:132
  488.3 3.4 convolution_bitcast_fusion
  491.8 48.9 %reduce-scatter.5.cloned.1.call-done = f32[384,1,1152]{2,0,1:T(8,128)} async-done(((f32[768,1,1152]{2,0,1:T(8,128)}), f32[384,1,1152]{2,0,1:T(8,128)}) %reduce-scatter.5.cloned.1.call-update) | async-done | bytes 1769488 | tf_op jit(solution)/shard_map/reduce_scatter | solution.py:64
  540.6 2.4 multiply_add_fusion
  543.0 3.0 copy.33
  (31 shorter events, 4.0 us)
Async XLA Ops:
  6.5 209.3 %copy-start = (bf16[576,1152]{1,0:T(8,128)(2,1)S(1)}, bf16[576,1152]{1,0:T(8,128)(2,1)}, u32[]{:S(2)}) copy-start(bf16[576,1152]{1,0:T(8,128)(2,1)} %param.17) | copy-start | bytes 3981316
  6.5 146.4 %copy-start.2 = (bf16[384,1,1152]{2,0,1:T(8,128)(2,1)S(1)}, bf16[384,1,1152]{2,0,1:T(8,128)(2,1)}, u32[]{:S(2)}) copy-start(bf16[384,1,1152]{2,0,1:T(8,128)(2,1)} %param.10) | copy-start | bytes 2654212
  6.5 182.3 %all-gather.3.cloned.1.call-start = ((), (), s32[]{:S(2)}) async-start(), calls=%async_computation.4 | async-start | bytes 2654208 | tf_op jit(solution)/shard_map/all_gather | solution.py:55
  154.7 118.6 %reduce-scatter.3.cloned.1.call-start = ((), (), s32[]{:S(2)}) async-start(), calls=%async_computation.5 | async-start | bytes 5308416 | tf_op jit(solution)/shard_map/reduce_scatter | solution.py:64
  219.4 93.4 %all-gather.5.cloned.1.call-start = ((), (), s32[]{:S(2)}) async-start(), calls=%async_computation.6 | async-start | bytes 2654208 | tf_op jit(solution)/shard_map/all_gather | solution.py:55
  273.2 2.0 copy-start.3
  277.2 263.5 %reduce-scatter.5.cloned.1.call-start = ((), (), s32[]{:S(2)}) async-start(), calls=%async_computation.7 | async-start | bytes 5308416 | tf_op jit(solution)/shard_map/reduce_scatter | solution.py:64
  456.4 31.9 %copy-start.4 = (bf16[576,1152]{1,0:T(8,128)(2,1)S(1)}, bf16[576,1152]{1,0:T(8,128)(2,1)}, u32[]{:S(2)}) copy-start(bf16[576,1152]{1,0:T(8,128)(2,1)} %param.19) | copy-start | bytes 3981316
  540.6 5.4 copy-start.1
Sparse Core Ops, SparseCore 0:
  154.8 33.9 all-gather.2
  219.5 53.7 reduce-scatter.2
  277.3 35.4 all-gather.4
  491.9 48.6 reduce-scatter.4
where the time goes:
time: 557 us; the launch traced here: 553 us
  blocking collectives  242 us (43%)
  waiting for transfers between devices  172 us (31%)
  local copies, waits for them, and re-layouts  48.6 us (9%)
  matrix products  47.7 us (9%)
  other arithmetic  27.4 us (5%)
  between operations  14 us (3%)
    psum x1, blocking collectives, modulation_rows(): total = lax.psum(term, ('seq', 'tp'))  141 us
    reduce_scatter x2, waiting for transfers between devices, project_rows(): lax.psum_scatter(term(jnp.int32(0), share * lax.axis_size('tp')), 'tp', s...  102 us
    all_to_all x1, blocking collectives, body(): moved = lax.all_to_all(qkv, 'seq', split_axis=0, concat_axis=1, tiled=True)  72.8 us
    all_gather x2, waiting for transfers between devices, gather_rows(): return lax.all_gather(tokens, 'tp', axis=0, tiled=True)  69.7 us
    all_to_all x1, blocking collectives, body(): lax.all_to_all(attended, 'seq', split_axis=1, concat_axis=0, tiled=True)  29 us
    unnamed x14, local copies, waits for them, and re-layouts  28.9 us
    dot_general x2, matrix products, project_in(): jnp.dot(tokens, flat, preferred_element_type=jnp.float32)  15.6 us
    sub x1, other arithmetic, soft_weights(): raised = jnp.exp(scores - peak)  12.1 us
  transfers between devices with their start and end apart: 4, of which 4 were waited for; matrix products, arithmetic and copies ran while one was open for 0% of the time, Pallas kernels for 0%

commit v1 on v0

v1 whole, which is shorter than its diff:
```python
import math

import jax
import jax.numpy as jnp
from jax import lax
from jax.sharding import PartitionSpec as P

HEAD_DIM = 72
FREQ = 256
SWAP = [(0, 1), (1, 0)]


def layer_norm(values):
    mean = jnp.mean(values, axis=-1, keepdims=True)
    centred = values - mean
    variance = jnp.mean(centred * centred, axis=-1, keepdims=True)
    return centred * lax.rsqrt(variance + 1e-06)


def modulate(tokens, mods):
    normed = layer_norm(tokens.astype(jnp.float32))
    return (normed * (1.0 + mods[1]) + mods[0]).astype(jnp.bfloat16)


def time_features(timestep):
    half = FREQ // 2
    ladder = jnp.exp(-math.log(10000.0) * jnp.arange(half, dtype=jnp.float32) / half)
    angles = timestep.astype(jnp.float32)[:, None] * ladder[None, :]
    return jnp.concatenate([jnp.cos(angles), jnp.sin(angles)], axis=-1)


def modulation_rows(timestep, embed_weight, block_weight):
    features = time_features(timestep)
    embedded = jax.nn.silu(
        jnp.dot(features, embed_weight.astype(jnp.float32), precision=lax.Precision.HIGHEST)
    )
    count, width = block_weight.shape
    group = lax.axis_size("seq") * lax.axis_size("tp")
    start = lax.axis_index(("seq", "tp")) * count
    mine = lax.dynamic_slice_in_dim(embedded, start, count, 1)
    term = jnp.dot(mine, block_weight.astype(jnp.float32), precision=lax.Precision.HIGHEST)
    rows = 32
    term = jnp.pad(term.reshape(width // 128, 128), ((0, rows - width // 128), (0, 0)))
    copies = jnp.broadcast_to(term[None], (group, rows, 128)).reshape(group * rows, 128)
    terms = lax.all_to_all(copies, ("seq", "tp"), 0, 0, tiled=True)
    total = jnp.sum(terms.reshape(group, rows, 128), axis=0)
    return total.reshape(-1)[:width].reshape(3, -1)


def other_half(weight):
    eighth = weight.shape[0] // lax.axis_size("clip")
    piece = lax.dynamic_slice_in_dim(weight, lax.axis_index("clip") * eighth, eighth, 0)
    group = lax.axis_size("seq") * lax.axis_size("tp")
    piece = lax.ppermute(piece, ("seq", "tp"), [(i, i ^ 3) for i in range(group)])
    return lax.all_gather(piece, "clip", axis=0, tiled=True)


def attend(scores, values, out):
    peak = jnp.max(scores, axis=-1, keepdims=True)
    raised = jnp.exp(scores - peak)
    weights = (raised / jnp.sum(raised, axis=-1, keepdims=True)).astype(jnp.bfloat16)
    return jnp.einsum(out, weights, values, preferred_element_type=jnp.float32)


def project_in(tokens, weight):
    return lax.dot_general(
        tokens, weight, (((1,), (1,)), ((), ())), preferred_element_type=jnp.float32
    ).astype(jnp.bfloat16)


def spatial_attend(queries, keys, values):
    scores = jnp.einsum("qhd,khd->hqk", queries, keys, preferred_element_type=jnp.float32)
    out = attend(scores / math.sqrt(HEAD_DIM), values, "hqk,khd->qhd")
    return out.astype(jnp.bfloat16).reshape(queries.shape[0], -1)


def temporal_attend(qkv, depth):
    grid = qkv.reshape(depth, -1, 3, 8, HEAD_DIM)
    scores = jnp.einsum(
        "fphd,gphd->phfg", grid[:, :, 0], grid[:, :, 1], preferred_element_type=jnp.float32
    )
    out = attend(scores / math.sqrt(HEAD_DIM), grid[:, :, 2], "phfg,gphd->fphd")
    return out.astype(jnp.bfloat16).reshape(qkv.shape[0], -1)


def body(
    frames,
    timestep,
    embed_weight,
    block_weight,
    spatial_table,
    temporal_table,
    spatial_qkv,
    spatial_out,
    temporal_qkv,
    temporal_out,
):
    width = frames.shape[-1]
    tokens = frames.reshape(-1, width)
    count = tokens.shape[0]
    partner = lax.ppermute(tokens, "tp", SWAP)
    spatial_in = jnp.transpose(spatial_qkv, (1, 2, 0)).reshape(-1, width)
    temporal_in = jnp.transpose(temporal_qkv, (1, 2, 0)).reshape(-1, width)
    spatial_out_other = other_half(spatial_out)
    temporal_in_other = other_half(temporal_in)
    temporal_out_other = other_half(temporal_out)

    modulation = modulation_rows(timestep, embed_weight, block_weight)
    spatial_mods = spatial_table + modulation
    temporal_mods = temporal_table + modulation

    own = project_in(modulate(tokens, spatial_mods), spatial_in)
    far = project_in(modulate(partner, spatial_mods), spatial_in)
    grid = jnp.concatenate([own, far], axis=0).reshape(2 * count, 3, 8, HEAD_DIM)
    attended_far = spatial_attend(grid[count:, 0], grid[:, 1], grid[:, 2])
    attended_other = lax.ppermute(attended_far, "tp", SWAP)
    attended_own = spatial_attend(grid[:count, 0], grid[:, 1], grid[:, 2])
    projected = jnp.dot(attended_own, spatial_out, preferred_element_type=jnp.float32)
    projected += jnp.dot(attended_other, spatial_out_other, preferred_element_type=jnp.float32)
    middle = tokens.astype(jnp.float32) + spatial_mods[2] * projected

    normed = modulate(middle, temporal_mods)
    moved = lax.all_to_all(normed, "seq", 0, 0, tiled=True)
    depth = lax.axis_size("seq")
    attended = jnp.concatenate(
        [
            temporal_attend(project_in(moved, temporal_in), depth),
            temporal_attend(project_in(moved, temporal_in_other), depth),
        ],
        axis=1,
    )
    returned = lax.all_to_all(attended, "seq", 0, 0, tiled=True)
    half = temporal_out.shape[0]
    projected = jnp.dot(returned[:, :half], temporal_out, preferred_element_type=jnp.float32)
    projected += jnp.dot(
        returned[:, half:], temporal_out_other, preferred_element_type=jnp.float32
    )
    return (middle + temporal_mods[2] * projected).reshape(frames.shape)


def solution(mesh):
    return jax.shard_map(
        body,
        mesh=mesh,
        in_specs=(
            P("tp", ("clip", "seq"), None),
            P("clip"),
            P(),
            P(("seq", "tp"), None),
            P(),
            P(),
            P(None, None, "tp"),
            P("tp", None),
            P(None, None, "tp"),
            P("tp", None),
        ),
        out_specs=P("tp", ("clip", "seq"), None),
        check_vma=False,
    )
```

time: 557 us -> 246 us (0.44)
  blocking collectives: 242 us -> 28.1 us
  waiting for transfers between devices: 172 us -> 58.8 us
  starting transfers between devices: 0.31 us -> 27.3 us
  matrix products: 47.7 us -> 69.7 us
  other arithmetic: 27.4 us -> 8.31 us
  local copies, waits for them, and re-layouts: 48.6 us -> 34.6 us
    psum x1 -> x0, blocking collectives: 141 us -> none  [modulation_rows(): total = lax.psum(term, ('seq', 'tp'))]
    reduce_scatter x2 -> x0, waiting for transfers between devices: 102 us -> none  [project_rows(): lax.psum_scatter(term(jnp.int32(0), share * lax.axis_size('tp')), 'tp', s...]
    all_to_all x2 -> x1, blocking collectives: 102 us -> 28.1 us  [body(): returned = lax.all_to_all(attended, 'seq', 0, 0, tiled=True)]
    all_gather x2 -> x3, waiting for transfers between devices: 69.7 us -> 0.02 us  [other_half(): return lax.all_gather(piece, 'clip', axis=0, tiled=True)]
    ppermute x0 -> x5, waiting for transfers between devices: none -> 41.3 us  [the longest x3 41.3 us: other_half(): lax.ppermute(piece, ('seq', 'tp'), [(i, i ^ 3) for i in range(group)])]
    unnamed x14 -> x28, local copies, waits for them, and re-layouts: 28.9 us -> 3.98 us
    all_to_all x0 -> x2, starting transfers between devices: none -> 20 us  [the longest x1 12.6 us: modulation_rows(): terms = lax.all_to_all(copies, ('seq', 'tp'), 0, 0, tiled=True)]
    all_to_all x0 -> x2, waiting for transfers between devices: none -> 17.5 us  [the longest x1 17.5 us: body(): moved = lax.all_to_all(normed, 'seq', 0, 0, tiled=True)]
  transfers between devices with their start and end apart: 4 -> 10, of which waited for: 4 -> 4; matrix products, arithmetic and copies ran while one was open for 0% -> 42% of each run, Pallas kernels for 0% -> 0%
where the time goes in v1:
time: 246 us; the launch traced here: 241 us
  matrix products  69.7 us (28%)
  waiting for transfers between devices  58.8 us (24%)
  local copies, waits for them, and re-layouts  34.6 us (14%)
  blocking collectives  28.1 us (11%)
  starting transfers between devices  27.3 us (11%)
  between operations  14.3 us (6%)
  other arithmetic  8.31 us (3%)
    ppermute x3, waiting for transfers between devices, other_half(): lax.ppermute(piece, ('seq', 'tp'), [(i, i ^ 3) for i in range(group)])  41.3 us
    all_to_all x1, blocking collectives, body(): returned = lax.all_to_all(attended, 'seq', 0, 0, tiled=True)  28.1 us
    sub x4, matrix products, attend(): raised = jnp.exp(scores - peak)  24.1 us
    dot_general x4, matrix products, project_in(): lax.dot_general(tokens, weight, (((1,), (1,)), ((), ())), preferred_eleme...  17.9 us
    all_to_all x1, waiting for transfers between devices, body(): moved = lax.all_to_all(normed, 'seq', 0, 0, tiled=True)  17.5 us
    dot_general x4, matrix products, attend(): return jnp.einsum(out, weights, values, preferred_element_type=jnp.float32)  15.4 us
    all_to_all x1, starting transfers between devices, modulation_rows(): terms = lax.all_to_all(copies, ('seq', 'tp'), 0, 0, tiled=True)  12.6 us
    reshape x2, local copies, waits for them, and re-layouts, temporal_attend(): grid = qkv.reshape(depth, -1, 3, 8, HEAD_DIM)  10.1 us
  transfers between devices with their start and end apart: 10, of which 4 were waited for; matrix products, arithmetic and copies ran while one was open for 42% of the time, Pallas kernels for 0%

profile of v1, /device:TPU:4, one launch (start us, length us, event | category | flops | bytes accessed | tf_op | source)
XLA Modules:
  0.0 241.1 jit_solution(14881551623964012644)
XLA Ops:
  8.5 5.4 %collective-permute-done.2 = bf16[72,1152]{1,0:T(8,128)(2,1)S(1)} collective-permute-done((bf16[72,1152]{1,0:T(8,128)(2,1)S(1)}, bf16[72,1152]{1,0:T(8,128)(2,1)S(1)}, u32[]{:S(2)}, u32[]{:S(2)}) %collective-permute-start.2) | collective-permute-done | bytes 165920 | tf_op jit(solution)/shard_map/ppermute | solution.py:54
  19.1 12.6 %all-to-all-start = ((f32[32,32,128]{2,1,0:T(8,128)}), f32[32,32,128]{2,1,0:T(8,128)}, u32[]{:S(2)}, u32[]{:S(2)}) async-start(f32[32,32,128]{2,1,0:T(8,128)} %broadcast_in_dim.2), calls=%async_computation | async-start | bytes 1048576 | tf_op jit(solution)/shard_map/all_to_all | solution.py:45
  33.2 2.9 %collective-permute-start.3 = (bf16[216,1152]{1,0:T(8,128)(2,1)S(1)}, bf16[216,1152]{1,0:T(8,128)(2,1)}, u32[]{:S(2)}, u32[]{:S(2)}) collective-permute-start(bf16[216,1152]{1,0:T(8,128)(2,1)S(1)} %constant_dynamic-slice_fusion.1), channel_id=1, source_target_pairs={{0,3},{1,2},{2,1},{3,0},{4,7},{5,6},{6,5},{7,4},{8,11},{9,10},{10,... | collective-permute-start | bytes 1493000 | tf_op jit(solution)/shard_map/ppermute | solution.py:54
  36.8 31.8 %collective-permute-done.3 = bf16[216,1152]{1,0:T(8,128)(2,1)} collective-permute-done((bf16[216,1152]{1,0:T(8,128)(2,1)S(1)}, bf16[216,1152]{1,0:T(8,128)(2,1)}, u32[]{:S(2)}, u32[]{:S(2)}) %collective-permute-start.3) | collective-permute-done | bytes 497696 | tf_op jit(solution)/shard_map/ppermute | solution.py:54
  71.0 4.8 %convolution_convert_fusion.3 = bf16[384,1728]{0,1:T(8,128)(2,1)S(1)} fusion(bf16[1728,1152]{1,0:T(8,128)(2,1)} %bitcast.163, bf16[384,1,1152]{2,0,1:T(8,128)(2,1)S(1)} %copy-done.2, f32[1152]{0:T(1024)S(1)} %get-tuple-element.9, f32[1152]{0:T(1024)S(1)} %get-tuple-element.10, f32[384]{0:T(512)S(1)} %add_rsqrt_fusion.2, f32[384]{0:T(512)S(1)} %broadcast_multiply_fusion.2), kind=kOutput, calls=%fused_computation.26 | convolution fusion | flops 1532141568 | bytes 6205440 | tf_op jit(solution)/shard_map/dot_general | solution.py:66
  75.8 2.5 %convolution_convert_fusion.2 = bf16[384,1728]{0,1:T(8,128)(2,1)S(1)} fusion(bf16[1728,1152]{1,0:T(8,128)(2,1)S(1)} %bitcast.164, bf16[384,1152]{1,0:T(8,128)(2,1)S(1)} %collective-permute-done, f32[1152]{0:T(1024)S(1)} %get-tuple-element.9, f32[1152]{0:T(1024)S(1)} %get-tuple-element.10, f32[384]{0:T(512)S(1)} %add_rsqrt_fusion.1, ...), kind=kOutput, calls=%fused_computation.25 | convolution fusion | flops 1532141568 | bytes 6205440 | tf_op jit(solution)/shard_map/dot_general | solution.py:66
  80.0 8.1 %fusion.82 = (f32[8,384]{1,0:T(8,128)S(1)}, f32[8,384,768]{2,1,0:T(8,128)}) fusion(bf16[768,3,8,72]{0,3,2,1:T(8,128)(2,1)} %bitcast.152), kind=kOutput, calls=%fused_computation.131 | convolution fusion | flops 346817280 | bytes 10776576 | tf_op jit(solution)/shard_map/sub | solution.py:60
  88.1 5.7 %fusion.33 = bf16[8,72,384]{2,1,0:T(8,128)(2,1)S(1)} fusion(f32[8,384,768]{2,1,0:T(8,128)} %get-tuple-element.22, f32[8,384]{1,0:T(8,128)S(1)} %get-tuple-element.21, bf16[768,3,8,72]{0,3,2,1:T(8,128)(2,1)} %bitcast.153), kind=kOutput, calls=%fused_computation.55 | convolution fusion | flops 344678400 | bytes 10776576 | tf_op jit(solution)/shard_map/hqk,khd->qhd/dot_general | solution.py:62
  93.8 1.7 collective-permute-start.1
  95.5 8.0 %fusion.81 = (f32[8,384]{1,0:T(8,128)S(1)}, f32[8,384,768]{2,1,0:T(8,128)}) fusion(bf16[768,3,8,72]{0,3,2,1:T(8,128)(2,1)} %bitcast.154), kind=kOutput, calls=%fused_computation.130 | convolution fusion | flops 346817280 | bytes 10776576 | tf_op jit(solution)/shard_map/sub | solution.py:60
  103.5 5.5 %fusion.34 = bf16[8,72,384]{2,1,0:T(8,128)(2,1)S(1)} fusion(f32[8,384,768]{2,1,0:T(8,128)} %get-tuple-element.20, f32[8,384]{1,0:T(8,128)S(1)} %get-tuple-element.19, bf16[768,3,8,72]{0,3,2,1:T(8,128)(2,1)} %bitcast.155), kind=kOutput, calls=%fused_computation.56 | convolution fusion | flops 344678400 | bytes 10776576 | tf_op jit(solution)/shard_map/hqk,khd->qhd/dot_general | solution.py:62
  109.7 2.1 fusion.86
  111.8 3.2 %fusion.83 = (f32[384]{0:T(512)S(1)}, f32[384,1152]{1,0:T(8,128)S(1)}) fusion(f32[384,1152]{1,0:T(8,128)} %fusion.86, bf16[384,576]{0,1:T(8,128)(2,1)S(1)} %collective-permute-done.1, bf16[576,1152]{1,0:T(8,128)(2,1)} %all-gather.4.cloned.1.call-done, f32[1152]{0:T(1024)S(1)} %get-tuple-element.8, bf16[384,1,1152]{2,0,1:T(8,128)(2,1)} %param.10), kind=kOutput, calls=%fused_computation.132 | convolution fusion | flops 511819392 | bytes 6199296 | tf_op jit(solution)/shard_map/dot_general | solution.py:119
  117.0 7.4 %all-to-all-start.1 = ((bf16[16,24,1152]{2,1,0:T(8,128)(2,1)}), bf16[16,24,1152]{2,1,0:T(8,128)(2,1)S(1)}, u32[]{:S(2)}, u32[]{:S(2)}) async-start(bf16[16,24,1152]{2,1,0:T(8,128)(2,1)} %bitcast.20), calls=%async_computation.1 | async-start | bytes 1769472 | tf_op jit(solution)/shard_map/all_to_all | solution.py:123
  127.0 4.1 %collective-permute-done.4 = bf16[72,1152]{1,0:T(8,128)(2,1)S(1)} collective-permute-done((bf16[72,1152]{1,0:T(8,128)(2,1)S(1)}, bf16[72,1152]{1,0:T(8,128)(2,1)S(1)}, u32[]{:S(2)}, u32[]{:S(2)}) %collective-permute-start.4) | collective-permute-done | bytes 165920 | tf_op jit(solution)/shard_map/ppermute | solution.py:54
  131.7 17.5 %all-to-all-done.1 = bf16[16,24,1152]{2,1,0:T(8,128)(2,1)S(1)} async-done(((bf16[16,24,1152]{2,1,0:T(8,128)(2,1)}), bf16[16,24,1152]{2,1,0:T(8,128)(2,1)S(1)}, u32[]{:S(2)}, u32[]{:S(2)}) %all-to-all-start.1) | async-done | bytes 884768 | tf_op jit(solution)/shard_map/all_to_all | solution.py:123
  150.1 4.8 %convolution_convert_fusion.1 = bf16[384,1728]{0,1:T(8,128)(2,1)S(1)} fusion(bf16[384,1152]{1,0:T(8,128)(2,1)} %bitcast.156, bf16[1728,1152]{1,0:T(8,128)(2,1)} %bitcast.162), kind=kOutput, calls=%fused_computation.24 | convolution fusion | flops 1529487360 | bytes 6193152 | tf_op jit(solution)/shard_map/dot_general | solution.py:66
  154.9 2.7 %copy.33 = bf16[384,1728]{1,0:T(8,128)(2,1)} copy(bf16[384,1728]{0,1:T(8,128)(2,1)S(1)} %convolution_convert_fusion.1) | data formatting | bytes 2654208 | tf_op jit(solution)/shard_map/convert_element_type | solution.py:68
  157.6 5.1 %reshape.169 = bf16[16,24,3,8,72]{4,3,2,1,0:T(8,128)(2,1)} reshape(bf16[384,1728]{1,0:T(8,128)(2,1)} %copy.33) | data formatting | bytes 2654208 | tf_op jit(solution)/shard_map/reshape | solution.py:78
  162.7 2.9 %fusion.78 = (bf16[16,24,1,8,72]{4,3,2,1,0:T(8,128)(2,1)S(1)}, bf16[16,24,1,8,72]{4,3,2,1,0:T(8,128)(2,1)}, bf16[16,24,1,8,72]{4,3,2,1,0:T(8,128)(2,1)}) fusion(bf16[16,24,3,8,72]{4,3,2,1,0:T(8,128)(2,1)} %reshape.169), kind=kLoop, calls=%fused_computation.127 | loop fusion | bytes 2654208 | tf_op jit(solution)/shard_map/slice | solution.py:82
  165.6 4.0 %fusion.85 = (f32[24,8,16]{2,1,0:T(8,128)S(1)}, f32[24,8,16,16]{2,3,1,0:T(8,128)}) fusion(bf16[16,24,1,8,72]{4,3,2,1,0:T(8,128)(2,1)} %get-tuple-element.13, bf16[16,24,1,8,72]{4,3,2,1,0:T(8,128)(2,1)} %get-tuple-element.12), kind=kOutput, calls=%fused_computation.134 | convolution fusion | flops 7225359 | bytes 1093632 | tf_op jit(solution)/shard_map/sub | solution.py:60
  169.6 2.1 fusion.31
  172.5 5.8 %convolution_convert_fusion = bf16[384,1728]{0,1:T(8,128)(2,1)} fusion(bf16[384,1152]{1,0:T(8,128)(2,1)} %bitcast.157, bf16[1728,1152]{1,0:T(8,128)(2,1)} %all-gather.6.cloned.1.call-done), kind=kOutput, calls=%fused_computation.23 | convolution fusion | flops 1529487360 | bytes 6193152 | tf_op jit(solution)/shard_map/dot_general | solution.py:66
  178.4 2.5 %copy.39 = bf16[384,1728]{1,0:T(8,128)(2,1)} copy(bf16[384,1728]{0,1:T(8,128)(2,1)} %convolution_convert_fusion) | data formatting | bytes 2654208 | tf_op jit(solution)/shard_map/convert_element_type | solution.py:68
  180.9 5.1 %reshape.170 = bf16[16,24,3,8,72]{4,3,2,1,0:T(8,128)(2,1)} reshape(bf16[384,1728]{1,0:T(8,128)(2,1)} %copy.39) | data formatting | bytes 2654208 | tf_op jit(solution)/shard_map/reshape | solution.py:78
  185.9 2.9 %fusion.79 = (bf16[16,24,1,8,72]{4,3,2,1,0:T(8,128)(2,1)S(1)}, bf16[16,24,1,8,72]{4,3,2,1,0:T(8,128)(2,1)}, bf16[16,24,1,8,72]{4,3,2,1,0:T(8,128)(2,1)}) fusion(bf16[16,24,3,8,72]{4,3,2,1,0:T(8,128)(2,1)} %reshape.170), kind=kLoop, calls=%fused_computation.128 | loop fusion | bytes 2654208 | tf_op jit(solution)/shard_map/slice | solution.py:82
  188.8 4.0 %fusion.84 = (f32[24,8,16]{2,1,0:T(8,128)S(1)}, f32[24,8,16,16]{2,3,1,0:T(8,128)}) fusion(bf16[16,24,1,8,72]{4,3,2,1,0:T(8,128)(2,1)} %get-tuple-element.16, bf16[16,24,1,8,72]{4,3,2,1,0:T(8,128)(2,1)} %get-tuple-element.15), kind=kOutput, calls=%fused_computation.133 | convolution fusion | flops 7225359 | bytes 1093632 | tf_op jit(solution)/shard_map/sub | solution.py:60
  192.8 2.1 fusion.32
  197.9 28.1 %all_to_all.27 = bf16[16,24,1152]{2,1,0:T(8,128)(2,1)S(1)} all-to-all(bf16[16,24,1152]{2,1,0:T(8,128)(2,1)S(1)} %pad_maximum_fusion.1), channel_id=1, replica_groups=mesh['clip'=8,'seq'=16,'tp'=2] {'seq'}, dimensions={0} | all-to-all | bytes 1769472 | tf_op jit(solution)/shard_map/all_to_all | solution.py:132
  226.0 2.1 fusion.55
  228.1 3.1 %fusion.18 = f32[384,1,1152]{2,0,1:T(8,128)S(1)} fusion(f32[384,1152]{1,0:T(8,128)S(1)} %get-tuple-element.24, f32[384,1152]{1,0:T(8,128)} %fusion.55, bf16[576,1152]{1,0:T(8,128)(2,1)} %all-gather.8.cloned.1.call-done, f32[1152]{0:T(1024)S(1)} %copy-done.10, bf16[384,1152]{1,0:T(8,128)(2,1)} %bitcast.151), kind=kOutput, calls=%fused_computation.22 | convolution fusion | flops 510935040 | bytes 7131648 | tf_op jit(solution)/shard_map/dot_general | solution.py:135
  231.3 3.0 %copy.45 = f32[384,1,1152]{2,1,0:T(1,128)} copy(f32[384,1,1152]{2,0,1:T(8,128)S(1)} %fusion.18) | data formatting | bytes 3538944 | tf_op jit(solution)/shard_map/reshape | solution.py:138
  (76 shorter events, 23.2 us)
Async XLA Ops:
  6.5 1.3 copy-start
  6.5 105.3 %all-gather.4.cloned.1.call-start = ((), (), s32[]{:S(2)}) async-start(), calls=%async_computation.3 | async-start | bytes 1492992 | tf_op jit(solution)/shard_map/all_gather | solution.py:55
  7.9 23.9 %copy-start.2 = (bf16[384,1,1152]{2,0,1:T(8,128)(2,1)S(1)}, bf16[384,1,1152]{2,0,1:T(8,128)(2,1)}, u32[]{:S(2)}) copy-start(bf16[384,1,1152]{2,0,1:T(8,128)(2,1)} %param.10) | copy-start | bytes 2654212
  7.9 6.1 %collective-permute-start.2 = (bf16[72,1152]{1,0:T(8,128)(2,1)S(1)}, bf16[72,1152]{1,0:T(8,128)(2,1)S(1)}, u32[]{:S(2)}, u32[]{:S(2)}) collective-permute-start(bf16[72,1152]{1,0:T(8,128)(2,1)S(1)} %constant_dynamic-slice_fusion.2), channel_id=1, source_target_pairs={{0,3},{1,2},{2,1},{3,0},{4,7},{5,6},{6,5},{7,4},{8,11},{9,10},{10,... | collective-permute-start | bytes 497672 | tf_op jit(solution)/shard_map/ppermute | solution.py:54
  13.9 0.7 copy-start.6
  19.1 50.1 %all-to-all-start = ((f32[32,32,128]{2,1,0:T(8,128)}), f32[32,32,128]{2,1,0:T(8,128)}, u32[]{:S(2)}, u32[]{:S(2)}) async-start(f32[32,32,128]{2,1,0:T(8,128)} %broadcast_in_dim.2), calls=%async_computation | async-start | bytes 1048576 | tf_op jit(solution)/shard_map/all_to_all | solution.py:45
  31.7 140.8 %all-gather.6.cloned.1.call-start = ((), (), s32[]{:S(2)}) async-start(), calls=%async_computation.4 | async-start | bytes 4478976 | tf_op jit(solution)/shard_map/all_gather | solution.py:55
  31.8 36.8 %collective-permute-start = (bf16[384,1152]{1,0:T(8,128)(2,1)S(1)}, bf16[384,1152]{1,0:T(8,128)(2,1)S(1)}, u32[]{:S(2)}, u32[]{:S(2)}) collective-permute-start(bf16[384,1152]{1,0:T(8,128)(2,1)S(1)} %bitcast.149), channel_id=1, source_target_pairs={{0,1},{1,0},{2,3},{3,2},{4,5},{5,4},{6,7},{7,6},{8,9},{9,8},{10,11... | collective-permute-start | bytes 2654216 | tf_op jit(solution)/shard_map/ppermute | solution.py:101
  33.2 35.3 %collective-permute-start.3 = (bf16[216,1152]{1,0:T(8,128)(2,1)S(1)}, bf16[216,1152]{1,0:T(8,128)(2,1)}, u32[]{:S(2)}, u32[]{:S(2)}) collective-permute-start(bf16[216,1152]{1,0:T(8,128)(2,1)S(1)} %constant_dynamic-slice_fusion.1), channel_id=1, source_target_pairs={{0,3},{1,2},{2,1},{3,0},{4,7},{5,6},{6,5},{7,4},{8,11},{9,10},{10,... | collective-permute-start | bytes 1493000 | tf_op jit(solution)/shard_map/ppermute | solution.py:54
  36.4 33.9 %copy-start.11 = (f32[3,1152]{1,0:T(4,128)S(1)}, f32[3,1152]{1,0:T(4,128)}, u32[]{:S(2)}) copy-start(f32[3,1152]{1,0:T(4,128)} %param.15) | copy-start | bytes 41476
  36.4 33.9 %copy-start.12 = (f32[3,1152]{1,0:T(4,128)S(1)}, f32[3,1152]{1,0:T(4,128)}, u32[]{:S(2)}) copy-start(f32[3,1152]{1,0:T(4,128)} %param.14) | copy-start | bytes 41476
  71.0 4.8 %copy-start.13 = (bf16[1152,3,576]{0,2,1:T(8,128)(2,1)S(1)}, bf16[1152,3,576]{0,2,1:T(8,128)(2,1)}, u32[]{:S(2)}) copy-start(bf16[1152,3,576]{0,2,1:T(8,128)(2,1)} %param.16) | copy-start | bytes 11943940
  93.8 18.1 %collective-permute-start.1 = (bf16[384,576]{0,1:T(8,128)(2,1)S(1)}, bf16[384,576]{0,1:T(8,128)(2,1)S(1)}, u32[]{:S(2)}, u32[]{:S(2)}) collective-permute-start(bf16[384,576]{0,1:T(8,128)(2,1)S(1)} %bitcast.165), channel_id=1, source_target_pairs={{0,1},{1,0},{2,3},{3,2},{4,5},{5,4},{6,7},{7,6},{8,9},{9,8},{10,11... | collective-permute-start | bytes 1327112 | tf_op jit(solution)/shard_map/ppermute | solution.py:116
  103.5 5.5 %copy-start.8 = (f32[3,1152]{1,0:T(4,128)S(1)}, f32[3,1152]{1,0:T(4,128)}, u32[]{:S(2)}) copy-start(f32[3,1152]{1,0:T(4,128)} %get-tuple-element.17) | copy-start | bytes 41476
  115.0 0.7 copy-start.9
  117.0 32.2 %all-to-all-start.1 = ((bf16[16,24,1152]{2,1,0:T(8,128)(2,1)}), bf16[16,24,1152]{2,1,0:T(8,128)(2,1)S(1)}, u32[]{:S(2)}, u32[]{:S(2)}) async-start(bf16[16,24,1152]{2,1,0:T(8,128)(2,1)} %bitcast.20), calls=%async_computation.1 | async-start | bytes 1769472 | tf_op jit(solution)/shard_map/all_to_all | solution.py:123
  124.4 103.7 %all-gather.8.cloned.1.call-start = ((), (), s32[]{:S(2)}) async-start(), calls=%async_computation.5 | async-start | bytes 1492992 | tf_op jit(solution)/shard_map/all_gather | solution.py:55
  125.4 5.6 %collective-permute-start.4 = (bf16[72,1152]{1,0:T(8,128)(2,1)S(1)}, bf16[72,1152]{1,0:T(8,128)(2,1)S(1)}, u32[]{:S(2)}, u32[]{:S(2)}) collective-permute-start(bf16[72,1152]{1,0:T(8,128)(2,1)S(1)} %constant_dynamic-slice_fusion), channel_id=1, source_target_pairs={{0,3},{1,2},{2,1},{3,0},{4,7},{5,6},{6,5},{7,4},{8,11},{9,10},{10,... | collective-permute-start | bytes 497672 | tf_op jit(solution)/shard_map/ppermute | solution.py:54
  131.0 0.7 copy-start.7
  149.2 0.9 copy-start.5
  196.5 29.5 %copy-start.4 = (bf16[576,1152]{1,0:T(8,128)(2,1)S(1)}, bf16[576,1152]{1,0:T(8,128)(2,1)}, u32[]{:S(2)}) copy-start(bf16[576,1152]{1,0:T(8,128)(2,1)} %param.19) | copy-start | bytes 3981316
  226.0 2.1 copy-start.3
  226.0 2.1 copy-start.10
  228.1 6.2 %copy-start.1 = (bf16[576,1152]{1,0:T(8,128)(2,1)S(1)}, bf16[576,1152]{1,0:T(8,128)(2,1)}, u32[]{:S(2)}) copy-start(bf16[576,1152]{1,0:T(8,128)(2,1)} %param.17) | copy-start | bytes 3981316
Sparse Core Ops, SparseCore 0:
  14.8 30.2 all-gather.3
  68.7 34.1 all-gather.5
  131.9 29.2 all-gather.7

commit v2 on v1

v2 whole, which is shorter than its diff:
```python
import functools
import math

import jax
import jax.numpy as jnp
from jax import lax
from jax.experimental import pallas as pl
from jax.experimental.pallas import tpu as pltpu
from jax.sharding import PartitionSpec as P

HEAD_DIM = 72
FREQ = 256
LANES = 128
SWAP = [(0, 1), (1, 0)]
VMEM = pl.BlockSpec(memory_space=pltpu.VMEM)
SMEM = pl.BlockSpec(memory_space=pltpu.SMEM)
HBM = pl.BlockSpec(memory_space=pl.ANY)
TERM_ROWS = 32
CHUNKS = 2
SCALE = math.log2(math.e) / math.sqrt(HEAD_DIM)
BF16 = jnp.bfloat16
F32 = jnp.float32


def call(kernel, outs, in_specs, scratch=(), flops=0, nbytes=0, out_specs=None, mib=60):
    return pl.pallas_call(
        kernel,
        out_shape=outs,
        in_specs=in_specs,
        out_specs=out_specs or jax.tree.map(lambda _: VMEM, outs),
        scratch_shapes=list(scratch),
        compiler_params=pltpu.CompilerParams(vmem_limit_bytes=mib * 1024 * 1024),
        cost_estimate=pl.CostEstimate(flops=flops, bytes_accessed=nbytes, transcendentals=0),
    )


def dot_nt(a, b):
    return lax.dot_general(a, b, (((1,), (1,)), ((), ())), preferred_element_type=F32)


def normalise(tokens, shift, scale):
    mean = jnp.mean(tokens, axis=-1, keepdims=True)
    centred = tokens - mean
    variance = jnp.mean(centred * centred, axis=-1, keepdims=True)
    return (centred * lax.rsqrt(variance + 1e-06) * (1.0 + scale) + shift).astype(BF16)


def fetch(source, target, sem):
    copy = pltpu.make_async_copy(source, target, sem)
    copy.start()
    return copy


def window(head):
    first = head * HEAD_DIM // LANES * LANES
    last = -(-(head + 1) * HEAD_DIM // LANES) * LANES
    return first, last


def padded(width):
    return -(-width // LANES) * LANES


def head_queries(queries, head):
    first, last = window(head)
    start = head * HEAD_DIM
    pieces = [queries[start : start + HEAD_DIM]]
    tokens = queries.shape[1]
    if start > first:
        pieces.insert(0, jnp.zeros((start - first, tokens), F32))
    if last > start + HEAD_DIM:
        pieces.append(jnp.zeros((last - start - HEAD_DIM, tokens), F32))
    return jnp.concatenate(pieces, axis=0).astype(BF16)


def head_values(values, head):
    start = head * HEAD_DIM
    ones = jnp.ones((8, values.shape[1]), F32)
    return jnp.concatenate([values[start : start + HEAD_DIM], ones], axis=0).astype(BF16)


def head_scores(queries, keys, head):
    first, last = window(head)
    return jnp.dot(keys[:, first:last], head_queries(queries, head), preferred_element_type=F32)


def head_output(scores, values):
    peak = jnp.max(scores, axis=0, keepdims=True)
    raised = jnp.exp2(scores - peak).astype(BF16)
    out = jnp.dot(values, raised, preferred_element_type=F32)
    return out[:HEAD_DIM] / out[HEAD_DIM : HEAD_DIM + 1]


def modulation_table(terms, table):
    group = terms.shape[0] // TERM_ROWS
    total = jnp.sum(terms[...].reshape(group, TERM_ROWS, LANES), axis=0)
    tiles = table.shape[1] // LANES
    rows = []
    for row in range(3):
        parts = [total[row * tiles + t : row * tiles + t + 1] for t in range(tiles)]
        rows.append(jnp.concatenate(parts, axis=1))
    return jnp.concatenate(rows, axis=0)


def fetch_parts(w_hbm, w, sems):
    half = w.shape[1]
    return [fetch(w_hbm.at[pl.ds(p * half, half)], w.at[p], sems.at[p]) for p in range(3)]


def spatial_kernel(
    heads,
    tok_hbm,
    far_hbm,
    terms_hbm,
    table,
    next_table,
    w_hbm,
    after,
    mods_out,
    next_out,
    q_out,
    k_out,
    v_out,
    att_out,
    tok,
    far,
    terms,
    w,
    q,
    near_q,
    k,
    v,
    scores,
    sems,
):
    count, half = far.shape[0], heads * HEAD_DIM
    in_terms = fetch(terms_hbm, terms, sems.at[3])
    in_far = fetch(far_hbm, far, sems.at[4])
    in_w = fetch_parts(w_hbm, w, sems)
    in_tok = fetch(tok_hbm, tok, sems.at[5])
    near, beyond = pl.ds(0, count), pl.ds(count, count)
    k[:, k.shape[1] - LANES :] = jnp.zeros((2 * count, LANES), BF16)
    in_terms.wait()
    modulation = modulation_table(terms, table)
    mods = table[...] + modulation
    mods_out[...] = mods
    next_out[...] = next_table[...] + modulation
    in_far.wait()
    normed_far = normalise(far[...].astype(F32), mods[0:1], mods[1:2])
    in_w[0].wait()
    q[...] = dot_nt(w[0], normed_far) * SCALE
    in_w[1].wait()
    k[beyond, :half] = dot_nt(normed_far, w[1]).astype(BF16)
    in_tok.wait()
    normed = normalise(tok[...].astype(F32), mods[0:1], mods[1:2])
    k[near, :half] = dot_nt(normed, w[1]).astype(BF16)
    out_k = fetch(k, k_out, sems.at[6])
    for head in range(heads):
        scores[head] = head_scores(q, k, head)
    in_w[2].wait()
    values = dot_nt(w[2], normed)
    for head in range(heads):
        v[head, :, :count] = head_values(values, head)
    values = dot_nt(w[2], normed_far)
    for head in range(heads):
        v[head, :, count:] = head_values(values, head)
    out_v = fetch(v, v_out, sems.at[7])
    near_q[...] = (dot_nt(w[0], normed) * SCALE).astype(BF16)
    out_q = fetch(near_q, q_out, sems.at[8])
    outs = [head_output(scores[head], v[head]) for head in range(heads)]
    att_out[...] = jnp.concatenate(outs, axis=0).T.astype(BF16)
    for copy in (out_k, out_v, out_q):
        copy.wait()


def near_kernel(
    heads, q_hbm, k_hbm, v_hbm, tok_hbm, mods, w_hbm, part_out, q, k, v, tok, w, scores, sems
):
    in_q = fetch(q_hbm, q, sems.at[0])
    in_k = fetch(k_hbm, k, sems.at[1])
    in_v = fetch(v_hbm, v, sems.at[2])
    in_w = fetch(w_hbm, w, sems.at[3])
    in_tok = fetch(tok_hbm, tok, sems.at[4])
    in_q.wait()
    in_k.wait()
    queries = q[...].astype(F32)
    for head in range(heads):
        scores[head] = head_scores(queries, k, head)
    in_v.wait()
    outs = [head_output(scores[head], v[head]) for head in range(heads)]
    attended = jnp.concatenate(outs, axis=0).T.astype(BF16)
    in_w.wait()
    projected = jnp.dot(attended, w[...], preferred_element_type=F32)
    in_tok.wait()
    part_out[...] = tok[...].astype(F32) + mods[2:3] * projected


def piece_kernel(clip, first_hbm, second_hbm, after, out_hbm, piece, sems):
    rows = piece.shape[0]
    split = first_hbm.shape[0] // rows
    index = clip[0]

    @pl.when(index < split)
    def _():
        span = pl.ds(pl.multiple_of(index * rows, rows), rows)
        fetch(first_hbm.at[span], piece, sems.at[0]).wait()

    @pl.when(index >= split)
    def _():
        span = pl.ds(pl.multiple_of((index - split) * rows, rows), rows)
        fetch(second_hbm.at[span], piece, sems.at[0]).wait()

    fetch(piece, out_hbm, sems.at[1]).wait()


def middle_kernel(
    part_hbm, att, w_hbm, mods, next_mods, middle_hbm, normed_out, part, w, middle, sems
):
    in_w = fetch(w_hbm, w, sems.at[0])
    in_part = fetch(part_hbm, part, sems.at[1])
    in_w.wait()
    projected = jnp.dot(att[...], w[...], preferred_element_type=F32)
    in_part.wait()
    middle[...] = part[...] + mods[2:3] * projected
    copy = fetch(middle, middle_hbm, sems.at[2])
    normed_out[...] = normalise(middle[...], next_mods[0:1], next_mods[1:2])
    copy.wait()


def temporal_kernel(
    heads, positions, moved, own_hbm, other_hbm, att_out, w, k, scores, out, sems
):
    half = heads * HEAD_DIM
    count, width = moved.shape
    depth = count // positions
    groups = positions // 8
    block = depth * 8
    copies = []
    for part in range(3):
        for side, source in enumerate((own_hbm, other_hbm)):
            rows = pl.ds(side * half, half)
            copies.append(
                fetch(
                    source.at[pl.ds(part * half, half)],
                    w.at[part, rows],
                    sems.at[part * 2 + side],
                )
            )
    here = lax.rem(lax.broadcasted_iota(jnp.int32, (block, block), 0), 8)
    there = lax.rem(lax.broadcasted_iota(jnp.int32, (block, block), 1), 8)
    bias = jnp.where(here == there, 0.0, -1e30)
    grid = moved[...].astype(F32).reshape(depth, positions, width)
    tokens = jnp.concatenate(
        [grid[:, g * 8 : g * 8 + 8].reshape(block, width) for g in range(groups)], axis=0
    ).astype(BF16)
    copies[0].wait()
    copies[1].wait()
    queries = dot_nt(w[0], tokens) * SCALE
    copies[2].wait()
    copies[3].wait()
    k[...] = dot_nt(tokens, w[1]).astype(BF16)
    copies[4].wait()
    copies[5].wait()
    values = dot_nt(w[2], tokens)
    spans = [slice(g * block, (g + 1) * block) for g in range(groups)]
    for head in range(2 * heads):
        first, last = window(head)
        head_q = head_queries(queries, head)
        for g, span in enumerate(spans):
            scores[head * groups + g] = (
                jnp.dot(k[span, first:last], head_q[:, span], preferred_element_type=F32) + bias
            )
    for head in range(2 * heads):
        head_v = head_values(values, head)
        outs = [
            head_output(scores[head * groups + g], head_v[:, span])
            for g, span in enumerate(spans)
        ]
        out[pl.ds(head * HEAD_DIM, HEAD_DIM), :] = jnp.concatenate(outs, axis=1)
    result = out[...].T
    by_group = [result[span].reshape(depth, 8, 2 * half) for span in spans]
    att_out[...] = jnp.concatenate(by_group, axis=1).reshape(count, 2 * half).astype(BF16)


def final_kernel(att, own_w, other_w, middle_hbm, mods, out_hbm, w, middle, out, sems):
    half = own_w.shape[0]
    copies = [
        fetch(own_w, w.at[pl.ds(0, half)], sems.at[0]),
        fetch(other_w.at[pl.ds(3 * half, half)], w.at[pl.ds(half, half)], sems.at[1]),
        fetch(middle_hbm, middle, sems.at[2]),
    ]
    count, width = middle.shape
    tiles = width // LANES
    chunk = count // CHUNKS
    copies[0].wait()
    copies[1].wait()
    stores = []
    for part in range(CHUNKS):
        rows = pl.ds(part * chunk, chunk)
        projected = jnp.dot(att[rows, :], w[...], preferred_element_type=F32)
        if part == 0:
            copies[2].wait()
        result = middle[rows, :] + mods[2:3] * projected
        base = part * chunk * tiles
        for tile in range(tiles):
            out[pl.ds(base + tile, chunk, tiles), :] = result[
                :, tile * LANES : (tile + 1) * LANES
            ]
        span = pl.ds(base, chunk * tiles)
        stores.append(fetch(out.at[span], out_hbm.at[span], sems.at[3 + part]))
    for store in stores:
        store.wait()


def time_features(timestep):
    half = FREQ // 2
    ladder = jnp.exp(-math.log(10000.0) * jnp.arange(half, dtype=F32) / half)
    angles = timestep.astype(F32)[:, None] * ladder[None, :]
    return jnp.concatenate([jnp.cos(angles), jnp.sin(angles)], axis=-1)


def modulation_terms(timestep, embed_weight, block_weight):
    features = time_features(timestep)
    embedded = jax.nn.silu(
        jnp.dot(features, embed_weight.astype(F32), precision=lax.Precision.HIGHEST)
    )
    count, width = block_weight.shape
    start = lax.axis_index(("seq", "tp")) * count
    mine = lax.dynamic_slice_in_dim(embedded, start, count, 1)
    term = jnp.dot(mine, block_weight.astype(F32), precision=lax.Precision.HIGHEST)
    tiles = width // LANES
    return jnp.pad(term.reshape(tiles, LANES), ((0, TERM_ROWS - tiles), (0, 0)))


def follows(index, value):
    return index + (value.astype(F32) > 1e30).astype(jnp.int32)


def eighth(weight):
    rows = weight.shape[0] // lax.axis_size("clip")
    return lax.dynamic_slice_in_dim(weight, lax.axis_index("clip") * rows, rows, 0)


def body(
    frames,
    timestep,
    embed_weight,
    block_weight,
    spatial_table,
    temporal_table,
    spatial_qkv,
    spatial_out,
    temporal_qkv,
    temporal_out,
):
    width = frames.shape[-1]
    tokens = frames.reshape(-1, width)
    count = tokens.shape[0]
    half = spatial_out.shape[0]
    heads = half // HEAD_DIM
    far = lax.ppermute(tokens, "tp", SWAP)
    spatial_in = jnp.transpose(spatial_qkv, (1, 2, 0)).reshape(-1, width)
    temporal_in = jnp.transpose(temporal_qkv, (1, 2, 0)).reshape(-1, width)

    shape = jax.ShapeDtypeStruct
    dma = pltpu.SemaphoreType.DMA
    group = lax.axis_size("seq") * lax.axis_size("tp")
    across = [(i, i ^ 3) for i in range(group)]
    clip = lax.axis_index("clip")
    out_piece = lax.ppermute(eighth(spatial_out), ("seq", "tp"), across)
    term = modulation_terms(timestep, embed_weight, block_weight)
    copies = jnp.broadcast_to(term[None], (group,) + term.shape).reshape(-1, LANES)
    terms = lax.all_to_all(copies, ("seq", "tp"), 0, 0, tiled=True)
    spatial_out_other = lax.all_gather(out_piece, "clip", axis=0, tiled=True)
    rows = 4 * half // lax.axis_size("clip")
    own_piece = call(
        piece_kernel,
        shape((rows, width), BF16),
        [SMEM] + [HBM] * 3,
        [pltpu.VMEM((rows, width), BF16), dma((2,))],
        flops=20_000_000_000,
        nbytes=1_500_000,
        out_specs=HBM,
    )(clip.astype(jnp.int32).reshape(1), temporal_in, temporal_out, far)
    piece = lax.ppermute(own_piece, ("seq", "tp"), across)

    tokens_shape = (count, width)
    k_shape = (2 * count, padded(half))
    v_shape = (heads, HEAD_DIM + 8, 2 * count)
    all_scores = pltpu.VMEM((heads, 2 * count, count), F32)
    spatial_mods, temporal_mods, near_q, k, v, far_attended = call(
        functools.partial(spatial_kernel, heads),
        (
            shape((3, width), F32),
            shape((3, width), F32),
            shape((half, count), BF16),
            shape(k_shape, BF16),
            shape(v_shape, BF16),
            shape((count, half), BF16),
        ),
        [HBM] * 3 + [VMEM] * 2 + [HBM] * 2,
        [
            pltpu.VMEM(tokens_shape, BF16),
            pltpu.VMEM(tokens_shape, BF16),
            pltpu.VMEM(terms.shape, F32),
            pltpu.VMEM((3, half, width), BF16),
            pltpu.VMEM((half, count), F32),
            pltpu.VMEM((half, count), BF16),
            pltpu.VMEM(k_shape, BF16),
            pltpu.VMEM(v_shape, BF16),
            all_scores,
            dma((9,)),
        ],
        flops=14 * count * half * width,
        nbytes=14_000_000,
        out_specs=(VMEM, VMEM, HBM, HBM, HBM, VMEM),
    )(tokens, far, terms, spatial_table, temporal_table, spatial_in, own_piece)
    attended = lax.ppermute(far_attended, "tp", SWAP)
    late = follows(0, far_attended[0, 0]) > 0
    piece = jnp.where(late, jnp.zeros_like(piece), piece)
    gathered = lax.all_gather(piece, "clip", axis=0, tiled=True)
    part = call(
        functools.partial(near_kernel, heads),
        shape(tokens_shape, F32),
        [HBM] * 4 + [VMEM, HBM],
        [
            pltpu.VMEM((half, count), BF16),
            pltpu.VMEM(k_shape, BF16),
            pltpu.VMEM(v_shape, BF16),
            pltpu.VMEM(tokens_shape, BF16),
            pltpu.VMEM((half, width), BF16),
            all_scores,
            dma((5,)),
        ],
        flops=6 * count * half * width,
        nbytes=8_000_000,
    )(near_q, k, v, tokens, spatial_mods, spatial_out)
    middle, normed = call(
        middle_kernel,
        (shape(tokens_shape, F32), shape(tokens_shape, BF16)),
        [HBM, VMEM, HBM, VMEM, VMEM],
        [
            pltpu.VMEM(tokens_shape, F32),
            pltpu.VMEM((half, width), BF16),
            pltpu.VMEM(tokens_shape, F32),
            dma((3,)),
        ],
        flops=2 * count * half * width,
        nbytes=6_000_000,
        out_specs=(HBM, VMEM),
        mib=60,
    )(part, attended, spatial_out_other, spatial_mods, temporal_mods)

    moved = lax.all_to_all(normed, "seq", 0, 0, tiled=True)
    positions = count // lax.axis_size("seq")
    block = 8 * lax.axis_size("seq")
    attended = call(
        functools.partial(temporal_kernel, heads, positions),
        shape((count, 2 * half), BF16),
        [VMEM, HBM, HBM],
        [
            pltpu.VMEM((3, 2 * half, width), BF16),
            pltpu.VMEM((count, 2 * half), BF16),
            pltpu.VMEM((2 * heads * (positions // 8), block, block), F32),
            pltpu.VMEM((2 * half, count), F32),
            dma((6,)),
        ],
        flops=12 * count * half * width,
        nbytes=10_000_000,
        mib=60,
    )(moved, temporal_in, gathered)
    returned = lax.all_to_all(attended, "seq", 0, 0, tiled=True)
    tiles = width // LANES
    out = call(
        final_kernel,
        shape((count * tiles, LANES), F32),
        [VMEM, HBM, HBM, HBM, VMEM],
        [
            pltpu.VMEM((2 * half, width), BF16),
            pltpu.VMEM((count, width), F32),
            pltpu.VMEM((count * tiles, LANES), F32),
            dma((3 + CHUNKS,)),
        ],
        flops=4 * count * half * width,
        nbytes=8_000_000,
        out_specs=HBM,
        mib=60,
    )(returned, temporal_out, gathered, middle, temporal_mods)
    return out.reshape(frames.shape)


def solution(mesh):
    return jax.shard_map(
        body,
        mesh=mesh,
        in_specs=(
            P("tp", ("clip", "seq"), None),
            P("clip"),
            P(),
            P(("seq", "tp"), None),
            P(),
            P(),
            P(None, None, "tp"),
            P("tp", None),
            P(None, None, "tp"),
            P("tp", None),
        ),
        out_specs=P("tp", ("clip", "seq"), None),
        check_vma=False,
    )
```

time: 246 us -> 167 us (0.68); the launches traced: 241 us -> 166 us
  matrix products: 69.7 us -> 0.68 us
  Pallas kernels: 0 us -> 43.8 us
  waiting for transfers between devices: 58.8 us -> 17.8 us
  blocking collectives: 28.1 us -> 63.7 us
  local copies, waits for them, and re-layouts: 34.6 us -> 7.36 us
  starting transfers between devices: 27.3 us -> 17.2 us
  other arithmetic: 8.31 us -> 0.95 us
    dot_general x14 -> x2, matrix products: 45.6 us -> 0.68 us  [the longest x1 0.36 us: modulation_terms(): jnp.dot(features, embed_weight.astype(F32), precision=lax.Precision.HIGHEST)]
    pallas_call x0 -> x6, Pallas kernels: none -> 43.8 us  [the longest x1 12.4 us: body(): call(functools.partial(spatial_kernel, heads), (shape((3, width), F32), s...]
    all_to_all x0 -> x1, blocking collectives: none -> 34.8 us  [body(): moved = lax.all_to_all(normed, 'seq', 0, 0, tiled=True)]
    sub x4 -> x0, matrix products: 24.1 us -> none  [attend(): raised = jnp.exp(scores - peak)]
    ppermute x5 -> x4, waiting for transfers between devices: 41.3 us -> 17.6 us  [the longest x1 12.4 us: body(): out_piece = lax.ppermute(eighth(spatial_out), ('seq', 'tp'), across)]
    all_to_all x2 -> x1, waiting for transfers between devices: 17.5 us -> 0.14 us  [body(): terms = lax.all_to_all(copies, ('seq', 'tp'), 0, 0, tiled=True)]
    reshape x4 -> x0, local copies, waits for them, and re-layouts: 13.2 us -> none  [the longest x2 10.1 us: temporal_attend(): grid = qkv.reshape(depth, -1, 3, 8, HEAD_DIM)]
    all_to_all x2 -> x1, starting transfers between devices: 20 us -> 12.2 us  [body(): terms = lax.all_to_all(copies, ('seq', 'tp'), 0, 0, tiled=True)]
  transfers between devices with their start and end apart: 10 -> 7, of which waited for: 4 -> 4; matrix products, arithmetic and copies ran while one was open for 42% -> 3% of each run, Pallas kernels for 0% -> 17%
where the time goes in v2:
time: 167 us; the launch traced here: 166 us
  blocking collectives  63.7 us (38%)
  Pallas kernels  43.8 us (26%)
  waiting for transfers between devices  17.8 us (11%)
  starting transfers between devices  17.2 us (10%)
  between operations  14.9 us (9%)
  local copies, waits for them, and re-layouts  7.36 us (4%)
    all_to_all x1, blocking collectives, body(): moved = lax.all_to_all(normed, 'seq', 0, 0, tiled=True)  34.8 us
    all_to_all x1, blocking collectives, body(): returned = lax.all_to_all(attended, 'seq', 0, 0, tiled=True)  28.9 us
    pallas_call x1, Pallas kernels, body(): call(functools.partial(spatial_kernel, heads), (shape((3, width), F32), s...  12.4 us
    ppermute x1, waiting for transfers between devices, body(): out_piece = lax.ppermute(eighth(spatial_out), ('seq', 'tp'), across)  12.4 us
    all_to_all x1, starting transfers between devices, body(): terms = lax.all_to_all(copies, ('seq', 'tp'), 0, 0, tiled=True)  12.2 us
    pallas_call x1, Pallas kernels, body(): call(functools.partial(temporal_kernel, heads, positions), shape((count,...  10.2 us
    pallas_call x1, Pallas kernels, body(): call(functools.partial(near_kernel, heads), shape(tokens_shape, F32), [HB...  8.03 us
    pallas_call x1, Pallas kernels, body(): call(middle_kernel, (shape(tokens_shape, F32), shape(tokens_shape, BF16))...  5.72 us
  transfers between devices with their start and end apart: 7, of which 4 were waited for; matrix products, arithmetic and copies ran while one was open for 3% of the time, Pallas kernels for 17%

profile of v2, /device:TPU:4, one launch (start us, length us, event | category | flops | bytes accessed | tf_op | source)
XLA Modules:
  0.0 166.4 jit_solution(13258760811371406765)
XLA Ops:
  6.5 2.2 %collective-permute-start = (bf16[384,1152]{1,0:T(8,128)(2,1)}, bf16[384,1152]{1,0:T(8,128)(2,1)S(1)}, u32[]{:S(2)}, u32[]{:S(2)}) collective-permute-start(bf16[384,1152]{1,0:T(8,128)(2,1)} %bitcast.34), channel_id=1, source_target_pairs={{0,1},{1,0},{2,3},{3,2},{4,5},{5,4},{6,7},{7,6},{8,9},{9,8},{10,11... | collective-permute-start | bytes 2654216 | tf_op jit(solution)/shard_map/ppermute | solution.py:361
  8.8 0.9 constant_dynamic-slice_fusion
  9.7 0.5 collective-permute-start.2
  10.9 1.1 dot_general.12
  12.0 0.1 fusion.9
  12.1 0.4 convolution_reduce_fusion
  12.4 0.3 fusion
  12.8 0.9 broadcast_in_dim.4
  13.6 12.2 %all-to-all-start = ((f32[32,32,128]{2,1,0:T(8,128)}), f32[32,32,128]{2,1,0:T(8,128)S(1)}, u32[]{:S(2)}, u32[]{:S(2)}) async-start(f32[32,32,128]{2,1,0:T(8,128)} %broadcast_in_dim.4), calls=%async_computation | async-start | bytes 1048576 | tf_op jit(solution)/shard_map/all_to_all | solution.py:373
  25.8 0.0 all-gather.3.cloned.1.call-start
  25.9 12.4 %collective-permute-done.2 = bf16[72,1152]{1,0:T(8,128)(2,1)S(1)} collective-permute-done((bf16[72,1152]{1,0:T(8,128)(2,1)S(1)}, bf16[72,1152]{1,0:T(8,128)(2,1)S(1)}, u32[]{:S(2)}, u32[]{:S(2)}) %collective-permute-start.2) | collective-permute-done | bytes 165920 | tf_op jit(solution)/shard_map/ppermute | solution.py:370
  38.2 0.7 copy-done.3
  38.9 0.0 all-gather.3.cloned.1.call-update
  38.9 0.0 all-gather.5.cloned.1.call-start
  39.0 0.9 copy-done.4
  39.9 1.9 %shard_map.100.after = bf16[288,1152]{1,0:T(8,128)(2,1)} custom-call(s32[1]{0:T(128)} %bitcast.10.clip, bf16[1728,1152]{1,0:T(8,128)(2,1)} %bitcast.41, bf16[576,1152]{1,0:T(8,128)(2,1)} %own_w.1, bf16[384,1152]{1,0:T(8,128)(2,1)} %copy-done.4), custom_call_target="tpu_custom_call" | custom-call | flops 20000000000 | bytes 1500000 | tf_op jit(solution)/shard_map/pallas_call | solution.py:376
  41.8 0.1 collective-permute-start.3
  41.9 0.1 all-to-all-done
  42.1 0.8 copy-done.1
  42.9 12.4 %shard_map.101 = (f32[3,1152]{1,0:T(4,128)}, f32[3,1152]{1,0:T(4,128)}, bf16[576,384]{1,0:T(8,128)(2,1)}, bf16[768,640]{1,0:T(8,128)(2,1)}, bf16[8,80,768]{2,1,0:T(8,128)(2,1)}, /*index=5*/bf16[384,576]{1,0:T(8,128)(2,1)}) custom-call(bf16[384,1152]{1,0:T(8,128)(2,1)} %bitcast.35, bf16[384,1152]{1,0:T(8,128)(2,1)} %copy-done.4, f32[1024,128]{1,0:T(8,128)} %bitcast.37, ...), custom_call_target="tpu_custom_call" | custom-call | flops 3567255552 | bytes 14000000 | tf_op jit(solution)/shard_map/pallas_call | solution.py:391
  55.2 1.2 slice.3
  57.1 1.6 collective-permute-done.3
  58.7 0.9 broadcast_select_fusion
  59.7 2.1 %collective-permute-start.1 = (bf16[384,576]{1,0:T(8,128)(2,1)S(1)}, bf16[384,576]{1,0:T(8,128)(2,1)S(1)}, u32[]{:S(2)}, u32[]{:S(2)}) collective-permute-start(bf16[384,576]{1,0:T(8,128)(2,1)S(1)} %copy-done.5), channel_id=1, source_target_pairs={{0,1},{1,0},{2,3},{3,2},{4,5},{5,4},{6,7},{7,6},{8,9},{9,8},{10,11... | collective-permute-start | bytes 1327112 | tf_op jit(solution)/shard_map/ppermute | solution.py:418
  61.8 8.0 %shard_map.102.part_hbm = f32[384,1152]{1,0:T(8,128)} custom-call(bf16[576,384]{1,0:T(8,128)(2,1)} %get-tuple-element.13.q_hbm, bf16[768,640]{1,0:T(8,128)(2,1)} %get-tuple-element.14.k_hbm, bf16[8,80,768]{2,1,0:T(8,128)(2,1)} %get-tuple-element.15.v_hbm, bf16[384,1152]{1,0:T(8,128)(2,1)} %bitcast.36, f32[3,1152]{1,0:T(4,128)} %get-tuple-element.16.mods, ...), custom_call_target="tpu_custom_call" | custom-call | flops 1528823808 | bytes 8000000 | tf_op jit(solution)/shard_map/pallas_call | solution.py:422
  69.8 3.7 %collective-permute-done.1.att = bf16[384,576]{1,0:T(8,128)(2,1)S(1)} collective-permute-done((bf16[384,576]{1,0:T(8,128)(2,1)S(1)}, bf16[384,576]{1,0:T(8,128)(2,1)S(1)}, u32[]{:S(2)}, u32[]{:S(2)}) %collective-permute-start.1) | collective-permute-done | bytes 442400 | tf_op jit(solution)/shard_map/ppermute | solution.py:418
  73.5 0.8 copy-done.2
  74.3 5.7 %shard_map.103 = (f32[384,1152]{1,0:T(8,128)}, bf16[384,1152]{1,0:T(8,128)(2,1)}) custom-call(f32[384,1152]{1,0:T(8,128)} %shard_map.102.part_hbm, bf16[384,576]{1,0:T(8,128)(2,1)} %copy-done.2, bf16[576,1152]{1,0:T(8,128)(2,1)} %all-gather.3.cloned.1.call-done.w_hbm, f32[3,1152]{1,0:T(4,128)} %get-tuple-element.16.mods, ...), custom_call_target="tpu_custom_call" | custom-call | flops 509607936 | bytes 6000000 | tf_op jit(solution)/shard_map/pallas_call | solution.py:438
  80.0 34.8 %all_to_all.30 = bf16[16,24,1152]{2,1,0:T(8,128)(2,1)} all-to-all(bf16[16,24,1152]{2,1,0:T(8,128)(2,1)} %bitcast.31), channel_id=1, replica_groups=mesh['clip'=8,'seq'=16,'tp'=2] {'seq'}, dimensions={0} | all-to-all | bytes 1769472 | tf_op jit(solution)/shard_map/all_to_all | solution.py:454
  114.8 10.2 %shard_map.104 = bf16[384,1152]{1,0:T(8,128)(2,1)} custom-call(bf16[384,1152]{1,0:T(8,128)(2,1)} %bitcast.32, bf16[1728,1152]{1,0:T(8,128)(2,1)} %bitcast.42, bf16[2304,1152]{1,0:T(8,128)(2,1)} %all-gather.5.cloned.1.call-done.other_hbm.other_w), custom_call_target="tpu_custom_call" | custom-call | flops 3057647616 | bytes 10000000 | tf_op jit(solution)/shard_map/pallas_call | solution.py:457
  125.0 28.9 %all_to_all.31 = bf16[16,24,1152]{2,1,0:T(8,128)(2,1)} all-to-all(bf16[16,24,1152]{2,1,0:T(8,128)(2,1)} %bitcast.33), channel_id=1, replica_groups=mesh['clip'=8,'seq'=16,'tp'=2] {'seq'}, dimensions={0} | all-to-all | bytes 1769472 | tf_op jit(solution)/shard_map/all_to_all | solution.py:472
  153.9 5.6 %shard_map.105 = f32[3456,128]{1,0:T(8,128)} custom-call(bf16[384,1152]{1,0:T(8,128)(2,1)} %bitcast.30, bf16[576,1152]{1,0:T(8,128)(2,1)} %own_w.1, bf16[2304,1152]{1,0:T(8,128)(2,1)} %all-gather.5.cloned.1.call-done.other_hbm.other_w, f32[384,1152]{1,0:T(8,128)} %get-tuple-element.20.middle_hbm, f32[3,1152]{1,0:T(4,128)} %get-tuple-element.18.next_mods.mods), custom_call_target="tpu_custom_call" | custom-call | flops 1019215872 | bytes 8000000 | tf_op jit(solution)/shard_map/pallas_call | solution.py:474
  (14 shorter events, 0.0 us)
Async XLA Ops:
  6.5 5.5 %copy-start = (bf16[256,1152]{1,0:T(8,128)(2,1)S(1)}, bf16[256,1152]{1,0:T(8,128)(2,1)}, u32[]{:S(2)}) copy-start(bf16[256,1152]{1,0:T(8,128)(2,1)} %param.12) | copy-start | bytes 1769476
  6.5 32.4 %collective-permute-start = (bf16[384,1152]{1,0:T(8,128)(2,1)}, bf16[384,1152]{1,0:T(8,128)(2,1)S(1)}, u32[]{:S(2)}, u32[]{:S(2)}) collective-permute-start(bf16[384,1152]{1,0:T(8,128)(2,1)} %bitcast.34), channel_id=1, source_target_pairs={{0,1},{1,0},{2,3},{3,2},{4,5},{5,4},{6,7},{7,6},{8,9},{9,8},{10,11... | collective-permute-start | bytes 2654216 | tf_op jit(solution)/shard_map/ppermute | solution.py:361
  9.7 28.5 %collective-permute-start.2 = (bf16[72,1152]{1,0:T(8,128)(2,1)S(1)}, bf16[72,1152]{1,0:T(8,128)(2,1)S(1)}, u32[]{:S(2)}, u32[]{:S(2)}) collective-permute-start(bf16[72,1152]{1,0:T(8,128)(2,1)S(1)} %constant_dynamic-slice_fusion), channel_id=1, source_target_pairs={{0,3},{1,2},{2,1},{3,0},{4,7},{5,6},{6,5},{7,4},{8,11},{9,10},{10,... | collective-permute-start | bytes 497672 | tf_op jit(solution)/shard_map/ppermute | solution.py:370
  13.6 28.4 %all-to-all-start = ((f32[32,32,128]{2,1,0:T(8,128)}), f32[32,32,128]{2,1,0:T(8,128)S(1)}, u32[]{:S(2)}, u32[]{:S(2)}) async-start(f32[32,32,128]{2,1,0:T(8,128)} %broadcast_in_dim.4), calls=%async_computation | async-start | bytes 1048576 | tf_op jit(solution)/shard_map/all_to_all | solution.py:373
  25.8 47.7 %all-gather.3.cloned.1.call-start = ((), (), s32[]{:S(2)}) async-start(), calls=%async_computation.3 | async-start | bytes 1492992 | tf_op jit(solution)/shard_map/all_gather | solution.py:374
  38.2 0.7 copy-start.3
  38.9 75.9 %all-gather.5.cloned.1.call-start = ((), (), s32[]{:S(2)}) async-start(), calls=%async_computation.4 | async-start | bytes 5971968 | tf_op jit(solution)/shard_map/all_gather | solution.py:421
  39.0 0.9 copy-start.4
  41.8 16.9 %collective-permute-start.3 = (bf16[288,1152]{1,0:T(8,128)(2,1)}, bf16[288,1152]{1,0:T(8,128)(2,1)S(1)}, u32[]{:S(2)}, u32[]{:S(2)}) collective-permute-start(bf16[288,1152]{1,0:T(8,128)(2,1)} %shard_map.100.after), channel_id=1, source_target_pairs={{0,3},{1,2},{2,1},{3,0},{4,7},{5,6},{6,5},{7,4},{8,11},{9,10},{10,... | collective-permute-start | bytes 1990664 | tf_op jit(solution)/shard_map/ppermute | solution.py:385
  42.1 0.8 copy-start.1
  55.2 4.4 %copy-start.5 = (bf16[384,576]{1,0:T(8,128)(2,1)S(1)}, bf16[384,576]{1,0:T(8,128)(2,1)}, u32[]{:S(2)}) copy-start(bf16[384,576]{1,0:T(8,128)(2,1)} %get-tuple-element.17) | copy-start | bytes 1327108
  59.7 13.8 %collective-permute-start.1 = (bf16[384,576]{1,0:T(8,128)(2,1)S(1)}, bf16[384,576]{1,0:T(8,128)(2,1)S(1)}, u32[]{:S(2)}, u32[]{:S(2)}) collective-permute-start(bf16[384,576]{1,0:T(8,128)(2,1)S(1)} %copy-done.5), channel_id=1, source_target_pairs={{0,1},{1,0},{2,3},{3,2},{4,5},{5,4},{6,7},{7,6},{8,9},{9,8},{10,11... | collective-permute-start | bytes 1327112 | tf_op jit(solution)/shard_map/ppermute | solution.py:418
  73.5 0.8 copy-start.2
Sparse Core Ops, SparseCore 0:
  39.0 29.9 all-gather.2
  70.8 39.2 all-gather.4

commit v3 on v2

--- a/solution.py
+++ b/solution.py
@@ -13,7 +13,6 @@
 LANES = 128
 SWAP = [(0, 1), (1, 0)]
 VMEM = pl.BlockSpec(memory_space=pltpu.VMEM)
-SMEM = pl.BlockSpec(memory_space=pltpu.SMEM)
 HBM = pl.BlockSpec(memory_space=pl.ANY)
 TERM_ROWS = 32
 CHUNKS = 2
@@ -22,14 +21,14 @@
 F32 = jnp.float32
 
 
-def call(kernel, outs, in_specs, scratch=(), flops=0, nbytes=0, out_specs=None, mib=60):
+def call(kernel, outs, in_specs, scratch=(), flops=0, nbytes=0, out_specs=None, mib=63.1):
     return pl.pallas_call(
         kernel,
         out_shape=outs,
         in_specs=in_specs,
         out_specs=out_specs or jax.tree.map(lambda _: VMEM, outs),
         scratch_shapes=list(scratch),
-        compiler_params=pltpu.CompilerParams(vmem_limit_bytes=mib * 1024 * 1024),
+        compiler_params=pltpu.CompilerParams(vmem_limit_bytes=int(mib * 1024 * 1024)),
         cost_estimate=pl.CostEstimate(flops=flops, bytes_accessed=nbytes, transcendentals=0),
     )
 
@@ -118,7 +117,7 @@
     after,
     mods_out,
     next_out,
-    q_out,
+    normed_out,
     k_out,
     v_out,
     att_out,
@@ -127,7 +126,6 @@
     terms,
     w,
     q,
-    near_q,
     k,
     v,
     scores,
@@ -153,6 +151,8 @@
     k[beyond, :half] = dot_nt(normed_far, w[1]).astype(BF16)
     in_tok.wait()
     normed = normalise(tok[...].astype(F32), mods[0:1], mods[1:2])
+    tok[...] = normed
+    out_normed = fetch(tok, normed_out, sems.at[8])
     k[near, :half] = dot_nt(normed, w[1]).astype(BF16)
     out_k = fetch(k, k_out, sems.at[6])
     for head in range(heads):
@@ -165,51 +165,57 @@
     for head in range(heads):
         v[head, :, count:] = head_values(values, head)
     out_v = fetch(v, v_out, sems.at[7])
-    near_q[...] = (dot_nt(w[0], normed) * SCALE).astype(BF16)
-    out_q = fetch(near_q, q_out, sems.at[8])
     outs = [head_output(scores[head], v[head]) for head in range(heads)]
     att_out[...] = jnp.concatenate(outs, axis=0).T.astype(BF16)
-    for copy in (out_k, out_v, out_q):
+    for copy in (out_k, out_v, out_normed):
         copy.wait()
 
 
 def near_kernel(
-    heads, q_hbm, k_hbm, v_hbm, tok_hbm, mods, w_hbm, part_out, q, k, v, tok, w, scores, sems
+    heads,
+    normed_hbm,
+    in_w_hbm,
+    k_hbm,
+    v_hbm,
+    tok_hbm,
+    mods,
+    w_hbm,
+    part_out,
+    normed,
+    in_w,
+    k,
+    v,
+    tok,
+    w,
+    scores,
+    sems,
 ):
-    in_q = fetch(q_hbm, q, sems.at[0])
-    in_k = fetch(k_hbm, k, sems.at[1])
-    in_v = fetch(v_hbm, v, sems.at[2])
-    in_w = fetch(w_hbm, w, sems.at[3])
-    in_tok = fetch(tok_hbm, tok, sems.at[4])
-    in_q.wait()
-    in_k.wait()
-    queries = q[...].astype(F32)
+    half = heads * HEAD_DIM
+    copies = [
+        fetch(normed_hbm, normed, sems.at[0]),
+        fetch(in_w_hbm.at[pl.ds(0, half)], in_w, sems.at[1]),
+        fetch(k_hbm, k, sems.at[2]),
+        fetch(v_hbm, v, sems.at[3]),
+        fetch(w_hbm, w, sems.at[4]),
+        fetch(tok_hbm, tok, sems.at[5]),
+    ]
+    copies[0].wait()
+    copies[1].wait()
+    queries = dot_nt(in_w[...], normed[...]) * SCALE
+    copies[2].wait()
     for head in range(heads):
         scores[head] = head_scores(queries, k, head)
-    in_v.wait()
+    copies[3].wait()
     outs = [head_output(scores[head], v[head]) for head in range(heads)]
     attended = jnp.concatenate(outs, axis=0).T.astype(BF16)
-    in_w.wait()
+    copies[4].wait()
     projected = jnp.dot(attended, w[...], preferred_element_type=F32)
-    in_tok.wait()
+    copies[5].wait()
     part_out[...] = tok[...].astype(F32) + mods[2:3] * projected
 
 
-def piece_kernel(clip, first_hbm, second_hbm, after, out_hbm, piece, sems):
-    rows = piece.shape[0]
-    split = first_hbm.shape[0] // rows
-    index = clip[0]
-
-    @pl.when(index < split)
-    def _():
-        span = pl.ds(pl.multiple_of(index * rows, rows), rows)
-        fetch(first_hbm.at[span], piece, sems.at[0]).wait()
-
-    @pl.when(index >= split)
-    def _():
-        span = pl.ds(pl.multiple_of((index - split) * rows, rows), rows)
-        fetch(second_hbm.at[span], piece, sems.at[0]).wait()
-
+def piece_kernel(own_hbm, after, out_hbm, piece, sems):
+    fetch(own_hbm, piece, sems.at[0]).wait()
     fetch(piece, out_hbm, sems.at[1]).wait()
 
 
@@ -259,9 +265,6 @@
     copies[2].wait()
     copies[3].wait()
     k[...] = dot_nt(tokens, w[1]).astype(BF16)
-    copies[4].wait()
-    copies[5].wait()
-    values = dot_nt(w[2], tokens)
     spans = [slice(g * block, (g + 1) * block) for g in range(groups)]
     for head in range(2 * heads):
         first, last = window(head)
@@ -270,6 +273,9 @@
             scores[head * groups + g] = (
                 jnp.dot(k[span, first:last], head_q[:, span], preferred_element_type=F32) + bias
             )
+    copies[4].wait()
+    copies[5].wait()
+    values = dot_nt(w[2], tokens)
     for head in range(2 * heads):
         head_v = head_values(values, head)
         outs = [
@@ -286,18 +292,21 @@
     half = own_w.shape[0]
     copies = [
         fetch(own_w, w.at[pl.ds(0, half)], sems.at[0]),
-        fetch(other_w.at[pl.ds(3 * half, half)], w.at[pl.ds(half, half)], sems.at[1]),
+        fetch(other_w, w.at[pl.ds(half, half)], sems.at[1]),
         fetch(middle_hbm, middle, sems.at[2]),
     ]
     count, width = middle.shape
     tiles = width // LANES
     chunk = count // CHUNKS
+    split = half // LANES * LANES
     copies[0].wait()
+    early = jnp.dot(att[:, :split], w[:split, :], preferred_element_type=F32)
     copies[1].wait()
     stores = []
     for part in range(CHUNKS):
         rows = pl.ds(part * chunk, chunk)
-        projected = jnp.dot(att[rows, :], w[...], preferred_element_type=F32)
+        projected = early[part * chunk : (part + 1) * chunk]
+        projected += jnp.dot(att[rows, split:], w[split:, :], preferred_element_type=F32)
         if part == 0:
             copies[2].wait()
         result = middle[rows, :] + mods[2:3] * projected
@@ -330,10 +339,6 @@
     term = jnp.dot(mine, block_weight.astype(F32), precision=lax.Precision.HIGHEST)
     tiles = width // LANES
     return jnp.pad(term.reshape(tiles, LANES), ((0, TERM_ROWS - tiles), (0, 0)))
-
-
-def follows(index, value):
-    return index + (value.astype(F32) > 1e30).astype(jnp.int32)
 
 
 def eighth(weight):
@@ -366,34 +371,34 @@
     dma = pltpu.SemaphoreType.DMA
     group = lax.axis_size("seq") * lax.axis_size("tp")
     across = [(i, i ^ 3) for i in range(group)]
-    clip = lax.axis_index("clip")
     out_piece = lax.ppermute(eighth(spatial_out), ("seq", "tp"), across)
     term = modulation_terms(timestep, embed_weight, block_weight)
     copies = jnp.broadcast_to(term[None], (group,) + term.shape).reshape(-1, LANES)
     terms = lax.all_to_all(copies, ("seq", "tp"), 0, 0, tiled=True)
-    spatial_out_other = lax.all_gather(out_piece, "clip", axis=0, tiled=True)
-    rows = 4 * half // lax.axis_size("clip")
+    own_piece = eighth(temporal_in)
     own_piece = call(
         piece_kernel,
-        shape((rows, width), BF16),
-        [SMEM] + [HBM] * 3,
-        [pltpu.VMEM((rows, width), BF16), dma((2,))],
+        shape(own_piece.shape, BF16),
+        [HBM] * 2,
+        [pltpu.VMEM(own_piece.shape, BF16), dma((2,))],
         flops=20_000_000_000,
         nbytes=1_500_000,
         out_specs=HBM,
-    )(clip.astype(jnp.int32).reshape(1), temporal_in, temporal_out, far)
+    )(own_piece, far)
+    out_piece, _ = lax.optimization_barrier((out_piece, (own_piece, terms)))
+    spatial_out_other = lax.all_gather(out_piece, "clip", axis=0, tiled=True)
     piece = lax.ppermute(own_piece, ("seq", "tp"), across)
 
     tokens_shape = (count, width)
     k_shape = (2 * count, padded(half))
     v_shape = (heads, HEAD_DIM + 8, 2 * count)
     all_scores = pltpu.VMEM((heads, 2 * count, count), F32)
-    spatial_mods, temporal_mods, near_q, k, v, far_attended = call(
+    spatial_mods, temporal_mods, normed, k, v, far_attended = call(
         functools.partial(spatial_kernel, heads),
         (
             shape((3, width), F32),
             shape((3, width), F32),
-            shape((half, count), BF16),
+            shape(tokens_shape, BF16),
             shape(k_shape, BF16),
             shape(v_shape, BF16),
             shape((count, half), BF16),
@@ -405,7 +410,6 @@
             pltpu.VMEM(terms.shape, F32),
             pltpu.VMEM((3, half, width), BF16),
             pltpu.VMEM((half, count), F32),
-            pltpu.VMEM((half, count), BF16),
             pltpu.VMEM(k_shape, BF16),
             pltpu.VMEM(v_shape, BF16),
             all_scores,
@@ -414,27 +418,29 @@
         flops=14 * count * half * width,
         nbytes=14_000_000,
         out_specs=(VMEM, VMEM, HBM, HBM, HBM, VMEM),
+        mib=63.1,
     )(tokens, far, terms, spatial_table, temporal_table, spatial_in, own_piece)
     attended = lax.ppermute(far_attended, "tp", SWAP)
-    late = follows(0, far_attended[0, 0]) > 0
-    piece = jnp.where(late, jnp.zeros_like(piece), piece)
-    gathered = lax.all_gather(piece, "clip", axis=0, tiled=True)
     part = call(
         functools.partial(near_kernel, heads),
         shape(tokens_shape, F32),
-        [HBM] * 4 + [VMEM, HBM],
+        [HBM] * 5 + [VMEM, HBM],
         [
-            pltpu.VMEM((half, count), BF16),
+            pltpu.VMEM(tokens_shape, BF16),
+            pltpu.VMEM((half, width), BF16),
             pltpu.VMEM(k_shape, BF16),
             pltpu.VMEM(v_shape, BF16),
             pltpu.VMEM(tokens_shape, BF16),
             pltpu.VMEM((half, width), BF16),
             all_scores,
-            dma((5,)),
+            dma((6,)),
         ],
         flops=6 * count * half * width,
         nbytes=8_000_000,
-    )(near_q, k, v, tokens, spatial_mods, spatial_out)
+        mib=63.1,
+    )(normed, spatial_in, k, v, tokens, spatial_mods, spatial_out)
+    piece, _ = lax.optimization_barrier((piece, (attended, part)))
+    temporal_in_other = lax.all_gather(piece, "clip", axis=0, tiled=True)
     middle, normed = call(
         middle_kernel,
         (shape(tokens_shape, F32), shape(tokens_shape, BF16)),
@@ -448,9 +454,12 @@
         flops=2 * count * half * width,
         nbytes=6_000_000,
         out_specs=(HBM, VMEM),
-        mib=60,
+        mib=63.1,
     )(part, attended, spatial_out_other, spatial_mods, temporal_mods)
 
+    out_piece, _ = lax.optimization_barrier((eighth(temporal_out), normed))
+    out_piece = lax.ppermute(out_piece, ("seq", "tp"), across)
+    temporal_out_other = lax.all_gather(out_piece, "clip", axis=0, tiled=True)
     moved = lax.all_to_all(normed, "seq", 0, 0, tiled=True)
     positions = count // lax.axis_size("seq")
     block = 8 * lax.axis_size("seq")
@@ -467,8 +476,8 @@
         ],
         flops=12 * count * half * width,
         nbytes=10_000_000,
-        mib=60,
-    )(moved, temporal_in, gathered)
+        mib=63.1,
+    )(moved, temporal_in, temporal_in_other)
     returned = lax.all_to_all(attended, "seq", 0, 0, tiled=True)
     tiles = width // LANES
     out = call(
@@ -484,8 +493,8 @@
         flops=4 * count * half * width,
         nbytes=8_000_000,
         out_specs=HBM,
-        mib=60,
-    )(returned, temporal_out, gathered, middle, temporal_mods)
+        mib=63.1,
+    )(returned, temporal_out, temporal_out_other, middle, temporal_mods)
     return out.reshape(frames.shape)
 
 

time: 167 us -> 161 us (0.964)
  blocking collectives: 63.7 us -> 0 us
  waiting for transfers between devices: 17.8 us -> 63.5 us
  starting transfers between devices: 17.2 us -> 31.3 us
    all_to_all x2 -> x0, blocking collectives: 63.7 us -> none  [the longest x1 34.8 us: body(): moved = lax.all_to_all(normed, 'seq', 0, 0, tiled=True)]
    all_to_all x0 -> x2, waiting for transfers between devices: none -> 32.9 us  [the longest x1 17.7 us: body(): moved = lax.all_to_all(normed, 'seq', 0, 0, tiled=True)]
    all_to_all x0 -> x2, starting transfers between devices: none -> 12.1 us  [the longest x1 7.78 us: body(): moved = lax.all_to_all(normed, 'seq', 0, 0, tiled=True)]
    all_gather x1 -> x2, waiting for transfers between devices: 0.01 us -> 10.6 us  [the longest x1 10.6 us: body(): temporal_out_other = lax.all_gather(out_piece, 'clip', axis=0, tiled=True)]
    ppermute x1, waiting for transfers between devices: 12.4 us -> 2.65 us  [body(): out_piece = lax.ppermute(eighth(spatial_out), ('seq', 'tp'), across)]
    ppermute x1, waiting for transfers between devices: 0.01 us -> 7.49 us  [body(): far = lax.ppermute(tokens, 'tp', SWAP)]
    ppermute x0 -> x1, waiting for transfers between devices: none -> 4.3 us  [body(): out_piece = lax.ppermute(out_piece, ('seq', 'tp'), across)]
    dynamic_slice x1 -> x3, local copies, waits for them, and re-layouts: 0.93 us -> 4.41 us  [eighth(): lax.dynamic_slice_in_dim(weight, lax.axis_index('clip') * rows, rows, 0)]
  transfers between devices with their start and end apart: 7 -> 11, of which waited for: 4 -> 9; matrix products, arithmetic and copies ran while one was open for 3% -> 4% of each run, Pallas kernels for 17% -> 24%
where the time goes in v3:
time: 161 us
  waiting for transfers between devices  63.5 us (39%)
  Pallas kernels  43.9 us (27%)
  starting transfers between devices  31.3 us (19%)
  between operations  13.9 us (9%)
  local copies, waits for them, and re-layouts  7.2 us (4%)
    all_to_all x1, waiting for transfers between devices, body(): moved = lax.all_to_all(normed, 'seq', 0, 0, tiled=True)  17.7 us
    all_to_all x1, waiting for transfers between devices, body(): returned = lax.all_to_all(attended, 'seq', 0, 0, tiled=True)  15.2 us
    pallas_call x1, Pallas kernels, body(): call(functools.partial(spatial_kernel, heads), (shape((3, width), F32), s...  11.6 us
    all_gather x1, waiting for transfers between devices, body(): temporal_out_other = lax.all_gather(out_piece, 'clip', axis=0, tiled=True)  10.6 us
    all_to_all x1, starting transfers between devices, body(): terms = lax.all_to_all(copies, ('seq', 'tp'), 0, 0, tiled=True)  10.5 us
    pallas_call x1, Pallas kernels, body(): call(functools.partial(temporal_kernel, heads, positions), shape((count,...  10.1 us
    pallas_call x1, Pallas kernels, body(): call(functools.partial(near_kernel, heads), shape(tokens_shape, F32), [HB...  9.2 us
    all_to_all x1, starting transfers between devices, body(): moved = lax.all_to_all(normed, 'seq', 0, 0, tiled=True)  7.78 us
  transfers between devices with their start and end apart: 11, of which 9 were waited for; matrix products, arithmetic and copies ran while one was open for 4% of the time, Pallas kernels for 24%

profile of v3, /device:TPU:4, one launch (start us, length us, event | category | flops | bytes accessed | tf_op | source)
XLA Modules:
  0.0 160.6 jit_solution(13158353241091364263)
XLA Ops:
  6.5 2.2 %collective-permute-start = (bf16[384,1152]{1,0:T(8,128)(2,1)}, bf16[384,1152]{1,0:T(8,128)(2,1)}, u32[]{:S(2)}, u32[]{:S(2)}) collective-permute-start(bf16[384,1152]{1,0:T(8,128)(2,1)} %bitcast.30), channel_id=1, source_target_pairs={{0,1},{1,0},{2,3},{3,2},{4,5},{5,4},{6,7},{7,6},{8,9},{9,8},{10,11... | collective-permute-start | bytes 2654216 | tf_op jit(solution)/shard_map/ppermute | solution.py:366
  9.5 1.1 dot_general.12
  10.6 0.4 convolution_reduce_fusion
  11.0 0.3 fusion
  11.3 0.9 broadcast_in_dim.2
  12.2 10.5 %all-to-all-start = ((f32[32,32,128]{2,1,0:T(8,128)}), f32[32,32,128]{2,1,0:T(8,128)}, u32[]{:S(2)}, u32[]{:S(2)}) async-start(f32[32,32,128]{2,1,0:T(8,128)} %broadcast_in_dim.2), calls=%async_computation | async-start | bytes 1048576 | tf_op jit(solution)/shard_map/all_to_all | solution.py:377
  22.8 1.6 constant_dynamic-slice_fusion.1
  24.4 0.6 collective-permute-start.2
  25.0 1.8 %constant_dynamic-slice_fusion.2.own_hbm = bf16[216,1152]{1,0:T(8,128)(2,1)} fusion(bf16[1728,1152]{1,0:T(8,128)(2,1)} %bitcast.37, s32[]{:T(128)S(6)} %select_n.11), kind=kLoop, calls=%fused_computation.9 | loop fusion | bytes 995332 | tf_op jit(solution)/shard_map/dynamic_slice | solution.py:346
  26.8 7.5 %collective-permute-done.after.far_hbm = bf16[384,1152]{1,0:T(8,128)(2,1)} collective-permute-done((bf16[384,1152]{1,0:T(8,128)(2,1)}, bf16[384,1152]{1,0:T(8,128)(2,1)}, u32[]{:S(2)}, u32[]{:S(2)}) %collective-permute-start) | collective-permute-done | bytes 884768 | tf_op jit(solution)/shard_map/ppermute | solution.py:366
  34.3 1.8 %shard_map.100.after = bf16[216,1152]{1,0:T(8,128)(2,1)} custom-call(bf16[216,1152]{1,0:T(8,128)(2,1)} %constant_dynamic-slice_fusion.2.own_hbm, bf16[384,1152]{1,0:T(8,128)(2,1)} %collective-permute-done.after.far_hbm), custom_call_target="tpu_custom_call" | custom-call | flops 20000000000 | bytes 1500000 | tf_op jit(solution)/shard_map/pallas_call | solution.py:379
  36.2 2.6 %collective-permute-done.2 = bf16[72,1152]{1,0:T(8,128)(2,1)S(1)} collective-permute-done((bf16[72,1152]{1,0:T(8,128)(2,1)}, bf16[72,1152]{1,0:T(8,128)(2,1)S(1)}, u32[]{:S(2)}, u32[]{:S(2)}) %collective-permute-start.2) | collective-permute-done | bytes 165920 | tf_op jit(solution)/shard_map/ppermute | solution.py:374
  38.8 0.5 all-to-all-done
  39.4 0.1 copy-done.1
  39.6 0.6 collective-permute-start.3
  40.2 11.6 %shard_map.101 = (f32[3,1152]{1,0:T(4,128)}, f32[3,1152]{1,0:T(4,128)}, bf16[384,1152]{1,0:T(8,128)(2,1)}, bf16[768,640]{1,0:T(8,128)(2,1)}, bf16[8,80,768]{2,1,0:T(8,128)(2,1)}, /*index=5*/bf16[384,576]{1,0:T(8,128)(2,1)}) custom-call(bf16[384,1152]{1,0:T(8,128)(2,1)} %bitcast.31, bf16[384,1152]{1,0:T(8,128)(2,1)} %collective-permute-done.after.far_hbm, ...), custom_call_target="tpu_custom_call" | custom-call | flops 3567255552 | bytes 14000000 | tf_op jit(solution)/shard_map/pallas_call | solution.py:396
  51.8 3.0 %collective-permute-start.1 = (bf16[384,576]{1,0:T(8,128)(2,1)}, bf16[384,576]{1,0:T(8,128)(2,1)}, u32[]{:S(2)}, u32[]{:S(2)}) collective-permute-start(bf16[384,576]{1,0:T(8,128)(2,1)} %get-tuple-element.20), channel_id=1, source_target_pairs={{0,1},{1,0},{2,3},{3,2},{4,5},{5,4},{6,7},{7,6},{8,9},{9,8},{10,11... | collective-permute-start | bytes 1327112 | tf_op jit(solution)/shard_map/ppermute | solution.py:423
  54.8 9.2 %shard_map.102.part_hbm = f32[384,1152]{1,0:T(8,128)} custom-call(bf16[384,1152]{1,0:T(8,128)(2,1)} %get-tuple-element.16.normed_hbm, bf16[1728,1152]{1,0:T(8,128)(2,1)} %bitcast.29, bf16[768,640]{1,0:T(8,128)(2,1)} %get-tuple-element.17.k_hbm, bf16[8,80,768]{2,1,0:T(8,128)(2,1)} %get-tuple-element.18.v_hbm, bf16[384,1152]{1,0:T(8,128)(2,1)} %bitcast.32, ...), custom_call_target="tpu_custom_call" | custom-call | flops 1528823808 | bytes 8000000 | tf_op jit(solution)/shard_map/pallas_call | solution.py:424
  64.0 2.8 %collective-permute-done.1.att = bf16[384,576]{1,0:T(8,128)(2,1)} collective-permute-done((bf16[384,576]{1,0:T(8,128)(2,1)}, bf16[384,576]{1,0:T(8,128)(2,1)}, u32[]{:S(2)}, u32[]{:S(2)}) %collective-permute-start.1) | collective-permute-done | bytes 442400 | tf_op jit(solution)/shard_map/ppermute | solution.py:423
  66.9 2.1 %all-gather.4.cloned.1.call-done.w_hbm = bf16[576,1152]{1,0:T(8,128)(2,1)} async-done(((bf16[72,1152]{1,0:T(8,128)(2,1)}), bf16[576,1152]{1,0:T(8,128)(2,1)}) %all-gather.4.cloned.1.call-update) | async-done | bytes 1327120 | tf_op jit(solution)/shard_map/all_gather | solution.py:389
  69.0 5.7 %shard_map.103 = (f32[384,1152]{1,0:T(8,128)}, bf16[384,1152]{1,0:T(8,128)(2,1)}) custom-call(f32[384,1152]{1,0:T(8,128)} %shard_map.102.part_hbm, bf16[384,576]{1,0:T(8,128)(2,1)} %collective-permute-done.1.att, bf16[576,1152]{1,0:T(8,128)(2,1)} %all-gather.4.cloned.1.call-done.w_hbm, f32[3,1152]{1,0:T(4,128)} %get-tuple-element.19.mods, ...), custom_call_target="tpu_custom_call" | custom-call | flops 509607936 | bytes 6000000 | tf_op jit(solution)/shard_map/pallas_call | solution.py:444
  74.7 7.8 %all-to-all-start.1 = ((bf16[16,24,1152]{2,1,0:T(8,128)(2,1)}), bf16[16,24,1152]{2,1,0:T(8,128)(2,1)}, u32[]{:S(2)}, u32[]{:S(2)}) async-start(bf16[16,24,1152]{2,1,0:T(8,128)(2,1)} %bitcast.33), calls=%async_computation.1 | async-start | bytes 1769472 | tf_op jit(solution)/shard_map/all_to_all | solution.py:463
  82.5 1.0 constant_dynamic-slice_fusion
  83.5 2.1 %collective-permute-start.4 = (bf16[72,1152]{1,0:T(8,128)(2,1)S(1)}, bf16[72,1152]{1,0:T(8,128)(2,1)S(1)}, u32[]{:S(2)}, u32[]{:S(2)}) collective-permute-start(bf16[72,1152]{1,0:T(8,128)(2,1)S(1)} %constant_dynamic-slice_fusion), channel_id=1, source_target_pairs={{0,3},{1,2},{2,1},{3,0},{4,7},{5,6},{6,5},{7,4},{8,11},{9,10},{10,... | collective-permute-start | bytes 497672 | tf_op jit(solution)/shard_map/ppermute | solution.py:461
  85.6 4.3 %collective-permute-done.4 = bf16[72,1152]{1,0:T(8,128)(2,1)S(1)} collective-permute-done((bf16[72,1152]{1,0:T(8,128)(2,1)S(1)}, bf16[72,1152]{1,0:T(8,128)(2,1)S(1)}, u32[]{:S(2)}, u32[]{:S(2)}) %collective-permute-start.4) | collective-permute-done | bytes 165920 | tf_op jit(solution)/shard_map/ppermute | solution.py:461
  89.9 0.7 copy-done.2
  90.6 17.7 %all-to-all-done.1 = bf16[16,24,1152]{2,1,0:T(8,128)(2,1)} async-done(((bf16[16,24,1152]{2,1,0:T(8,128)(2,1)}), bf16[16,24,1152]{2,1,0:T(8,128)(2,1)}, u32[]{:S(2)}, u32[]{:S(2)}) %all-to-all-start.1) | async-done | bytes 884768 | tf_op jit(solution)/shard_map/all_to_all | solution.py:463
  108.3 10.1 %shard_map.104 = bf16[384,1152]{1,0:T(8,128)(2,1)} custom-call(bf16[384,1152]{1,0:T(8,128)(2,1)} %bitcast.13.moved, bf16[1728,1152]{1,0:T(8,128)(2,1)} %bitcast.38, bf16[1728,1152]{1,0:T(8,128)(2,1)} %all-gather.6.cloned.1.call-done.other_hbm), custom_call_target="tpu_custom_call" | custom-call | flops 3057647616 | bytes 10000000 | tf_op jit(solution)/shard_map/pallas_call | solution.py:466
  118.4 4.3 %all-to-all-start.2 = ((bf16[16,24,1152]{2,1,0:T(8,128)(2,1)}), bf16[16,24,1152]{2,1,0:T(8,128)(2,1)}, u32[]{:S(2)}, u32[]{:S(2)}) async-start(bf16[16,24,1152]{2,1,0:T(8,128)(2,1)} %bitcast.34), calls=%async_computation.2 | async-start | bytes 1769472 | tf_op jit(solution)/shard_map/all_to_all | solution.py:481
  122.8 10.6 %all-gather.8.cloned.1.call-done.other_w = bf16[576,1152]{1,0:T(8,128)(2,1)} async-done(((bf16[72,1152]{1,0:T(8,128)(2,1)}), bf16[576,1152]{1,0:T(8,128)(2,1)}) %all-gather.8.cloned.1.call-update) | async-done | bytes 1327120 | tf_op jit(solution)/shard_map/all_gather | solution.py:462
  133.4 15.2 %all-to-all-done.2 = bf16[16,24,1152]{2,1,0:T(8,128)(2,1)} async-done(((bf16[16,24,1152]{2,1,0:T(8,128)(2,1)}), bf16[16,24,1152]{2,1,0:T(8,128)(2,1)}, u32[]{:S(2)}, u32[]{:S(2)}) %all-to-all-start.2) | async-done | bytes 884768 | tf_op jit(solution)/shard_map/all_to_all | solution.py:481
  148.6 5.5 %shard_map.105 = f32[3456,128]{1,0:T(8,128)} custom-call(bf16[384,1152]{1,0:T(8,128)(2,1)} %bitcast.15.att, bf16[576,1152]{1,0:T(8,128)(2,1)} %own_w.1, bf16[576,1152]{1,0:T(8,128)(2,1)} %all-gather.8.cloned.1.call-done.other_w, f32[384,1152]{1,0:T(8,128)} %get-tuple-element.26.middle_hbm, f32[3,1152]{1,0:T(4,128)} %get-tuple-element.22.next_mods.mods), custom_call_target="tpu_custom_call" | custom-call | flops 1019215872 | bytes 8000000 | tf_op jit(solution)/shard_map/pallas_call | solution.py:483
  (15 shorter events, 0.2 us)
Async XLA Ops:
  6.5 4.1 %copy-start = (bf16[256,1152]{1,0:T(8,128)(2,1)S(1)}, bf16[256,1152]{1,0:T(8,128)(2,1)}, u32[]{:S(2)}) copy-start(bf16[256,1152]{1,0:T(8,128)(2,1)} %param.12) | copy-start | bytes 1769476
  6.5 27.8 %collective-permute-start = (bf16[384,1152]{1,0:T(8,128)(2,1)}, bf16[384,1152]{1,0:T(8,128)(2,1)}, u32[]{:S(2)}, u32[]{:S(2)}) collective-permute-start(bf16[384,1152]{1,0:T(8,128)(2,1)} %bitcast.30), channel_id=1, source_target_pairs={{0,1},{1,0},{2,3},{3,2},{4,5},{5,4},{6,7},{7,6},{8,9},{9,8},{10,11... | collective-permute-start | bytes 2654216 | tf_op jit(solution)/shard_map/ppermute | solution.py:366
  12.2 27.1 %all-to-all-start = ((f32[32,32,128]{2,1,0:T(8,128)}), f32[32,32,128]{2,1,0:T(8,128)}, u32[]{:S(2)}, u32[]{:S(2)}) async-start(f32[32,32,128]{2,1,0:T(8,128)} %broadcast_in_dim.2), calls=%async_computation | async-start | bytes 1048576 | tf_op jit(solution)/shard_map/all_to_all | solution.py:377
  22.8 46.3 %all-gather.4.cloned.1.call-start = ((), (), s32[]{:S(2)}) async-start(), calls=%async_computation.3 | async-start | bytes 1492992 | tf_op jit(solution)/shard_map/all_gather | solution.py:389
  24.4 14.4 %collective-permute-start.2 = (bf16[72,1152]{1,0:T(8,128)(2,1)}, bf16[72,1152]{1,0:T(8,128)(2,1)S(1)}, u32[]{:S(2)}, u32[]{:S(2)}) collective-permute-start(bf16[72,1152]{1,0:T(8,128)(2,1)} %constant_dynamic-slice_fusion.1), channel_id=1, source_target_pairs={{0,3},{1,2},{2,1},{3,0},{4,7},{5,6},{6,5},{7,4},{8,11},{9,10},{10,... | collective-permute-start | bytes 497672 | tf_op jit(solution)/shard_map/ppermute | solution.py:374
  38.8 0.7 copy-start.1
  39.5 68.8 %all-gather.6.cloned.1.call-start = ((), (), s32[]{:S(2)}) async-start(), calls=%async_computation.4 | async-start | bytes 4478976 | tf_op jit(solution)/shard_map/all_gather | solution.py:443
  39.6 24.5 %collective-permute-start.3 = (bf16[216,1152]{1,0:T(8,128)(2,1)}, bf16[216,1152]{1,0:T(8,128)(2,1)}, u32[]{:S(2)}, u32[]{:S(2)}) collective-permute-start(bf16[216,1152]{1,0:T(8,128)(2,1)} %shard_map.100.after), channel_id=1, source_target_pairs={{0,3},{1,2},{2,1},{3,0},{4,7},{5,6},{6,5},{7,4},{8,11},{9,10},{10,... | collective-permute-start | bytes 1493000 | tf_op jit(solution)/shard_map/ppermute | solution.py:390
  51.8 15.1 %collective-permute-start.1 = (bf16[384,576]{1,0:T(8,128)(2,1)}, bf16[384,576]{1,0:T(8,128)(2,1)}, u32[]{:S(2)}, u32[]{:S(2)}) collective-permute-start(bf16[384,576]{1,0:T(8,128)(2,1)} %get-tuple-element.20), channel_id=1, source_target_pairs={{0,1},{1,0},{2,3},{3,2},{4,5},{5,4},{6,7},{7,6},{8,9},{9,8},{10,11... | collective-permute-start | bytes 1327112 | tf_op jit(solution)/shard_map/ppermute | solution.py:423
  74.7 33.6 %all-to-all-start.1 = ((bf16[16,24,1152]{2,1,0:T(8,128)(2,1)}), bf16[16,24,1152]{2,1,0:T(8,128)(2,1)}, u32[]{:S(2)}, u32[]{:S(2)}) async-start(bf16[16,24,1152]{2,1,0:T(8,128)(2,1)} %bitcast.33), calls=%async_computation.1 | async-start | bytes 1769472 | tf_op jit(solution)/shard_map/all_to_all | solution.py:463
  82.5 50.9 %all-gather.8.cloned.1.call-start = ((), (), s32[]{:S(2)}) async-start(), calls=%async_computation.5 | async-start | bytes 1492992 | tf_op jit(solution)/shard_map/all_gather | solution.py:462
  83.5 6.4 %collective-permute-start.4 = (bf16[72,1152]{1,0:T(8,128)(2,1)S(1)}, bf16[72,1152]{1,0:T(8,128)(2,1)S(1)}, u32[]{:S(2)}, u32[]{:S(2)}) collective-permute-start(bf16[72,1152]{1,0:T(8,128)(2,1)S(1)} %constant_dynamic-slice_fusion), channel_id=1, source_target_pairs={{0,3},{1,2},{2,1},{3,0},{4,7},{5,6},{6,5},{7,4},{8,11},{9,10},{10,... | collective-permute-start | bytes 497672 | tf_op jit(solution)/shard_map/ppermute | solution.py:461
  89.9 0.7 copy-start.2
  118.4 30.1 %all-to-all-start.2 = ((bf16[16,24,1152]{2,1,0:T(8,128)(2,1)}), bf16[16,24,1152]{2,1,0:T(8,128)(2,1)}, u32[]{:S(2)}, u32[]{:S(2)}) async-start(bf16[16,24,1152]{2,1,0:T(8,128)(2,1)} %bitcast.34), calls=%async_computation.2 | async-start | bytes 1769472 | tf_op jit(solution)/shard_map/all_to_all | solution.py:481
Sparse Core Ops, SparseCore 0:
  39.6 29.3 all-gather.3
  70.9 33.9 all-gather.5
  106.7 26.5 all-gather.7

commit v4 on v3

--- a/solution.py
+++ b/solution.py
@@ -15,7 +15,7 @@
 VMEM = pl.BlockSpec(memory_space=pltpu.VMEM)
 HBM = pl.BlockSpec(memory_space=pl.ANY)
 TERM_ROWS = 32
-CHUNKS = 2
+CHUNKS = 4
 SCALE = math.log2(math.e) / math.sqrt(HEAD_DIM)
 BF16 = jnp.bfloat16
 F32 = jnp.float32
@@ -90,9 +90,7 @@
     return out[:HEAD_DIM] / out[HEAD_DIM : HEAD_DIM + 1]
 
 
-def modulation_table(terms, table):
-    group = terms.shape[0] // TERM_ROWS
-    total = jnp.sum(terms[...].reshape(group, TERM_ROWS, LANES), axis=0)
+def modulation_table(total, table):
     tiles = table.shape[1] // LANES
     rows = []
     for row in range(3):
@@ -110,7 +108,8 @@
     heads,
     tok_hbm,
     far_hbm,
-    terms_hbm,
+    own_total,
+    other_total,
     table,
     next_table,
     w_hbm,
@@ -123,7 +122,6 @@
     att_out,
     tok,
     far,
-    terms,
     w,
     q,
     k,
@@ -132,14 +130,12 @@
     sems,
 ):
     count, half = far.shape[0], heads * HEAD_DIM
-    in_terms = fetch(terms_hbm, terms, sems.at[3])
     in_far = fetch(far_hbm, far, sems.at[4])
     in_w = fetch_parts(w_hbm, w, sems)
     in_tok = fetch(tok_hbm, tok, sems.at[5])
     near, beyond = pl.ds(0, count), pl.ds(count, count)
     k[:, k.shape[1] - LANES :] = jnp.zeros((2 * count, LANES), BF16)
-    in_terms.wait()
-    modulation = modulation_table(terms, table)
+    modulation = modulation_table(own_total[...] + other_total[...], table)
     mods = table[...] + modulation
     mods_out[...] = mods
     next_out[...] = next_table[...] + modulation
@@ -220,11 +216,13 @@
 
 
 def middle_kernel(
-    part_hbm, att, w_hbm, mods, next_mods, middle_hbm, normed_out, part, w, middle, sems
+    part_hbm, att_hbm, w_hbm, mods, next_mods, middle_hbm, normed_out, part, att, w, middle, sems
 ):
     in_w = fetch(w_hbm, w, sems.at[0])
+    in_att = fetch(att_hbm, att, sems.at[3])
     in_part = fetch(part_hbm, part, sems.at[1])
     in_w.wait()
+    in_att.wait()
     projected = jnp.dot(att[...], w[...], preferred_element_type=F32)
     in_part.wait()
     middle[...] = part[...] + mods[2:3] * projected
@@ -234,9 +232,10 @@
 
 
 def temporal_kernel(
-    heads, positions, moved, own_hbm, other_hbm, att_out, w, k, scores, out, sems
+    heads, positions, moved_hbm, own_hbm, other_hbm, att_out, moved, w, k, scores, out, sems
 ):
     half = heads * HEAD_DIM
+    in_moved = fetch(moved_hbm, moved, sems.at[6])
     count, width = moved.shape
     depth = count // positions
     groups = positions // 8
@@ -255,6 +254,7 @@
     here = lax.rem(lax.broadcasted_iota(jnp.int32, (block, block), 0), 8)
     there = lax.rem(lax.broadcasted_iota(jnp.int32, (block, block), 1), 8)
     bias = jnp.where(here == there, 0.0, -1e30)
+    in_moved.wait()
     grid = moved[...].astype(F32).reshape(depth, positions, width)
     tokens = jnp.concatenate(
         [grid[:, g * 8 : g * 8 + 8].reshape(block, width) for g in range(groups)], axis=0
@@ -288,8 +288,11 @@
     att_out[...] = jnp.concatenate(by_group, axis=1).reshape(count, 2 * half).astype(BF16)
 
 
-def final_kernel(att, own_w, other_w, middle_hbm, mods, out_hbm, w, middle, out, sems):
+def final_kernel(
+    att_hbm, own_w, other_w, middle_hbm, mods, out_hbm, att, w, middle, out, sems
+):
     half = own_w.shape[0]
+    in_att = fetch(att_hbm, att, sems.at[3 + CHUNKS])
     copies = [
         fetch(own_w, w.at[pl.ds(0, half)], sems.at[0]),
         fetch(other_w, w.at[pl.ds(half, half)], sems.at[1]),
@@ -299,6 +302,7 @@
     tiles = width // LANES
     chunk = count // CHUNKS
     split = half // LANES * LANES
+    in_att.wait()
     copies[0].wait()
     early = jnp.dot(att[:, :split], w[:split, :], preferred_element_type=F32)
     copies[1].wait()
@@ -373,8 +377,10 @@
     across = [(i, i ^ 3) for i in range(group)]
     out_piece = lax.ppermute(eighth(spatial_out), ("seq", "tp"), across)
     term = modulation_terms(timestep, embed_weight, block_weight)
-    copies = jnp.broadcast_to(term[None], (group,) + term.shape).reshape(-1, LANES)
-    terms = lax.all_to_all(copies, ("seq", "tp"), 0, 0, tiled=True)
+    copies = jnp.broadcast_to(term[None], (lax.axis_size("seq"),) + term.shape)
+    terms = lax.all_to_all(copies.reshape(-1, LANES), "seq", 0, 0, tiled=True)
+    own_total = jnp.sum(terms.reshape(copies.shape), axis=0)
+    other_total = lax.ppermute(own_total, "tp", SWAP)
     own_piece = eighth(temporal_in)
     own_piece = call(
         piece_kernel,
@@ -385,7 +391,7 @@
         nbytes=1_500_000,
         out_specs=HBM,
     )(own_piece, far)
-    out_piece, _ = lax.optimization_barrier((out_piece, (own_piece, terms)))
+    out_piece, _ = lax.optimization_barrier((out_piece, (own_total, far)))
     spatial_out_other = lax.all_gather(out_piece, "clip", axis=0, tiled=True)
     piece = lax.ppermute(own_piece, ("seq", "tp"), across)
 
@@ -403,11 +409,10 @@
             shape(v_shape, BF16),
             shape((count, half), BF16),
         ),
-        [HBM] * 3 + [VMEM] * 2 + [HBM] * 2,
+        [HBM] * 2 + [VMEM] * 4 + [HBM] * 2,
         [
             pltpu.VMEM(tokens_shape, BF16),
             pltpu.VMEM(tokens_shape, BF16),
-            pltpu.VMEM(terms.shape, F32),
             pltpu.VMEM((3, half, width), BF16),
             pltpu.VMEM((half, count), F32),
             pltpu.VMEM(k_shape, BF16),
@@ -419,7 +424,7 @@
         nbytes=14_000_000,
         out_specs=(VMEM, VMEM, HBM, HBM, HBM, VMEM),
         mib=63.1,
-    )(tokens, far, terms, spatial_table, temporal_table, spatial_in, own_piece)
+    )(tokens, far, own_total, other_total, spatial_table, temporal_table, spatial_in, own_piece)
     attended = lax.ppermute(far_attended, "tp", SWAP)
     part = call(
         functools.partial(near_kernel, heads),
@@ -444,12 +449,13 @@
     middle, normed = call(
         middle_kernel,
         (shape(tokens_shape, F32), shape(tokens_shape, BF16)),
-        [HBM, VMEM, HBM, VMEM, VMEM],
+        [HBM] * 3 + [VMEM] * 2,
         [
             pltpu.VMEM(tokens_shape, F32),
+            pltpu.VMEM((count, half), BF16),
             pltpu.VMEM((half, width), BF16),
             pltpu.VMEM(tokens_shape, F32),
-            dma((3,)),
+            dma((4,)),
         ],
         flops=2 * count * half * width,
         nbytes=6_000_000,
@@ -466,13 +472,14 @@
     attended = call(
         functools.partial(temporal_kernel, heads, positions),
         shape((count, 2 * half), BF16),
-        [VMEM, HBM, HBM],
+        [HBM] * 3,
         [
+            pltpu.VMEM(tokens_shape, BF16),
             pltpu.VMEM((3, 2 * half, width), BF16),
             pltpu.VMEM((count, 2 * half), BF16),
             pltpu.VMEM((2 * heads * (positions // 8), block, block), F32),
             pltpu.VMEM((2 * half, count), F32),
-            dma((6,)),
+            dma((7,)),
         ],
         flops=12 * count * half * width,
         nbytes=10_000_000,
@@ -483,12 +490,13 @@
     out = call(
         final_kernel,
         shape((count * tiles, LANES), F32),
-        [VMEM, HBM, HBM, HBM, VMEM],
+        [HBM] * 4 + [VMEM],
         [
+            pltpu.VMEM(tokens_shape, BF16),
             pltpu.VMEM((2 * half, width), BF16),
             pltpu.VMEM((count, width), F32),
             pltpu.VMEM((count * tiles, LANES), F32),
-            dma((3 + CHUNKS,)),
+            dma((4 + CHUNKS,)),
         ],
         flops=4 * count * half * width,
         nbytes=8_000_000,

time: 161 us -> 156 us (0.969)
  waiting for transfers between devices: 63.5 us -> 55.5 us
  starting transfers between devices: 31.3 us -> 34.6 us
    ppermute x1, waiting for transfers between devices: 7.49 us -> 0.01 us  [body(): far = lax.ppermute(tokens, 'tp', SWAP)]
    all_to_all x1, waiting for transfers between devices: 0.54 us -> 6.95 us  [body(): terms = lax.all_to_all(copies.reshape(-1, LANES), 'seq', 0, 0, tiled=True)]
    ppermute x1, waiting for transfers between devices: 2.65 us -> 0.01 us  [body(): out_piece = lax.ppermute(eighth(spatial_out), ('seq', 'tp'), across)]
    all_to_all x1, starting transfers between devices: 10.5 us -> 8.37 us  [body(): terms = lax.all_to_all(copies.reshape(-1, LANES), 'seq', 0, 0, tiled=True)]
    all_gather x1, waiting for transfers between devices: 2.14 us -> 0.48 us  [body(): spatial_out_other = lax.all_gather(out_piece, 'clip', axis=0, tiled=True)]
  transfers between devices with their start and end apart: 11 -> 12, of which waited for: 9 -> 8; matrix products, arithmetic and copies ran while one was open for 4% -> 4% of each run, Pallas kernels for 24% -> 24%
where the time goes in v4:
time: 156 us; the launch traced here: 155 us
  waiting for transfers between devices  55.5 us (36%)
  Pallas kernels  42.4 us (27%)
  starting transfers between devices  34.6 us (22%)
  between operations  13.9 us (9%)
  local copies, waits for them, and re-layouts  7.82 us (5%)
    all_to_all x1, waiting for transfers between devices, body(): moved = lax.all_to_all(normed, 'seq', 0, 0, tiled=True)  16.6 us
    all_to_all x1, waiting for transfers between devices, body(): returned = lax.all_to_all(attended, 'seq', 0, 0, tiled=True)  14.3 us
    pallas_call x1, Pallas kernels, body(): call(functools.partial(spatial_kernel, heads), (shape((3, width), F32), s...  11.5 us
    all_gather x1, waiting for transfers between devices, body(): temporal_out_other = lax.all_gather(out_piece, 'clip', axis=0, tiled=True)  11.5 us
    pallas_call x1, Pallas kernels, body(): call(functools.partial(temporal_kernel, heads, positions), shape((count,...  9.21 us
    pallas_call x1, Pallas kernels, body(): call(functools.partial(near_kernel, heads), shape(tokens_shape, F32), [HB...  9.18 us
    all_to_all x1, starting transfers between devices, body(): moved = lax.all_to_all(normed, 'seq', 0, 0, tiled=True)  9.14 us
    all_to_all x1, starting transfers between devices, body(): terms = lax.all_to_all(copies.reshape(-1, LANES), 'seq', 0, 0, tiled=True)  8.37 us
  transfers between devices with their start and end apart: 12, of which 8 were waited for; matrix products, arithmetic and copies ran while one was open for 4% of the time, Pallas kernels for 24%

profile of v4, /device:TPU:4, one launch (start us, length us, event | category | flops | bytes accessed | tf_op | source)
XLA Modules:
  0.0 155.1 jit_solution(48948963613320037)
XLA Ops:
  6.5 2.2 %collective-permute-start = (bf16[384,1152]{1,0:T(8,128)(2,1)}, bf16[384,1152]{1,0:T(8,128)(2,1)S(1)}, u32[]{:S(2)}, u32[]{:S(2)}) collective-permute-start(bf16[384,1152]{1,0:T(8,128)(2,1)} %bitcast.29), channel_id=1, source_target_pairs={{0,1},{1,0},{2,3},{3,2},{4,5},{5,4},{6,7},{7,6},{8,9},{9,8},{10,11... | collective-permute-start | bytes 2654216 | tf_op jit(solution)/shard_map/ppermute | solution.py:370
  9.5 1.1 dot_general.12
  10.6 0.4 convolution_reduce_fusion
  11.3 0.7 broadcast_in_dim.2
  12.1 8.4 %all-to-all-start = ((f32[16,32,128]{2,1,0:T(8,128)}), f32[16,32,128]{2,1,0:T(8,128)S(1)}, u32[]{:S(2)}, u32[]{:S(2)}) async-start(f32[16,32,128]{2,1,0:T(8,128)} %broadcast_in_dim.2), calls=%async_computation | async-start | bytes 524288 | tf_op jit(solution)/shard_map/all_to_all | solution.py:381
  20.5 0.9 constant_dynamic-slice_fusion.1
  21.4 2.1 %collective-permute-start.3 = (bf16[72,1152]{1,0:T(8,128)(2,1)S(1)}, bf16[72,1152]{1,0:T(8,128)(2,1)S(1)}, u32[]{:S(2)}, u32[]{:S(2)}) collective-permute-start(bf16[72,1152]{1,0:T(8,128)(2,1)S(1)} %constant_dynamic-slice_fusion.1), channel_id=1, source_target_pairs={{0,3},{1,2},{2,1},{3,0},{4,7},{5,6},{6,5},{7,4},{8,11},{9,10},{10,... | collective-permute-start | bytes 497672 | tf_op jit(solution)/shard_map/ppermute | solution.py:378
  23.5 1.9 %constant_dynamic-slice_fusion.2.own_hbm = bf16[216,1152]{1,0:T(8,128)(2,1)} fusion(bf16[1728,1152]{1,0:T(8,128)(2,1)} %bitcast.36, s32[]{:T(128)S(6)} %select_n.11), kind=kLoop, calls=%fused_computation.9 | loop fusion | bytes 995332 | tf_op jit(solution)/shard_map/dynamic_slice | solution.py:350
  25.4 6.9 %all-to-all-done = f32[16,32,128]{2,1,0:T(8,128)S(1)} async-done(((f32[16,32,128]{2,1,0:T(8,128)}), f32[16,32,128]{2,1,0:T(8,128)S(1)}, u32[]{:S(2)}, u32[]{:S(2)}) %all-to-all-start) | async-done | bytes 262176 | tf_op jit(solution)/shard_map/all_to_all | solution.py:381
  32.4 1.6 %collective-permute-start.1 = (f32[32,128]{1,0:T(8,128)S(1)}, f32[32,128]{1,0:T(8,128)S(1)}, u32[]{:S(2)}, u32[]{:S(2)}) collective-permute-start(f32[32,128]{1,0:T(8,128)S(1)} %reduce_sum.9.own_total), channel_id=1, source_target_pairs={{0,1},{1,0},{2,3},{3,2},{4,5},{5,4},{6,7},{7,6},{8,9},{9,8},{10,11... | collective-permute-start | bytes 49160 | tf_op jit(solution)/shard_map/ppermute | solution.py:383
  34.0 0.6 copy-done.1
  34.9 1.8 %shard_map.100.after = bf16[216,1152]{1,0:T(8,128)(2,1)} custom-call(bf16[216,1152]{1,0:T(8,128)(2,1)} %constant_dynamic-slice_fusion.2.own_hbm, bf16[384,1152]{1,0:T(8,128)(2,1)} %copy-done.4), custom_call_target="tpu_custom_call" | custom-call | flops 20000000000 | bytes 1500000 | tf_op jit(solution)/shard_map/pallas_call | solution.py:385
  36.8 0.4 collective-permute-start.4
  37.2 0.5 collective-permute-done.1.other_total
  37.7 0.6 copy-done.5
  38.3 11.5 %shard_map.101 = (f32[3,1152]{1,0:T(4,128)}, f32[3,1152]{1,0:T(4,128)}, bf16[384,1152]{1,0:T(8,128)(2,1)}, bf16[768,640]{1,0:T(8,128)(2,1)}, bf16[8,80,768]{2,1,0:T(8,128)(2,1)}, /*index=5*/bf16[384,576]{1,0:T(8,128)(2,1)}) custom-call(bf16[384,1152]{1,0:T(8,128)(2,1)} %bitcast.30, bf16[384,1152]{1,0:T(8,128)(2,1)} %copy-done.4, f32[32,128]{1,0:T(8,128)} %copy-done.3, ...), custom_call_target="tpu_custom_call" | custom-call | flops 3567255552 | bytes 14000000 | tf_op jit(solution)/shard_map/pallas_call | solution.py:402
  49.8 2.8 %collective-permute-start.2 = (bf16[384,576]{1,0:T(8,128)(2,1)}, bf16[384,576]{1,0:T(8,128)(2,1)}, u32[]{:S(2)}, u32[]{:S(2)}) collective-permute-start(bf16[384,576]{1,0:T(8,128)(2,1)} %get-tuple-element.20), channel_id=1, source_target_pairs={{0,1},{1,0},{2,3},{3,2},{4,5},{5,4},{6,7},{7,6},{8,9},{9,8},{10,11... | collective-permute-start | bytes 1327112 | tf_op jit(solution)/shard_map/ppermute | solution.py:428
  52.5 9.2 %shard_map.102.part_hbm = f32[384,1152]{1,0:T(8,128)} custom-call(bf16[384,1152]{1,0:T(8,128)(2,1)} %get-tuple-element.16.normed_hbm, bf16[1728,1152]{1,0:T(8,128)(2,1)} %bitcast.28, bf16[768,640]{1,0:T(8,128)(2,1)} %get-tuple-element.17.k_hbm, bf16[8,80,768]{2,1,0:T(8,128)(2,1)} %get-tuple-element.18.v_hbm, bf16[384,1152]{1,0:T(8,128)(2,1)} %bitcast.31, ...), custom_call_target="tpu_custom_call" | custom-call | flops 1528823808 | bytes 8000000 | tf_op jit(solution)/shard_map/pallas_call | solution.py:429
  61.7 1.7 %collective-permute-done.2.att_hbm = bf16[384,576]{1,0:T(8,128)(2,1)} collective-permute-done((bf16[384,576]{1,0:T(8,128)(2,1)}, bf16[384,576]{1,0:T(8,128)(2,1)}, u32[]{:S(2)}, u32[]{:S(2)}) %collective-permute-start.2) | collective-permute-done | bytes 442400 | tf_op jit(solution)/shard_map/ppermute | solution.py:428
  63.5 0.5 all-gather.4.cloned.1.call-done.w_hbm
  64.0 5.5 %shard_map.103 = (f32[384,1152]{1,0:T(8,128)}, bf16[384,1152]{1,0:T(8,128)(2,1)}) custom-call(f32[384,1152]{1,0:T(8,128)} %shard_map.102.part_hbm, bf16[384,576]{1,0:T(8,128)(2,1)} %collective-permute-done.2.att_hbm, bf16[576,1152]{1,0:T(8,128)(2,1)} %all-gather.4.cloned.1.call-done.w_hbm, f32[3,1152]{1,0:T(4,128)} %get-tuple-element.19.mods, ...), custom_call_target="tpu_custom_call" | custom-call | flops 509607936 | bytes 6000000 | tf_op jit(solution)/shard_map/pallas_call | solution.py:449
  69.4 9.1 %all-to-all-start.1 = ((bf16[16,24,1152]{2,1,0:T(8,128)(2,1)}), bf16[16,24,1152]{2,1,0:T(8,128)(2,1)}, u32[]{:S(2)}, u32[]{:S(2)}) async-start(bf16[16,24,1152]{2,1,0:T(8,128)(2,1)} %bitcast.32), calls=%async_computation.1 | async-start | bytes 1769472 | tf_op jit(solution)/shard_map/all_to_all | solution.py:469
  78.6 1.0 constant_dynamic-slice_fusion
  79.6 2.3 %collective-permute-start.5 = (bf16[72,1152]{1,0:T(8,128)(2,1)S(1)}, bf16[72,1152]{1,0:T(8,128)(2,1)S(1)}, u32[]{:S(2)}, u32[]{:S(2)}) collective-permute-start(bf16[72,1152]{1,0:T(8,128)(2,1)S(1)} %constant_dynamic-slice_fusion), channel_id=1, source_target_pairs={{0,3},{1,2},{2,1},{3,0},{4,7},{5,6},{6,5},{7,4},{8,11},{9,10},{10,... | collective-permute-start | bytes 497672 | tf_op jit(solution)/shard_map/ppermute | solution.py:467
  81.9 3.4 %collective-permute-done.5 = bf16[72,1152]{1,0:T(8,128)(2,1)S(1)} collective-permute-done((bf16[72,1152]{1,0:T(8,128)(2,1)S(1)}, bf16[72,1152]{1,0:T(8,128)(2,1)S(1)}, u32[]{:S(2)}, u32[]{:S(2)}) %collective-permute-start.5) | collective-permute-done | bytes 165920 | tf_op jit(solution)/shard_map/ppermute | solution.py:467
  85.2 0.7 copy-done.2
  85.9 16.6 %all-to-all-done.1 = bf16[16,24,1152]{2,1,0:T(8,128)(2,1)} async-done(((bf16[16,24,1152]{2,1,0:T(8,128)(2,1)}), bf16[16,24,1152]{2,1,0:T(8,128)(2,1)}, u32[]{:S(2)}, u32[]{:S(2)}) %all-to-all-start.1) | async-done | bytes 884768 | tf_op jit(solution)/shard_map/all_to_all | solution.py:469
  102.5 9.2 %shard_map.104 = bf16[384,1152]{1,0:T(8,128)(2,1)} custom-call(bf16[384,1152]{1,0:T(8,128)(2,1)} %bitcast.12.moved_hbm, bf16[1728,1152]{1,0:T(8,128)(2,1)} %bitcast.37, bf16[1728,1152]{1,0:T(8,128)(2,1)} %all-gather.6.cloned.1.call-done.other_hbm), custom_call_target="tpu_custom_call" | custom-call | flops 3057647616 | bytes 10000000 | tf_op jit(solution)/shard_map/pallas_call | solution.py:472
  111.8 5.7 %all-to-all-start.2 = ((bf16[16,24,1152]{2,1,0:T(8,128)(2,1)}), bf16[16,24,1152]{2,1,0:T(8,128)(2,1)}, u32[]{:S(2)}, u32[]{:S(2)}) async-start(bf16[16,24,1152]{2,1,0:T(8,128)(2,1)} %bitcast.33), calls=%async_computation.2 | async-start | bytes 1769472 | tf_op jit(solution)/shard_map/all_to_all | solution.py:488
  117.4 11.5 %all-gather.8.cloned.1.call-done.other_w = bf16[576,1152]{1,0:T(8,128)(2,1)} async-done(((bf16[72,1152]{1,0:T(8,128)(2,1)}), bf16[576,1152]{1,0:T(8,128)(2,1)}) %all-gather.8.cloned.1.call-update) | async-done | bytes 1327120 | tf_op jit(solution)/shard_map/all_gather | solution.py:468
  128.9 14.3 %all-to-all-done.2 = bf16[16,24,1152]{2,1,0:T(8,128)(2,1)} async-done(((bf16[16,24,1152]{2,1,0:T(8,128)(2,1)}), bf16[16,24,1152]{2,1,0:T(8,128)(2,1)}, u32[]{:S(2)}, u32[]{:S(2)}) %all-to-all-start.2) | async-done | bytes 884768 | tf_op jit(solution)/shard_map/all_to_all | solution.py:488
  143.2 5.3 %shard_map.105 = f32[3456,128]{1,0:T(8,128)} custom-call(bf16[384,1152]{1,0:T(8,128)(2,1)} %bitcast.14.att_hbm, bf16[576,1152]{1,0:T(8,128)(2,1)} %own_w.1, bf16[576,1152]{1,0:T(8,128)(2,1)} %all-gather.8.cloned.1.call-done.other_w, f32[384,1152]{1,0:T(8,128)} %get-tuple-element.26.middle_hbm, f32[3,1152]{1,0:T(4,128)} %get-tuple-element.22.next_mods.mods), custom_call_target="tpu_custom_call" | custom-call | flops 1019215872 | bytes 8000000 | tf_op jit(solution)/shard_map/pallas_call | solution.py:490
  (24 shorter events, 0.8 us)
Async XLA Ops:
  6.5 4.1 %copy-start = (bf16[256,1152]{1,0:T(8,128)(2,1)S(1)}, bf16[256,1152]{1,0:T(8,128)(2,1)}, u32[]{:S(2)}) copy-start(bf16[256,1152]{1,0:T(8,128)(2,1)} %param.12) | copy-start | bytes 1769476
  6.5 27.4 %collective-permute-start = (bf16[384,1152]{1,0:T(8,128)(2,1)}, bf16[384,1152]{1,0:T(8,128)(2,1)S(1)}, u32[]{:S(2)}, u32[]{:S(2)}) collective-permute-start(bf16[384,1152]{1,0:T(8,128)(2,1)} %bitcast.29), channel_id=1, source_target_pairs={{0,1},{1,0},{2,3},{3,2},{4,5},{5,4},{6,7},{7,6},{8,9},{9,8},{10,11... | collective-permute-start | bytes 2654216 | tf_op jit(solution)/shard_map/ppermute | solution.py:370
  12.1 20.2 %all-to-all-start = ((f32[16,32,128]{2,1,0:T(8,128)}), f32[16,32,128]{2,1,0:T(8,128)S(1)}, u32[]{:S(2)}, u32[]{:S(2)}) async-start(f32[16,32,128]{2,1,0:T(8,128)} %broadcast_in_dim.2), calls=%async_computation | async-start | bytes 524288 | tf_op jit(solution)/shard_map/all_to_all | solution.py:381
  20.5 43.5 %all-gather.4.cloned.1.call-start = ((), (), s32[]{:S(2)}) async-start(), calls=%async_computation.3 | async-start | bytes 1492992 | tf_op jit(solution)/shard_map/all_gather | solution.py:395
  21.4 12.5 %collective-permute-start.3 = (bf16[72,1152]{1,0:T(8,128)(2,1)S(1)}, bf16[72,1152]{1,0:T(8,128)(2,1)S(1)}, u32[]{:S(2)}, u32[]{:S(2)}) collective-permute-start(bf16[72,1152]{1,0:T(8,128)(2,1)S(1)} %constant_dynamic-slice_fusion.1), channel_id=1, source_target_pairs={{0,3},{1,2},{2,1},{3,0},{4,7},{5,6},{6,5},{7,4},{8,11},{9,10},{10,... | collective-permute-start | bytes 497672 | tf_op jit(solution)/shard_map/ppermute | solution.py:378
  32.4 4.4 %copy-start.3 = (f32[32,128]{1,0:T(8,128)}, f32[32,128]{1,0:T(8,128)S(1)}, u32[]{:S(2)}) copy-start(f32[32,128]{1,0:T(8,128)S(1)} %reduce_sum.9.own_total) | copy-start | bytes 49156
  32.4 5.3 %collective-permute-start.1 = (f32[32,128]{1,0:T(8,128)S(1)}, f32[32,128]{1,0:T(8,128)S(1)}, u32[]{:S(2)}, u32[]{:S(2)}) collective-permute-start(f32[32,128]{1,0:T(8,128)S(1)} %reduce_sum.9.own_total), channel_id=1, source_target_pairs={{0,1},{1,0},{2,3},{3,2},{4,5},{5,4},{6,7},{7,6},{8,9},{9,8},{10,11... | collective-permute-start | bytes 49160 | tf_op jit(solution)/shard_map/ppermute | solution.py:383
  34.0 0.7 copy-start.1
  34.0 1.0 copy-start.4
  34.9 67.6 %all-gather.6.cloned.1.call-start = ((), (), s32[]{:S(2)}) async-start(), calls=%async_computation.4 | async-start | bytes 4478976 | tf_op jit(solution)/shard_map/all_gather | solution.py:448
  36.8 26.7 %collective-permute-start.4 = (bf16[216,1152]{1,0:T(8,128)(2,1)}, bf16[216,1152]{1,0:T(8,128)(2,1)}, u32[]{:S(2)}, u32[]{:S(2)}) collective-permute-start(bf16[216,1152]{1,0:T(8,128)(2,1)} %shard_map.100.after), channel_id=1, source_target_pairs={{0,3},{1,2},{2,1},{3,0},{4,7},{5,6},{6,5},{7,4},{8,11},{9,10},{10,... | collective-permute-start | bytes 1493000 | tf_op jit(solution)/shard_map/ppermute | solution.py:396
  37.7 0.6 copy-start.5
  49.8 13.7 %collective-permute-start.2 = (bf16[384,576]{1,0:T(8,128)(2,1)}, bf16[384,576]{1,0:T(8,128)(2,1)}, u32[]{:S(2)}, u32[]{:S(2)}) collective-permute-start(bf16[384,576]{1,0:T(8,128)(2,1)} %get-tuple-element.20), channel_id=1, source_target_pairs={{0,1},{1,0},{2,3},{3,2},{4,5},{5,4},{6,7},{7,6},{8,9},{9,8},{10,11... | collective-permute-start | bytes 1327112 | tf_op jit(solution)/shard_map/ppermute | solution.py:428
  69.4 33.1 %all-to-all-start.1 = ((bf16[16,24,1152]{2,1,0:T(8,128)(2,1)}), bf16[16,24,1152]{2,1,0:T(8,128)(2,1)}, u32[]{:S(2)}, u32[]{:S(2)}) async-start(bf16[16,24,1152]{2,1,0:T(8,128)(2,1)} %bitcast.32), calls=%async_computation.1 | async-start | bytes 1769472 | tf_op jit(solution)/shard_map/all_to_all | solution.py:469
  78.6 50.3 %all-gather.8.cloned.1.call-start = ((), (), s32[]{:S(2)}) async-start(), calls=%async_computation.5 | async-start | bytes 1492992 | tf_op jit(solution)/shard_map/all_gather | solution.py:468
  79.6 5.6 %collective-permute-start.5 = (bf16[72,1152]{1,0:T(8,128)(2,1)S(1)}, bf16[72,1152]{1,0:T(8,128)(2,1)S(1)}, u32[]{:S(2)}, u32[]{:S(2)}) collective-permute-start(bf16[72,1152]{1,0:T(8,128)(2,1)S(1)} %constant_dynamic-slice_fusion), channel_id=1, source_target_pairs={{0,3},{1,2},{2,1},{3,0},{4,7},{5,6},{6,5},{7,4},{8,11},{9,10},{10,... | collective-permute-start | bytes 497672 | tf_op jit(solution)/shard_map/ppermute | solution.py:467
  85.2 0.7 copy-start.2
  111.8 31.5 %all-to-all-start.2 = ((bf16[16,24,1152]{2,1,0:T(8,128)(2,1)}), bf16[16,24,1152]{2,1,0:T(8,128)(2,1)}, u32[]{:S(2)}, u32[]{:S(2)}) async-start(bf16[16,24,1152]{2,1,0:T(8,128)(2,1)} %bitcast.33), calls=%async_computation.2 | async-start | bytes 1769472 | tf_op jit(solution)/shard_map/all_to_all | solution.py:488
Sparse Core Ops, SparseCore 0:
  34.8 29.1 all-gather.3
  65.8 34.5 all-gather.5
  102.3 26.5 all-gather.7

commit v5 on v4

--- a/solution.py
+++ b/solution.py
@@ -85,7 +85,7 @@
 
 def head_output(scores, values):
     peak = jnp.max(scores, axis=0, keepdims=True)
-    raised = jnp.exp2(scores - peak).astype(BF16)
+    raised = jnp.exp2((scores - peak) * SCALE).astype(BF16)
     out = jnp.dot(values, raised, preferred_element_type=F32)
     return out[:HEAD_DIM] / out[HEAD_DIM : HEAD_DIM + 1]
 
@@ -142,7 +142,7 @@
     in_far.wait()
     normed_far = normalise(far[...].astype(F32), mods[0:1], mods[1:2])
     in_w[0].wait()
-    q[...] = dot_nt(w[0], normed_far) * SCALE
+    q[...] = dot_nt(w[0], normed_far)
     in_w[1].wait()
     k[beyond, :half] = dot_nt(normed_far, w[1]).astype(BF16)
     in_tok.wait()
@@ -197,7 +197,7 @@
     ]
     copies[0].wait()
     copies[1].wait()
-    queries = dot_nt(in_w[...], normed[...]) * SCALE
+    queries = dot_nt(in_w[...], normed[...])
     copies[2].wait()
     for head in range(heads):
         scores[head] = head_scores(queries, k, head)
@@ -216,7 +216,19 @@
 
 
 def middle_kernel(
-    part_hbm, att_hbm, w_hbm, mods, next_mods, middle_hbm, normed_out, part, att, w, middle, sems
+    part_hbm,
+    att_hbm,
+    w_hbm,
+    mods,
+    next_mods,
+    middle_hbm,
+    normed_hbm,
+    part,
+    att,
+    w,
+    middle,
+    normed,
+    sems,
 ):
     in_w = fetch(w_hbm, w, sems.at[0])
     in_att = fetch(att_hbm, att, sems.at[3])
@@ -225,10 +237,17 @@
     in_att.wait()
     projected = jnp.dot(att[...], w[...], preferred_element_type=F32)
     in_part.wait()
-    middle[...] = part[...] + mods[2:3] * projected
-    copy = fetch(middle, middle_hbm, sems.at[2])
-    normed_out[...] = normalise(middle[...], next_mods[0:1], next_mods[1:2])
-    copy.wait()
+    half = middle.shape[0] // 2
+    copies = []
+    for side in range(2):
+        rows = pl.ds(side * half, half)
+        values = part[rows, :] + mods[2:3] * projected[side * half : (side + 1) * half]
+        middle[rows, :] = values
+        normed[rows, :] = normalise(values, next_mods[0:1], next_mods[1:2])
+        copies.append(fetch(normed.at[rows], normed_hbm.at[rows], sems.at[4 + 2 * side]))
+        copies.append(fetch(middle.at[rows], middle_hbm.at[rows], sems.at[5 + 2 * side]))
+    for copy in copies:
+        copy.wait()
 
 
 def temporal_kernel(
@@ -261,7 +280,7 @@
     ).astype(BF16)
     copies[0].wait()
     copies[1].wait()
-    queries = dot_nt(w[0], tokens) * SCALE
+    queries = dot_nt(w[0], tokens)
     copies[2].wait()
     copies[3].wait()
     k[...] = dot_nt(tokens, w[1]).astype(BF16)
@@ -455,11 +474,12 @@
             pltpu.VMEM((count, half), BF16),
             pltpu.VMEM((half, width), BF16),
             pltpu.VMEM(tokens_shape, F32),
-            dma((4,)),
+            pltpu.VMEM(tokens_shape, BF16),
+            dma((8,)),
         ],
         flops=2 * count * half * width,
         nbytes=6_000_000,
-        out_specs=(HBM, VMEM),
+        out_specs=(HBM, HBM),
         mib=63.1,
     )(part, attended, spatial_out_other, spatial_mods, temporal_mods)
 

time: 156 us -> 156 us (level)
  no operation moved by 1% of the time
where the time goes in v5:
time: 156 us; the launch traced here: 155 us
  waiting for transfers between devices  54.6 us (35%)
  Pallas kernels  42.6 us (27%)
  starting transfers between devices  35.6 us (23%)
  between operations  13.9 us (9%)
  local copies, waits for them, and re-layouts  7.82 us (5%)
    all_to_all x1, waiting for transfers between devices, body(): moved = lax.all_to_all(normed, 'seq', 0, 0, tiled=True)  16.1 us
    all_to_all x1, waiting for transfers between devices, body(): returned = lax.all_to_all(attended, 'seq', 0, 0, tiled=True)  14.4 us
    pallas_call x1, Pallas kernels, body(): call(functools.partial(spatial_kernel, heads), (shape((3, width), F32), s...  11.7 us
    all_gather x1, waiting for transfers between devices, body(): temporal_out_other = lax.all_gather(out_piece, 'clip', axis=0, tiled=True)  11.5 us
    all_to_all x1, starting transfers between devices, body(): moved = lax.all_to_all(normed, 'seq', 0, 0, tiled=True)  9.33 us
    pallas_call x1, Pallas kernels, body(): call(functools.partial(near_kernel, heads), shape(tokens_shape, F32), [HB...  9.3 us
    pallas_call x1, Pallas kernels, body(): call(functools.partial(temporal_kernel, heads, positions), shape((count,...  9.25 us
    all_to_all x1, starting transfers between devices, body(): terms = lax.all_to_all(copies.reshape(-1, LANES), 'seq', 0, 0, tiled=True)  8.37 us
  transfers between devices with their start and end apart: 12, of which 8 were waited for; matrix products, arithmetic and copies ran while one was open for 4% of the time, Pallas kernels for 24%

profile of v5, /device:TPU:4, one launch (start us, length us, event | category | flops | bytes accessed | tf_op | source)
XLA Modules:
  0.0 155.3 jit_solution(2775666948847159484)
XLA Ops:
  6.5 2.2 %collective-permute-start = (bf16[384,1152]{1,0:T(8,128)(2,1)}, bf16[384,1152]{1,0:T(8,128)(2,1)S(1)}, u32[]{:S(2)}, u32[]{:S(2)}) collective-permute-start(bf16[384,1152]{1,0:T(8,128)(2,1)} %bitcast.29), channel_id=1, source_target_pairs={{0,1},{1,0},{2,3},{3,2},{4,5},{5,4},{6,7},{7,6},{8,9},{9,8},{10,11... | collective-permute-start | bytes 2654216 | tf_op jit(solution)/shard_map/ppermute | solution.py:389
  9.5 1.1 dot_general.12
  10.6 0.4 convolution_reduce_fusion
  11.0 0.3 fusion
  11.3 0.7 broadcast_in_dim.2
  12.1 8.4 %all-to-all-start = ((f32[16,32,128]{2,1,0:T(8,128)}), f32[16,32,128]{2,1,0:T(8,128)S(1)}, u32[]{:S(2)}, u32[]{:S(2)}) async-start(f32[16,32,128]{2,1,0:T(8,128)} %broadcast_in_dim.2), calls=%async_computation | async-start | bytes 524288 | tf_op jit(solution)/shard_map/all_to_all | solution.py:400
  20.5 0.9 constant_dynamic-slice_fusion.1
  21.4 2.1 %collective-permute-start.3 = (bf16[72,1152]{1,0:T(8,128)(2,1)S(1)}, bf16[72,1152]{1,0:T(8,128)(2,1)S(1)}, u32[]{:S(2)}, u32[]{:S(2)}) collective-permute-start(bf16[72,1152]{1,0:T(8,128)(2,1)S(1)} %constant_dynamic-slice_fusion.1), channel_id=1, source_target_pairs={{0,3},{1,2},{2,1},{3,0},{4,7},{5,6},{6,5},{7,4},{8,11},{9,10},{10,... | collective-permute-start | bytes 497672 | tf_op jit(solution)/shard_map/ppermute | solution.py:397
  23.5 1.9 %constant_dynamic-slice_fusion.2.own_hbm = bf16[216,1152]{1,0:T(8,128)(2,1)} fusion(bf16[1728,1152]{1,0:T(8,128)(2,1)} %bitcast.36, s32[]{:T(128)S(6)} %select_n.11), kind=kLoop, calls=%fused_computation.9 | loop fusion | bytes 995332 | tf_op jit(solution)/shard_map/dynamic_slice | solution.py:369
  25.4 6.9 %all-to-all-done = f32[16,32,128]{2,1,0:T(8,128)S(1)} async-done(((f32[16,32,128]{2,1,0:T(8,128)}), f32[16,32,128]{2,1,0:T(8,128)S(1)}, u32[]{:S(2)}, u32[]{:S(2)}) %all-to-all-start) | async-done | bytes 262176 | tf_op jit(solution)/shard_map/all_to_all | solution.py:400
  32.4 1.6 %collective-permute-start.1 = (f32[32,128]{1,0:T(8,128)S(1)}, f32[32,128]{1,0:T(8,128)S(1)}, u32[]{:S(2)}, u32[]{:S(2)}) collective-permute-start(f32[32,128]{1,0:T(8,128)S(1)} %reduce_sum.9.own_total), channel_id=1, source_target_pairs={{0,1},{1,0},{2,3},{3,2},{4,5},{5,4},{6,7},{7,6},{8,9},{9,8},{10,11... | collective-permute-start | bytes 49160 | tf_op jit(solution)/shard_map/ppermute | solution.py:402
  34.0 0.6 copy-done.1
  34.9 1.8 %shard_map.100.after = bf16[216,1152]{1,0:T(8,128)(2,1)} custom-call(bf16[216,1152]{1,0:T(8,128)(2,1)} %constant_dynamic-slice_fusion.2.own_hbm, bf16[384,1152]{1,0:T(8,128)(2,1)} %copy-done.4), custom_call_target="tpu_custom_call" | custom-call | flops 20000000000 | bytes 1500000 | tf_op jit(solution)/shard_map/pallas_call | solution.py:404
  36.8 0.4 collective-permute-start.4
  37.2 0.5 collective-permute-done.1.other_total
  37.7 0.6 copy-done.5
  38.3 11.7 %shard_map.101 = (f32[3,1152]{1,0:T(4,128)}, f32[3,1152]{1,0:T(4,128)}, bf16[384,1152]{1,0:T(8,128)(2,1)}, bf16[768,640]{1,0:T(8,128)(2,1)}, bf16[8,80,768]{2,1,0:T(8,128)(2,1)}, /*index=5*/bf16[384,576]{1,0:T(8,128)(2,1)}) custom-call(bf16[384,1152]{1,0:T(8,128)(2,1)} %bitcast.30, bf16[384,1152]{1,0:T(8,128)(2,1)} %copy-done.4, f32[32,128]{1,0:T(8,128)} %copy-done.3, ...), custom_call_target="tpu_custom_call" | custom-call | flops 3567255552 | bytes 14000000 | tf_op jit(solution)/shard_map/pallas_call | solution.py:421
  50.0 2.8 %collective-permute-start.2 = (bf16[384,576]{1,0:T(8,128)(2,1)}, bf16[384,576]{1,0:T(8,128)(2,1)}, u32[]{:S(2)}, u32[]{:S(2)}) collective-permute-start(bf16[384,576]{1,0:T(8,128)(2,1)} %get-tuple-element.20), channel_id=1, source_target_pairs={{0,1},{1,0},{2,3},{3,2},{4,5},{5,4},{6,7},{7,6},{8,9},{9,8},{10,11... | collective-permute-start | bytes 1327112 | tf_op jit(solution)/shard_map/ppermute | solution.py:447
  52.7 9.3 %shard_map.102.part_hbm = f32[384,1152]{1,0:T(8,128)} custom-call(bf16[384,1152]{1,0:T(8,128)(2,1)} %get-tuple-element.16.normed_hbm, bf16[1728,1152]{1,0:T(8,128)(2,1)} %bitcast.28, bf16[768,640]{1,0:T(8,128)(2,1)} %get-tuple-element.17.k_hbm, bf16[8,80,768]{2,1,0:T(8,128)(2,1)} %get-tuple-element.18.v_hbm, bf16[384,1152]{1,0:T(8,128)(2,1)} %bitcast.31, ...), custom_call_target="tpu_custom_call" | custom-call | flops 1528823808 | bytes 8000000 | tf_op jit(solution)/shard_map/pallas_call | solution.py:448
  62.0 1.6 %collective-permute-done.2.att_hbm = bf16[384,576]{1,0:T(8,128)(2,1)} collective-permute-done((bf16[384,576]{1,0:T(8,128)(2,1)}, bf16[384,576]{1,0:T(8,128)(2,1)}, u32[]{:S(2)}, u32[]{:S(2)}) %collective-permute-start.2) | collective-permute-done | bytes 442400 | tf_op jit(solution)/shard_map/ppermute | solution.py:447
  63.9 5.2 %shard_map.103 = (f32[384,1152]{1,0:T(8,128)}, bf16[384,1152]{1,0:T(8,128)(2,1)}) custom-call(f32[384,1152]{1,0:T(8,128)} %shard_map.102.part_hbm, bf16[384,576]{1,0:T(8,128)(2,1)} %collective-permute-done.2.att_hbm, bf16[576,1152]{1,0:T(8,128)(2,1)} %all-gather.4.cloned.1.call-done.w_hbm, f32[3,1152]{1,0:T(4,128)} %get-tuple-element.19.mods, ...), custom_call_target="tpu_custom_call" | custom-call | flops 509607936 | bytes 6000000 | tf_op jit(solution)/shard_map/pallas_call | solution.py:468
  69.2 9.3 %all-to-all-start.1 = ((bf16[16,24,1152]{2,1,0:T(8,128)(2,1)}), bf16[16,24,1152]{2,1,0:T(8,128)(2,1)}, u32[]{:S(2)}, u32[]{:S(2)}) async-start(bf16[16,24,1152]{2,1,0:T(8,128)(2,1)} %bitcast.32), calls=%async_computation.1 | async-start | bytes 1769472 | tf_op jit(solution)/shard_map/all_to_all | solution.py:489
  78.6 1.0 constant_dynamic-slice_fusion
  79.5 2.3 %collective-permute-start.5 = (bf16[72,1152]{1,0:T(8,128)(2,1)S(1)}, bf16[72,1152]{1,0:T(8,128)(2,1)S(1)}, u32[]{:S(2)}, u32[]{:S(2)}) collective-permute-start(bf16[72,1152]{1,0:T(8,128)(2,1)S(1)} %constant_dynamic-slice_fusion), channel_id=1, source_target_pairs={{0,3},{1,2},{2,1},{3,0},{4,7},{5,6},{6,5},{7,4},{8,11},{9,10},{10,... | collective-permute-start | bytes 497672 | tf_op jit(solution)/shard_map/ppermute | solution.py:487
  81.8 3.3 %collective-permute-done.5 = bf16[72,1152]{1,0:T(8,128)(2,1)S(1)} collective-permute-done((bf16[72,1152]{1,0:T(8,128)(2,1)S(1)}, bf16[72,1152]{1,0:T(8,128)(2,1)S(1)}, u32[]{:S(2)}, u32[]{:S(2)}) %collective-permute-start.5) | collective-permute-done | bytes 165920 | tf_op jit(solution)/shard_map/ppermute | solution.py:487
  85.2 0.7 copy-done.2
  85.9 16.1 %all-to-all-done.1 = bf16[16,24,1152]{2,1,0:T(8,128)(2,1)} async-done(((bf16[16,24,1152]{2,1,0:T(8,128)(2,1)}), bf16[16,24,1152]{2,1,0:T(8,128)(2,1)}, u32[]{:S(2)}, u32[]{:S(2)}) %all-to-all-start.1) | async-done | bytes 884768 | tf_op jit(solution)/shard_map/all_to_all | solution.py:489
  101.9 9.2 %shard_map.104 = bf16[384,1152]{1,0:T(8,128)(2,1)} custom-call(bf16[384,1152]{1,0:T(8,128)(2,1)} %bitcast.12.moved_hbm, bf16[1728,1152]{1,0:T(8,128)(2,1)} %bitcast.37, bf16[1728,1152]{1,0:T(8,128)(2,1)} %all-gather.6.cloned.1.call-done.other_hbm), custom_call_target="tpu_custom_call" | custom-call | flops 3057647616 | bytes 10000000 | tf_op jit(solution)/shard_map/pallas_call | solution.py:492
  111.2 6.4 %all-to-all-start.2 = ((bf16[16,24,1152]{2,1,0:T(8,128)(2,1)}), bf16[16,24,1152]{2,1,0:T(8,128)(2,1)}, u32[]{:S(2)}, u32[]{:S(2)}) async-start(bf16[16,24,1152]{2,1,0:T(8,128)(2,1)} %bitcast.33), calls=%async_computation.2 | async-start | bytes 1769472 | tf_op jit(solution)/shard_map/all_to_all | solution.py:508
  117.7 11.5 %all-gather.8.cloned.1.call-done.other_w = bf16[576,1152]{1,0:T(8,128)(2,1)} async-done(((bf16[72,1152]{1,0:T(8,128)(2,1)}), bf16[576,1152]{1,0:T(8,128)(2,1)}) %all-gather.8.cloned.1.call-update) | async-done | bytes 1327120 | tf_op jit(solution)/shard_map/all_gather | solution.py:488
  129.1 14.4 %all-to-all-done.2 = bf16[16,24,1152]{2,1,0:T(8,128)(2,1)} async-done(((bf16[16,24,1152]{2,1,0:T(8,128)(2,1)}), bf16[16,24,1152]{2,1,0:T(8,128)(2,1)}, u32[]{:S(2)}, u32[]{:S(2)}) %all-to-all-start.2) | async-done | bytes 884768 | tf_op jit(solution)/shard_map/all_to_all | solution.py:508
  143.5 5.3 %shard_map.105 = f32[3456,128]{1,0:T(8,128)} custom-call(bf16[384,1152]{1,0:T(8,128)(2,1)} %bitcast.14.att_hbm, bf16[576,1152]{1,0:T(8,128)(2,1)} %own_w.1, bf16[576,1152]{1,0:T(8,128)(2,1)} %all-gather.8.cloned.1.call-done.other_w, f32[384,1152]{1,0:T(8,128)} %get-tuple-element.26.middle_hbm, f32[3,1152]{1,0:T(4,128)} %get-tuple-element.22.next_mods.mods), custom_call_target="tpu_custom_call" | custom-call | flops 1019215872 | bytes 8000000 | tf_op jit(solution)/shard_map/pallas_call | solution.py:510
  (24 shorter events, 0.8 us)
Async XLA Ops:
  6.5 4.1 %copy-start = (bf16[256,1152]{1,0:T(8,128)(2,1)S(1)}, bf16[256,1152]{1,0:T(8,128)(2,1)}, u32[]{:S(2)}) copy-start(bf16[256,1152]{1,0:T(8,128)(2,1)} %param.12) | copy-start | bytes 1769476
  6.5 27.4 %collective-permute-start = (bf16[384,1152]{1,0:T(8,128)(2,1)}, bf16[384,1152]{1,0:T(8,128)(2,1)S(1)}, u32[]{:S(2)}, u32[]{:S(2)}) collective-permute-start(bf16[384,1152]{1,0:T(8,128)(2,1)} %bitcast.29), channel_id=1, source_target_pairs={{0,1},{1,0},{2,3},{3,2},{4,5},{5,4},{6,7},{7,6},{8,9},{9,8},{10,11... | collective-permute-start | bytes 2654216 | tf_op jit(solution)/shard_map/ppermute | solution.py:389
  12.1 20.2 %all-to-all-start = ((f32[16,32,128]{2,1,0:T(8,128)}), f32[16,32,128]{2,1,0:T(8,128)S(1)}, u32[]{:S(2)}, u32[]{:S(2)}) async-start(f32[16,32,128]{2,1,0:T(8,128)} %broadcast_in_dim.2), calls=%async_computation | async-start | bytes 524288 | tf_op jit(solution)/shard_map/all_to_all | solution.py:400
  20.5 43.5 %all-gather.4.cloned.1.call-start = ((), (), s32[]{:S(2)}) async-start(), calls=%async_computation.3 | async-start | bytes 1492992 | tf_op jit(solution)/shard_map/all_gather | solution.py:414
  21.4 12.5 %collective-permute-start.3 = (bf16[72,1152]{1,0:T(8,128)(2,1)S(1)}, bf16[72,1152]{1,0:T(8,128)(2,1)S(1)}, u32[]{:S(2)}, u32[]{:S(2)}) collective-permute-start(bf16[72,1152]{1,0:T(8,128)(2,1)S(1)} %constant_dynamic-slice_fusion.1), channel_id=1, source_target_pairs={{0,3},{1,2},{2,1},{3,0},{4,7},{5,6},{6,5},{7,4},{8,11},{9,10},{10,... | collective-permute-start | bytes 497672 | tf_op jit(solution)/shard_map/ppermute | solution.py:397
  32.4 4.4 %copy-start.3 = (f32[32,128]{1,0:T(8,128)}, f32[32,128]{1,0:T(8,128)S(1)}, u32[]{:S(2)}) copy-start(f32[32,128]{1,0:T(8,128)S(1)} %reduce_sum.9.own_total) | copy-start | bytes 49156
  32.4 5.3 %collective-permute-start.1 = (f32[32,128]{1,0:T(8,128)S(1)}, f32[32,128]{1,0:T(8,128)S(1)}, u32[]{:S(2)}, u32[]{:S(2)}) collective-permute-start(f32[32,128]{1,0:T(8,128)S(1)} %reduce_sum.9.own_total), channel_id=1, source_target_pairs={{0,1},{1,0},{2,3},{3,2},{4,5},{5,4},{6,7},{7,6},{8,9},{9,8},{10,11... | collective-permute-start | bytes 49160 | tf_op jit(solution)/shard_map/ppermute | solution.py:402
  34.0 0.7 copy-start.1
  34.0 1.0 copy-start.4
  34.9 67.0 %all-gather.6.cloned.1.call-start = ((), (), s32[]{:S(2)}) async-start(), calls=%async_computation.4 | async-start | bytes 4478976 | tf_op jit(solution)/shard_map/all_gather | solution.py:467
  36.8 26.9 %collective-permute-start.4 = (bf16[216,1152]{1,0:T(8,128)(2,1)}, bf16[216,1152]{1,0:T(8,128)(2,1)}, u32[]{:S(2)}, u32[]{:S(2)}) collective-permute-start(bf16[216,1152]{1,0:T(8,128)(2,1)} %shard_map.100.after), channel_id=1, source_target_pairs={{0,3},{1,2},{2,1},{3,0},{4,7},{5,6},{6,5},{7,4},{8,11},{9,10},{10,... | collective-permute-start | bytes 1493000 | tf_op jit(solution)/shard_map/ppermute | solution.py:415
  37.7 0.6 copy-start.5
  50.0 13.7 %collective-permute-start.2 = (bf16[384,576]{1,0:T(8,128)(2,1)}, bf16[384,576]{1,0:T(8,128)(2,1)}, u32[]{:S(2)}, u32[]{:S(2)}) collective-permute-start(bf16[384,576]{1,0:T(8,128)(2,1)} %get-tuple-element.20), channel_id=1, source_target_pairs={{0,1},{1,0},{2,3},{3,2},{4,5},{5,4},{6,7},{7,6},{8,9},{9,8},{10,11... | collective-permute-start | bytes 1327112 | tf_op jit(solution)/shard_map/ppermute | solution.py:447
  69.2 32.8 %all-to-all-start.1 = ((bf16[16,24,1152]{2,1,0:T(8,128)(2,1)}), bf16[16,24,1152]{2,1,0:T(8,128)(2,1)}, u32[]{:S(2)}, u32[]{:S(2)}) async-start(bf16[16,24,1152]{2,1,0:T(8,128)(2,1)} %bitcast.32), calls=%async_computation.1 | async-start | bytes 1769472 | tf_op jit(solution)/shard_map/all_to_all | solution.py:489
  78.5 50.6 %all-gather.8.cloned.1.call-start = ((), (), s32[]{:S(2)}) async-start(), calls=%async_computation.5 | async-start | bytes 1492992 | tf_op jit(solution)/shard_map/all_gather | solution.py:488
  79.5 5.6 %collective-permute-start.5 = (bf16[72,1152]{1,0:T(8,128)(2,1)S(1)}, bf16[72,1152]{1,0:T(8,128)(2,1)S(1)}, u32[]{:S(2)}, u32[]{:S(2)}) collective-permute-start(bf16[72,1152]{1,0:T(8,128)(2,1)S(1)} %constant_dynamic-slice_fusion), channel_id=1, source_target_pairs={{0,3},{1,2},{2,1},{3,0},{4,7},{5,6},{6,5},{7,4},{8,11},{9,10},{10,... | collective-permute-start | bytes 497672 | tf_op jit(solution)/shard_map/ppermute | solution.py:487
  85.2 0.7 copy-start.2
  111.2 32.3 %all-to-all-start.2 = ((bf16[16,24,1152]{2,1,0:T(8,128)(2,1)}), bf16[16,24,1152]{2,1,0:T(8,128)(2,1)}, u32[]{:S(2)}, u32[]{:S(2)}) async-start(bf16[16,24,1152]{2,1,0:T(8,128)(2,1)} %bitcast.33), calls=%async_computation.2 | async-start | bytes 1769472 | tf_op jit(solution)/shard_map/all_to_all | solution.py:508
Sparse Core Ops, SparseCore 0:
  34.8 29.1 all-gather.3
  65.8 34.7 all-gather.5
  102.5 26.5 all-gather.7

commit v6 on v4

--- a/solution.py
+++ b/solution.py
@@ -113,7 +113,6 @@
     table,
     next_table,
     w_hbm,
-    after,
     mods_out,
     next_out,
     normed_out,
@@ -208,11 +207,6 @@
     projected = jnp.dot(attended, w[...], preferred_element_type=F32)
     copies[5].wait()
     part_out[...] = tok[...].astype(F32) + mods[2:3] * projected
-
-
-def piece_kernel(own_hbm, after, out_hbm, piece, sems):
-    fetch(own_hbm, piece, sems.at[0]).wait()
-    fetch(piece, out_hbm, sems.at[1]).wait()
 
 
 def middle_kernel(
@@ -382,15 +376,7 @@
     own_total = jnp.sum(terms.reshape(copies.shape), axis=0)
     other_total = lax.ppermute(own_total, "tp", SWAP)
     own_piece = eighth(temporal_in)
-    own_piece = call(
-        piece_kernel,
-        shape(own_piece.shape, BF16),
-        [HBM] * 2,
-        [pltpu.VMEM(own_piece.shape, BF16), dma((2,))],
-        flops=20_000_000_000,
-        nbytes=1_500_000,
-        out_specs=HBM,
-    )(own_piece, far)
+    own_piece, _ = lax.optimization_barrier((own_piece, far))
     out_piece, _ = lax.optimization_barrier((out_piece, (own_total, far)))
     spatial_out_other = lax.all_gather(out_piece, "clip", axis=0, tiled=True)
     piece = lax.ppermute(own_piece, ("seq", "tp"), across)
@@ -409,7 +395,7 @@
             shape(v_shape, BF16),
             shape((count, half), BF16),
         ),
-        [HBM] * 2 + [VMEM] * 4 + [HBM] * 2,
+        [HBM] * 2 + [VMEM] * 4 + [HBM],
         [
             pltpu.VMEM(tokens_shape, BF16),
             pltpu.VMEM(tokens_shape, BF16),
@@ -424,7 +410,7 @@
         nbytes=14_000_000,
         out_specs=(VMEM, VMEM, HBM, HBM, HBM, VMEM),
         mib=63.1,
-    )(tokens, far, own_total, other_total, spatial_table, temporal_table, spatial_in, own_piece)
+    )(tokens, far, own_total, other_total, spatial_table, temporal_table, spatial_in)
     attended = lax.ppermute(far_attended, "tp", SWAP)
     part = call(
         functools.partial(near_kernel, heads),

time: 156 us -> 158 us (1.013)
  waiting for transfers between devices: 55.5 us -> 59.7 us
  Pallas kernels: 42.4 us -> 40.7 us
    all_to_all x1, waiting for transfers between devices: 6.95 us -> 8.82 us  [body(): terms = lax.all_to_all(copies.reshape(-1, LANES), 'seq', 0, 0, tiled=True)]
    pallas_call x1 -> x0, Pallas kernels: 1.82 us -> none  [body(): call(piece_kernel, shape(own_piece.shape, BF16), [HBM] * 2, [pltpu.VMEM(o...]
    ppermute x1, waiting for transfers between devices: 1.71 us -> 3.31 us  [body(): attended = lax.ppermute(far_attended, 'tp', SWAP)]
  transfers between devices with their start and end apart: 12 -> 12, of which waited for: 8 -> 8; matrix products, arithmetic and copies ran while one was open for 4% -> 4% of each run, Pallas kernels for 24% -> 23%
where the time goes in v6:
time: 158 us; the launch traced here: 157 us
  waiting for transfers between devices  59.7 us (38%)
  Pallas kernels  40.7 us (26%)
  starting transfers between devices  34.5 us (22%)
  between operations  13.9 us (9%)
  local copies, waits for them, and re-layouts  7.52 us (5%)
    all_to_all x1, waiting for transfers between devices, body(): moved = lax.all_to_all(normed, 'seq', 0, 0, tiled=True)  15.5 us
    all_to_all x1, waiting for transfers between devices, body(): returned = lax.all_to_all(attended, 'seq', 0, 0, tiled=True)  14.3 us
    pallas_call x1, Pallas kernels, body(): call(functools.partial(spatial_kernel, heads), (shape((3, width), F32), s...  11.5 us
    all_gather x1, waiting for transfers between devices, body(): temporal_out_other = lax.all_gather(out_piece, 'clip', axis=0, tiled=True)  11.5 us
    all_to_all x1, starting transfers between devices, body(): moved = lax.all_to_all(normed, 'seq', 0, 0, tiled=True)  9.65 us
    pallas_call x1, Pallas kernels, body(): call(functools.partial(near_kernel, heads), shape(tokens_shape, F32), [HB...  9.22 us
    pallas_call x1, Pallas kernels, body(): call(functools.partial(temporal_kernel, heads, positions), shape((count,...  9.22 us
    all_to_all x1, waiting for transfers between devices, body(): terms = lax.all_to_all(copies.reshape(-1, LANES), 'seq', 0, 0, tiled=True)  8.82 us
  transfers between devices with their start and end apart: 12, of which 8 were waited for; matrix products, arithmetic and copies ran while one was open for 4% of the time, Pallas kernels for 23%

profile of v6, /device:TPU:4, one launch (start us, length us, event | category | flops | bytes accessed | tf_op | source)
XLA Modules:
  0.0 157.1 jit_solution(11646257090599386626)
XLA Ops:
  6.5 2.2 %collective-permute-start = (bf16[384,1152]{1,0:T(8,128)(2,1)}, bf16[384,1152]{1,0:T(8,128)(2,1)S(1)}, u32[]{:S(2)}, u32[]{:S(2)}) collective-permute-start(bf16[384,1152]{1,0:T(8,128)(2,1)} %bitcast.29), channel_id=1, source_target_pairs={{0,1},{1,0},{2,3},{3,2},{4,5},{5,4},{6,7},{7,6},{8,9},{9,8},{10,11... | collective-permute-start | bytes 2654216 | tf_op jit(solution)/shard_map/ppermute | solution.py:364
  9.5 1.1 dot_general.12
  10.6 0.4 convolution_reduce_fusion
  11.0 0.3 fusion
  11.3 0.7 broadcast_in_dim.2
  12.1 8.4 %all-to-all-start = ((f32[16,32,128]{2,1,0:T(8,128)}), f32[16,32,128]{2,1,0:T(8,128)S(1)}, u32[]{:S(2)}, u32[]{:S(2)}) async-start(f32[16,32,128]{2,1,0:T(8,128)} %broadcast_in_dim.2), calls=%async_computation | async-start | bytes 524288 | tf_op jit(solution)/shard_map/all_to_all | solution.py:375
  20.5 0.9 constant_dynamic-slice_fusion.2
  21.4 2.1 %collective-permute-start.3 = (bf16[72,1152]{1,0:T(8,128)(2,1)S(1)}, bf16[72,1152]{1,0:T(8,128)(2,1)S(1)}, u32[]{:S(2)}, u32[]{:S(2)}) collective-permute-start(bf16[72,1152]{1,0:T(8,128)(2,1)S(1)} %constant_dynamic-slice_fusion.2), channel_id=1, source_target_pairs={{0,3},{1,2},{2,1},{3,0},{4,7},{5,6},{6,5},{7,4},{8,11},{9,10},{10,... | collective-permute-start | bytes 497672 | tf_op jit(solution)/shard_map/ppermute | solution.py:372
  23.5 8.8 %all-to-all-done = f32[16,32,128]{2,1,0:T(8,128)S(1)} async-done(((f32[16,32,128]{2,1,0:T(8,128)}), f32[16,32,128]{2,1,0:T(8,128)S(1)}, u32[]{:S(2)}, u32[]{:S(2)}) %all-to-all-start) | async-done | bytes 262176 | tf_op jit(solution)/shard_map/all_to_all | solution.py:375
  32.4 0.8 collective-permute-done.3
  33.2 0.7 copy-done.1
  33.9 0.8 collective-permute-start.1
  34.7 1.8 %constant_dynamic-slice_fusion.1 = bf16[216,1152]{1,0:T(8,128)(2,1)} fusion(bf16[1728,1152]{1,0:T(8,128)(2,1)} %bitcast.36, s32[]{:T(128)S(6)} %select_n.12), kind=kLoop, calls=%fused_computation.8 | loop fusion | bytes 995332 | tf_op jit(solution)/shard_map/dynamic_slice | solution.py:344
  36.6 2.0 %collective-permute-start.4 = (bf16[216,1152]{1,0:T(8,128)(2,1)}, bf16[216,1152]{1,0:T(8,128)(2,1)}, u32[]{:S(2)}, u32[]{:S(2)}) collective-permute-start(bf16[216,1152]{1,0:T(8,128)(2,1)} %constant_dynamic-slice_fusion.1), channel_id=1, source_target_pairs={{0,3},{1,2},{2,1},{3,0},{4,7},{5,6},{6,5},{7,4},{8,11},{9,10},{10,... | collective-permute-start | bytes 1493000 | tf_op jit(solution)/shard_map/ppermute | solution.py:382
  38.5 0.8 collective-permute-done.1.other_total
  39.4 0.6 copy-done.5
  40.0 11.5 %shard_map.100 = (f32[3,1152]{1,0:T(4,128)}, f32[3,1152]{1,0:T(4,128)}, bf16[384,1152]{1,0:T(8,128)(2,1)}, bf16[768,640]{1,0:T(8,128)(2,1)}, bf16[8,80,768]{2,1,0:T(8,128)(2,1)}, /*index=5*/bf16[384,576]{1,0:T(8,128)(2,1)}) custom-call(bf16[384,1152]{1,0:T(8,128)(2,1)} %bitcast.30, bf16[384,1152]{1,0:T(8,128)(2,1)} %copy-done.4, f32[32,128]{1,0:T(8,128)} %copy-done.3, ...), custom_call_target="tpu_custom_call" | custom-call | flops 3567255552 | bytes 14000000 | tf_op jit(solution)/shard_map/pallas_call | solution.py:388
  51.5 1.4 collective-permute-start.2
  52.9 9.2 %shard_map.101.part_hbm = f32[384,1152]{1,0:T(8,128)} custom-call(bf16[384,1152]{1,0:T(8,128)(2,1)} %get-tuple-element.17.normed_hbm, bf16[1728,1152]{1,0:T(8,128)(2,1)} %bitcast.28, bf16[768,640]{1,0:T(8,128)(2,1)} %get-tuple-element.18.k_hbm, bf16[8,80,768]{2,1,0:T(8,128)(2,1)} %get-tuple-element.19.v_hbm, bf16[384,1152]{1,0:T(8,128)(2,1)} %bitcast.31, ...), custom_call_target="tpu_custom_call" | custom-call | flops 1528823808 | bytes 8000000 | tf_op jit(solution)/shard_map/pallas_call | solution.py:415
  62.1 3.3 %collective-permute-done.2.att_hbm = bf16[384,576]{1,0:T(8,128)(2,1)} collective-permute-done((bf16[384,576]{1,0:T(8,128)(2,1)}, bf16[384,576]{1,0:T(8,128)(2,1)}, u32[]{:S(2)}, u32[]{:S(2)}) %collective-permute-start.2) | collective-permute-done | bytes 442400 | tf_op jit(solution)/shard_map/ppermute | solution.py:414
  65.5 5.5 %shard_map.102 = (f32[384,1152]{1,0:T(8,128)}, bf16[384,1152]{1,0:T(8,128)(2,1)}) custom-call(f32[384,1152]{1,0:T(8,128)} %shard_map.101.part_hbm, bf16[384,576]{1,0:T(8,128)(2,1)} %collective-permute-done.2.att_hbm, bf16[576,1152]{1,0:T(8,128)(2,1)} %all-gather.4.cloned.1.call-done.w_hbm, f32[3,1152]{1,0:T(4,128)} %get-tuple-element.20.mods, ...), custom_call_target="tpu_custom_call" | custom-call | flops 509607936 | bytes 6000000 | tf_op jit(solution)/shard_map/pallas_call | solution.py:435
  71.0 9.6 %all-to-all-start.1 = ((bf16[16,24,1152]{2,1,0:T(8,128)(2,1)}), bf16[16,24,1152]{2,1,0:T(8,128)(2,1)}, u32[]{:S(2)}, u32[]{:S(2)}) async-start(bf16[16,24,1152]{2,1,0:T(8,128)(2,1)} %bitcast.32), calls=%async_computation.1 | async-start | bytes 1769472 | tf_op jit(solution)/shard_map/all_to_all | solution.py:455
  80.7 1.0 constant_dynamic-slice_fusion
  81.6 1.1 collective-permute-start.5
  82.8 4.5 %collective-permute-done.5 = bf16[72,1152]{1,0:T(8,128)(2,1)S(1)} collective-permute-done((bf16[72,1152]{1,0:T(8,128)(2,1)S(1)}, bf16[72,1152]{1,0:T(8,128)(2,1)S(1)}, u32[]{:S(2)}, u32[]{:S(2)}) %collective-permute-start.5) | collective-permute-done | bytes 165920 | tf_op jit(solution)/shard_map/ppermute | solution.py:453
  87.3 0.7 copy-done.2
  88.0 15.5 %all-to-all-done.1 = bf16[16,24,1152]{2,1,0:T(8,128)(2,1)} async-done(((bf16[16,24,1152]{2,1,0:T(8,128)(2,1)}), bf16[16,24,1152]{2,1,0:T(8,128)(2,1)}, u32[]{:S(2)}, u32[]{:S(2)}) %all-to-all-start.1) | async-done | bytes 884768 | tf_op jit(solution)/shard_map/all_to_all | solution.py:455
  103.5 9.2 %shard_map.103 = bf16[384,1152]{1,0:T(8,128)(2,1)} custom-call(bf16[384,1152]{1,0:T(8,128)(2,1)} %bitcast.10.moved_hbm, bf16[1728,1152]{1,0:T(8,128)(2,1)} %bitcast.37, bf16[1728,1152]{1,0:T(8,128)(2,1)} %all-gather.6.cloned.1.call-done.other_hbm), custom_call_target="tpu_custom_call" | custom-call | flops 3057647616 | bytes 10000000 | tf_op jit(solution)/shard_map/pallas_call | solution.py:458
  112.7 6.8 %all-to-all-start.2 = ((bf16[16,24,1152]{2,1,0:T(8,128)(2,1)}), bf16[16,24,1152]{2,1,0:T(8,128)(2,1)}, u32[]{:S(2)}, u32[]{:S(2)}) async-start(bf16[16,24,1152]{2,1,0:T(8,128)(2,1)} %bitcast.33), calls=%async_computation.2 | async-start | bytes 1769472 | tf_op jit(solution)/shard_map/all_to_all | solution.py:474
  119.5 11.5 %all-gather.8.cloned.1.call-done.other_w = bf16[576,1152]{1,0:T(8,128)(2,1)} async-done(((bf16[72,1152]{1,0:T(8,128)(2,1)}), bf16[576,1152]{1,0:T(8,128)(2,1)}) %all-gather.8.cloned.1.call-update) | async-done | bytes 1327120 | tf_op jit(solution)/shard_map/all_gather | solution.py:454
  131.0 14.3 %all-to-all-done.2 = bf16[16,24,1152]{2,1,0:T(8,128)(2,1)} async-done(((bf16[16,24,1152]{2,1,0:T(8,128)(2,1)}), bf16[16,24,1152]{2,1,0:T(8,128)(2,1)}, u32[]{:S(2)}, u32[]{:S(2)}) %all-to-all-start.2) | async-done | bytes 884768 | tf_op jit(solution)/shard_map/all_to_all | solution.py:474
  145.3 5.3 %shard_map.104 = f32[3456,128]{1,0:T(8,128)} custom-call(bf16[384,1152]{1,0:T(8,128)(2,1)} %bitcast.15.att_hbm, bf16[576,1152]{1,0:T(8,128)(2,1)} %own_w.1, bf16[576,1152]{1,0:T(8,128)(2,1)} %all-gather.8.cloned.1.call-done.other_w, f32[384,1152]{1,0:T(8,128)} %get-tuple-element.28.middle_hbm, f32[3,1152]{1,0:T(4,128)} %get-tuple-element.23.next_mods.mods), custom_call_target="tpu_custom_call" | custom-call | flops 1019215872 | bytes 8000000 | tf_op jit(solution)/shard_map/pallas_call | solution.py:476
  (23 shorter events, 0.3 us)
Async XLA Ops:
  6.5 4.1 %copy-start = (bf16[256,1152]{1,0:T(8,128)(2,1)S(1)}, bf16[256,1152]{1,0:T(8,128)(2,1)}, u32[]{:S(2)}) copy-start(bf16[256,1152]{1,0:T(8,128)(2,1)} %param.12) | copy-start | bytes 1769476
  6.5 26.7 %collective-permute-start = (bf16[384,1152]{1,0:T(8,128)(2,1)}, bf16[384,1152]{1,0:T(8,128)(2,1)S(1)}, u32[]{:S(2)}, u32[]{:S(2)}) collective-permute-start(bf16[384,1152]{1,0:T(8,128)(2,1)} %bitcast.29), channel_id=1, source_target_pairs={{0,1},{1,0},{2,3},{3,2},{4,5},{5,4},{6,7},{7,6},{8,9},{9,8},{10,11... | collective-permute-start | bytes 2654216 | tf_op jit(solution)/shard_map/ppermute | solution.py:364
  12.1 20.2 %all-to-all-start = ((f32[16,32,128]{2,1,0:T(8,128)}), f32[16,32,128]{2,1,0:T(8,128)S(1)}, u32[]{:S(2)}, u32[]{:S(2)}) async-start(f32[16,32,128]{2,1,0:T(8,128)} %broadcast_in_dim.2), calls=%async_computation | async-start | bytes 524288 | tf_op jit(solution)/shard_map/all_to_all | solution.py:375
  20.5 45.0 %all-gather.4.cloned.1.call-start = ((), (), s32[]{:S(2)}) async-start(), calls=%async_computation.3 | async-start | bytes 1492992 | tf_op jit(solution)/shard_map/all_gather | solution.py:381
  21.4 11.8 %collective-permute-start.3 = (bf16[72,1152]{1,0:T(8,128)(2,1)S(1)}, bf16[72,1152]{1,0:T(8,128)(2,1)S(1)}, u32[]{:S(2)}, u32[]{:S(2)}) collective-permute-start(bf16[72,1152]{1,0:T(8,128)(2,1)S(1)} %constant_dynamic-slice_fusion.2), channel_id=1, source_target_pairs={{0,3},{1,2},{2,1},{3,0},{4,7},{5,6},{6,5},{7,4},{8,11},{9,10},{10,... | collective-permute-start | bytes 497672 | tf_op jit(solution)/shard_map/ppermute | solution.py:372
  32.4 7.0 %copy-start.3 = (f32[32,128]{1,0:T(8,128)}, f32[32,128]{1,0:T(8,128)S(1)}, u32[]{:S(2)}) copy-start(f32[32,128]{1,0:T(8,128)S(1)} %reduce_sum.9.own_total) | copy-start | bytes 49156
  33.2 0.7 copy-start.1
  33.2 6.2 %copy-start.4 = (bf16[384,1152]{1,0:T(8,128)(2,1)}, bf16[384,1152]{1,0:T(8,128)(2,1)S(1)}, u32[]{:S(2)}) copy-start(bf16[384,1152]{1,0:T(8,128)(2,1)S(1)} %collective-permute-done.far_hbm) | copy-start | bytes 2654212
  33.9 69.6 %all-gather.6.cloned.1.call-start = ((), (), s32[]{:S(2)}) async-start(), calls=%async_computation.4 | async-start | bytes 4478976 | tf_op jit(solution)/shard_map/all_gather | solution.py:434
  33.9 5.4 %collective-permute-start.1 = (f32[32,128]{1,0:T(8,128)S(1)}, f32[32,128]{1,0:T(8,128)S(1)}, u32[]{:S(2)}, u32[]{:S(2)}) collective-permute-start(f32[32,128]{1,0:T(8,128)S(1)} %reduce_sum.9.own_total), channel_id=1, source_target_pairs={{0,1},{1,0},{2,3},{3,2},{4,5},{5,4},{6,7},{7,6},{8,9},{9,8},{10,11... | collective-permute-start | bytes 49160 | tf_op jit(solution)/shard_map/ppermute | solution.py:377
  36.6 28.9 %collective-permute-start.4 = (bf16[216,1152]{1,0:T(8,128)(2,1)}, bf16[216,1152]{1,0:T(8,128)(2,1)}, u32[]{:S(2)}, u32[]{:S(2)}) collective-permute-start(bf16[216,1152]{1,0:T(8,128)(2,1)} %constant_dynamic-slice_fusion.1), channel_id=1, source_target_pairs={{0,3},{1,2},{2,1},{3,0},{4,7},{5,6},{6,5},{7,4},{8,11},{9,10},{10,... | collective-permute-start | bytes 1493000 | tf_op jit(solution)/shard_map/ppermute | solution.py:382
  39.4 0.6 copy-start.5
  51.5 14.0 %collective-permute-start.2 = (bf16[384,576]{1,0:T(8,128)(2,1)}, bf16[384,576]{1,0:T(8,128)(2,1)}, u32[]{:S(2)}, u32[]{:S(2)}) collective-permute-start(bf16[384,576]{1,0:T(8,128)(2,1)} %get-tuple-element.21), channel_id=1, source_target_pairs={{0,1},{1,0},{2,3},{3,2},{4,5},{5,4},{6,7},{7,6},{8,9},{9,8},{10,11... | collective-permute-start | bytes 1327112 | tf_op jit(solution)/shard_map/ppermute | solution.py:414
  71.0 32.5 %all-to-all-start.1 = ((bf16[16,24,1152]{2,1,0:T(8,128)(2,1)}), bf16[16,24,1152]{2,1,0:T(8,128)(2,1)}, u32[]{:S(2)}, u32[]{:S(2)}) async-start(bf16[16,24,1152]{2,1,0:T(8,128)(2,1)} %bitcast.32), calls=%async_computation.1 | async-start | bytes 1769472 | tf_op jit(solution)/shard_map/all_to_all | solution.py:455
  80.6 50.3 %all-gather.8.cloned.1.call-start = ((), (), s32[]{:S(2)}) async-start(), calls=%async_computation.5 | async-start | bytes 1492992 | tf_op jit(solution)/shard_map/all_gather | solution.py:454
  81.6 5.6 %collective-permute-start.5 = (bf16[72,1152]{1,0:T(8,128)(2,1)S(1)}, bf16[72,1152]{1,0:T(8,128)(2,1)S(1)}, u32[]{:S(2)}, u32[]{:S(2)}) collective-permute-start(bf16[72,1152]{1,0:T(8,128)(2,1)S(1)} %constant_dynamic-slice_fusion), channel_id=1, source_target_pairs={{0,3},{1,2},{2,1},{3,0},{4,7},{5,6},{6,5},{7,4},{8,11},{9,10},{10,... | collective-permute-start | bytes 497672 | tf_op jit(solution)/shard_map/ppermute | solution.py:453
  87.3 0.7 copy-start.2
  112.7 32.6 %all-to-all-start.2 = ((bf16[16,24,1152]{2,1,0:T(8,128)(2,1)}), bf16[16,24,1152]{2,1,0:T(8,128)(2,1)}, u32[]{:S(2)}, u32[]{:S(2)}) async-start(bf16[16,24,1152]{2,1,0:T(8,128)(2,1)} %bitcast.33), calls=%async_computation.2 | async-start | bytes 1769472 | tf_op jit(solution)/shard_map/all_to_all | solution.py:474
Sparse Core Ops, SparseCore 0:
  34.0 29.8 all-gather.3
  65.7 36.7 all-gather.5
  104.4 26.5 all-gather.7
